TPU v7x, 256 devices: a whole 4x4x8 slice. The times are simulated.
256 devices in a mesh: wide: 128 (over z, x, y), narrow: 2 (over core).
Axes of the slice: x: 4, y: 4, z: 8, core: 2. Of those that a mesh axis runs over, the one named last changes fastest.
Arguments:
- particle_position: float32 [2048, 3, 256], P(('wide', 'narrow')), may hold values from -1 to 1
- particle_velocity: float32 [2048, 3, 256], P(('wide', 'narrow')), may hold values from -4 to 4
- inverse_mass: float32 [2048, 256], P(('wide', 'narrow')), may hold values from 0.5 to 2
- facet_geometry: float32 [256, 4, 7, 128], P('wide')
- boulder_pose: float32 [256, 16], P('wide')
- boulder_velocity: float32 [256, 6], P('wide'), may hold values from -6 to 6
- boulder_slot: int32 [256], replicated, may hold values from 0 to 255, as said below
- block_home: int32 [2048], replicated, may hold values from 0 to 2047, as said below
- pair_facet: int32 [49152], P(('wide', 'narrow')), may hold values from 0 to 1023, as said below
- pair_block: int32 [49152], P(('wide', 'narrow')), may hold values from 0 to 2047, as said below
- pair_active: int32 [49152], P(('wide', 'narrow')), may hold values 0 or 1
Outputs:
- new_velocity: float32 [2048, 3, 256], P(('wide', 'narrow'))
- boulder_motion: float32 [256, 6], P('wide')
Inputs may be any that keep to these rules, and one draw needn't show every extreme that they name: `boulder_slot`: A permutation: each slot once. Slot s belongs to owner s // 2. `block_home`: A permutation: each storage row once. Storage row r lies on device r // 8 in the order of wide+narrow. `pair_facet`: the 192 pairs of each device come in 64 runs of 3 consecutive pairs; all pairs of a run name boulders of one owner, and the runs of one device name different owners, so no device names more than 3 facet blocks of one owner. Every pair names a particle block stored on the device that holds the pair: block_home[pair_block[i]] // 8 is that device.
All inputs are finite; a program needn't handle non-finite values. No bound on the sum of `pair_active` on one device may be relied on, other than what follows from the above.
Results may differ from a plain program's by a relative error of at most 0.0001.
Values sent between devices are 32-bit elements; how exact they have to be, the bound alone decides.
No kernel may reach another device: no remote copies, remote signals or barrier semaphores. Data moves between devices by JAX's collectives and lax.ppermute only.
A program may use at most 64 MiB of HBM per device.

v0:
```python
import math

import jax
import jax.numpy as jnp
from jax import lax
from jax.sharding import PartitionSpec as P

CAP = 3


PENALTY = 0.3
SHARPNESS = 4.0
CONTACT_GAP = 0.1
TIME_STEP = 0.5


def rotate_parts(boulder_pose, parts):
    result = []
    for row_index in range(3):
        summed = boulder_pose[:, 3 + 3 * row_index][:, None, None] * parts[0]
        summed = summed + boulder_pose[:, 4 + 3 * row_index][:, None, None] * parts[1]
        summed = summed + boulder_pose[:, 5 + 3 * row_index][:, None, None] * parts[2]
        result.append(summed)
    return result


def world_facets(geometry, boulder_pose):
    lever_arm = rotate_parts(
        boulder_pose, [geometry[:, :, 0], geometry[:, :, 1], geometry[:, :, 2]]
    )
    normal = rotate_parts(boulder_pose, [geometry[:, :, 3], geometry[:, :, 4], geometry[:, :, 5]])
    centroid = [
        boulder_pose[:, component][:, None, None] + lever_arm[component] for component in range(3)
    ]
    world_facet = jnp.stack(centroid + normal + [geometry[:, :, 6]], axis=2)
    return (world_facet, jnp.stack(lever_arm, axis=2))


def contact_tile(facet, points):
    offset = [points[component][None, :] - facet[component][:, None] for component in range(3)]
    distance = (
        facet[3][:, None] * offset[0]
        + facet[4][:, None] * offset[1]
        + facet[5][:, None] * offset[2]
    )
    square = offset[0] * offset[0] + offset[1] * offset[1] + offset[2] * offset[2]
    weight = jnp.exp(-square) * jax.nn.softplus(SHARPNESS * (CONTACT_GAP - distance)) / SHARPNESS
    facet_load = jnp.sum(weight, axis=1)
    pushed = facet[6][None, :] * facet[3:6]
    push_sum = jnp.dot(pushed, weight, precision=lax.Precision.HIGHEST)
    return (PENALTY * push_sum, facet_load)


def boulder_update(totals, world_facet, lever_arm, boulder_pose, boulder_velocity):
    scaled = -PENALTY * world_facet[:, :, 6] * totals
    push = [scaled * world_facet[:, :, 3 + component] for component in range(3)]
    force_sum = [jnp.sum(push[component], axis=(1, 2)) for component in range(3)]
    torque = [
        jnp.sum(lever_arm[:, :, 1] * push[2] - lever_arm[:, :, 2] * push[1], axis=(1, 2)),
        jnp.sum(lever_arm[:, :, 2] * push[0] - lever_arm[:, :, 0] * push[2], axis=(1, 2)),
        jnp.sum(lever_arm[:, :, 0] * push[1] - lever_arm[:, :, 1] * push[0], axis=(1, 2)),
    ]
    body_torque = []
    for column_index in range(3):
        summed = boulder_pose[:, 3 + column_index] * torque[0]
        summed = summed + boulder_pose[:, 6 + column_index] * torque[1]
        summed = summed + boulder_pose[:, 9 + column_index] * torque[2]
        body_torque.append(summed * boulder_pose[:, 13 + column_index])
    angular = []
    for row_index in range(3):
        summed = boulder_pose[:, 3 + 3 * row_index] * body_torque[0]
        summed = summed + boulder_pose[:, 4 + 3 * row_index] * body_torque[1]
        summed = summed + boulder_pose[:, 5 + 3 * row_index] * body_torque[2]
        angular.append(boulder_velocity[:, 3 + row_index] + TIME_STEP * summed)
    linear = [
        boulder_velocity[:, component] + TIME_STEP * boulder_pose[:, 12] * force_sum[component]
        for component in range(3)
    ]
    return jnp.stack(linear + angular, axis=1)


def shards(
    particle_position,
    particle_velocity,
    inverse_mass,
    facet_geometry,
    boulder_pose,
    boulder_velocity,
    boulder_slot,
    block_home,
    pair_facet,
    pair_block,
    pair_active,
):
    owners = lax.axis_size("wide")
    device = lax.axis_index("wide") * lax.axis_size("narrow") + lax.axis_index("narrow")
    local_boulders = facet_geometry.shape[0]
    facet_blocks = facet_geometry.shape[1]
    facet_count = facet_geometry.shape[-1]
    block_count = particle_position.shape[0]
    world_facet, lever_arm = world_facets(facet_geometry, boulder_pose)
    world_flat = world_facet.reshape(local_boulders * facet_blocks, 7, facet_count)
    pair_count = pair_facet.shape[0]
    run_count = pair_count // CAP
    slot_index = boulder_slot[pair_facet // facet_blocks]
    block_index = pair_facet % facet_blocks
    owner_rank = slot_index // local_boulders
    owner_row = slot_index % local_boulders * facet_blocks + block_index
    run_owner = owner_rank.reshape(run_count, CAP)[:, 0]
    requests = (
        jnp.zeros((owners, CAP), jnp.int32).at[run_owner].set(owner_row.reshape(run_count, CAP))
    )
    found = world_flat[lax.all_to_all(requests, "wide", split_axis=0, concat_axis=0, tiled=True)]
    arrived = lax.all_to_all(found, "wide", split_axis=0, concat_axis=0, tiled=True)
    facets = arrived[run_owner].reshape(pair_count, 7, facet_count)
    block_rows = block_home[pair_block] - device * block_count
    active = pair_active.astype(jnp.float32)
    group_size = math.gcd(pair_count, 64)

    def tile_group(members):
        facet_part, rows_part = members
        points = particle_position[rows_part]
        return jax.vmap(contact_tile)(facet_part, points)

    pushes, loads = lax.map(
        tile_group,
        (facets.reshape(-1, group_size, 7, facet_count), block_rows.reshape(-1, group_size)),
    )
    pushes = pushes.reshape(pair_count, 3, particle_position.shape[-1])
    loads = loads.reshape(pair_count, facet_count) * active[:, None]
    onehot = (block_rows[:, None] == jnp.arange(block_count, dtype=jnp.int32)[None, :]).astype(
        jnp.float32
    ) * active[:, None]
    force_sum = jnp.einsum("pb,pkn->bkn", onehot, pushes, precision=lax.Precision.HIGHEST)
    new_velocity = particle_velocity + TIME_STEP * inverse_mass[:, None, :] * force_sum
    outgoing = (
        jnp.zeros((owners, CAP, facet_count), jnp.float32)
        .at[run_owner]
        .set(loads.reshape(run_count, CAP, facet_count))
    )
    incoming, asked_rows = (
        lax.all_to_all(outgoing, "wide", split_axis=0, concat_axis=0, tiled=True),
        lax.all_to_all(
            requests.astype(jnp.float32), "wide", split_axis=0, concat_axis=0, tiled=True
        ),
    )
    asked_index = asked_rows.reshape(-1).astype(jnp.int32)
    placement = (
        asked_index[:, None] == jnp.arange(local_boulders * facet_blocks, dtype=jnp.int32)[None, :]
    ).astype(jnp.float32)
    totals = jnp.dot(
        placement.T, incoming.reshape(-1, facet_count), precision=lax.Precision.HIGHEST
    )
    totals = lax.psum(totals, "narrow")
    boulder_motion = boulder_update(
        totals.reshape(local_boulders, facet_blocks, facet_count),
        world_facet,
        lever_arm,
        boulder_pose,
        boulder_velocity,
    )
    return (new_velocity, boulder_motion)


def solution(mesh):
    return jax.shard_map(
        shards,
        mesh=mesh,
        in_specs=(
            P(("wide", "narrow"), None, None),
            P(("wide", "narrow"), None, None),
            P(("wide", "narrow"), None),
            P("wide", None, None, None),
            P("wide", None),
            P("wide", None),
            P(),
            P(),
            P(("wide", "narrow")),
            P(("wide", "narrow")),
            P(("wide", "narrow")),
        ),
        out_specs=(P(("wide", "narrow"), None, None), P("wide", None)),
        check_vma=False,
    )
```

profile of v0, /device:TPU:1, one launch (start us, length us, event | category | flops | bytes accessed | tf_op | source)
XLA Modules:
  0.0 224.3 jit_solution(6724212117346198395)
XLA Ops:
  1.4 2.0 gather_fusion.2
  4.5 1.3 scatter_custom_fusion
  5.8 16.3 %all-to-all-start = ((s32[128,1,3]{2,1,0:T(1,128)}), s32[128,1,3]{2,1,0:T(1,128)S(1)}, u32[]{:S(2)}, u32[]{:S(2)}) async-start(s32[128,1,3]{2,1,0:T(1,128)} %bitcast.32), calls=%async_computation | async-start | bytes 131072 | tf_op jit(solution)/shard_map/all_to_all | solution.py:113
  22.1 1.5 fusion.97
  24.8 8.1 %all-to-all-done = s32[128,1,3]{2,1,0:T(1,128)S(1)} async-done(((s32[128,1,3]{2,1,0:T(1,128)}), s32[128,1,3]{2,1,0:T(1,128)S(1)}, u32[]{:S(2)}, u32[]{:S(2)}) %all-to-all-start) | async-done | bytes 1568 | tf_op jit(solution)/shard_map/all_to_all | solution.py:113
  33.1 2.5 %gather_fusion.3 = f32[384,7,128]{2,1,0:T(8,128)} fusion(f32[8,7,128]{2,1,0:T(8,128)S(1)} %stack.39, s32[1024]{0:T(1024)S(1)} %pad_clamp_fusion.2), kind=kCustom, calls=%fused_computation.3 | custom fusion | bytes 2754048 | tf_op jit(solution)/shard_map/gather | solution.py:113
  35.6 6.3 %all-to-all-start.1 = ((f32[128,3,7,128]{3,2,1,0:T(8,128)}), f32[128,3,7,128]{3,2,1,0:T(8,128)S(1)}, u32[]{:S(2)}, u32[]{:S(2)}) async-start(f32[128,3,7,128]{3,2,1,0:T(8,128)} %bitcast.34), calls=%async_computation.1 | async-start | bytes 3145728 | tf_op jit(solution)/shard_map/all_to_all | solution.py:114
  42.0 1.5 convert_element_type.19
  43.5 1.4 gather_fusion.1
  45.1 0.7 mul.647
  45.8 33.8 %all-to-all-done.1 = f32[128,3,7,128]{3,2,1,0:T(8,128)S(1)} async-done(((f32[128,3,7,128]{3,2,1,0:T(8,128)}), f32[128,3,7,128]{3,2,1,0:T(8,128)S(1)}, u32[]{:S(2)}, u32[]{:S(2)}) %all-to-all-start.1) | async-done | bytes 1376288 | tf_op jit(solution)/shard_map/all_to_all | solution.py:114
  79.6 9.6 %all-to-all-start.2 = ((f32[128,1,3]{2,1,0:T(1,128)}), f32[128,1,3]{2,1,0:T(1,128)S(1)}, u32[]{:S(2)}, u32[]{:S(2)}) async-start(f32[128,1,3]{2,1,0:T(1,128)} %bitcast.39), calls=%async_computation.2 | async-start | bytes 131072 | tf_op jit(solution)/shard_map/all_to_all | solution.py:143
  89.9 91.9 %while.12 = (s32[]{:T(128)}, f32[3,64,3,256]{3,2,1,0:T(4,128)S(1)}, f32[3,64,128]{2,1,0:T(8,128)S(1)}, f32[3,64,7,128]{3,2,1,0:T(8,128)S(1)}, s32[3,64]{1,0:T(4,128)S(1)}, /*index=5*/f32[8,3,256]{2,1,0:T(4,128)S(1)}, s32[]{:T(128)}) while((s32[]{:T(128)}, f32[3,64,3,256]{3,2,1,0:T(4,128)S(1)}, f32[3,64,128]{2,1,0:T(8,128)S(1)}, ...), condition=%wide.region_3.4_spmd, body=%wide.region_1.3_spmd.sunk | while | flops 178324672 | bytes 3413085 | solution.py:125
  91.1 12.6 %fusion.110 = f32[64,128]{1,0:T(8,128)S(1)} fusion(f32[64,128]{1,0:T(8,128)S(1)} %bitcast.344, f32[64,128]{1,0:T(8,128)S(1)} %bitcast.346, f32[64,128]{1,0:T(8,128)S(1)} %bitcast.348, f32[64,128]{1,0:T(8,128)S(1)} %bitcast.350, f32[64,256]{1,0:T(8,128)S(1)} %get-tuple-element.197, f32[64,128]{1,0:T(8,128)S(1)} %bitcast.352, ...), kind=kLoop, calls=%fused_computation.24.clone.1 | loop fusion | flops 52420608 | bytes 425984 | tf_op jit(solution)/shard_map/while/body/eval_jaxpr/vmap()/reduce_sum | solution.py:48
  103.7 16.9 %fusion.109 = f32[3,64,3,256]{3,2,1,0:T(4,128)S(1)} fusion(f32[3,64,3,256]{3,2,1,0:T(4,128)S(1)} %get-tuple-element.211, s32[]{:T(128)} %get-tuple-element.210, f32[64,128]{1,0:T(8,128)S(1)} %bitcast.345, f32[64,128]{1,0:T(8,128)S(1)} %bitcast.347, f32[64,128]{1,0:T(8,128)S(1)} %bitcast.349, f32[64,128]{1,0:T(8,128)S(1)} %bitcast.351, ...), kind=kOutput, calls=%fused_computation.28.clone.1 | convolution fusion | flops 125902848 | bytes 819204 | tf_op jit(solution)/shard_map/while/body/eval_jaxpr/vmap()/dot_general | solution.py:50
  121.7 12.6 %fusion.110 = f32[64,128]{1,0:T(8,128)S(1)} fusion(f32[64,128]{1,0:T(8,128)S(1)} %bitcast.344, f32[64,128]{1,0:T(8,128)S(1)} %bitcast.346, f32[64,128]{1,0:T(8,128)S(1)} %bitcast.348, f32[64,128]{1,0:T(8,128)S(1)} %bitcast.350, f32[64,256]{1,0:T(8,128)S(1)} %get-tuple-element.197, f32[64,128]{1,0:T(8,128)S(1)} %bitcast.352, ...), kind=kLoop, calls=%fused_computation.24.clone.1 | loop fusion | flops 52420608 | bytes 425984 | tf_op jit(solution)/shard_map/while/body/eval_jaxpr/vmap()/reduce_sum | solution.py:48
  134.3 16.9 %fusion.109 = f32[3,64,3,256]{3,2,1,0:T(4,128)S(1)} fusion(f32[3,64,3,256]{3,2,1,0:T(4,128)S(1)} %get-tuple-element.211, s32[]{:T(128)} %get-tuple-element.210, f32[64,128]{1,0:T(8,128)S(1)} %bitcast.345, f32[64,128]{1,0:T(8,128)S(1)} %bitcast.347, f32[64,128]{1,0:T(8,128)S(1)} %bitcast.349, f32[64,128]{1,0:T(8,128)S(1)} %bitcast.351, ...), kind=kOutput, calls=%fused_computation.28.clone.1 | convolution fusion | flops 125902848 | bytes 819204 | tf_op jit(solution)/shard_map/while/body/eval_jaxpr/vmap()/dot_general | solution.py:50
  152.3 12.6 %fusion.110 = f32[64,128]{1,0:T(8,128)S(1)} fusion(f32[64,128]{1,0:T(8,128)S(1)} %bitcast.344, f32[64,128]{1,0:T(8,128)S(1)} %bitcast.346, f32[64,128]{1,0:T(8,128)S(1)} %bitcast.348, f32[64,128]{1,0:T(8,128)S(1)} %bitcast.350, f32[64,256]{1,0:T(8,128)S(1)} %get-tuple-element.197, f32[64,128]{1,0:T(8,128)S(1)} %bitcast.352, ...), kind=kLoop, calls=%fused_computation.24.clone.1 | loop fusion | flops 52420608 | bytes 425984 | tf_op jit(solution)/shard_map/while/body/eval_jaxpr/vmap()/reduce_sum | solution.py:48
  165.0 16.9 %fusion.109 = f32[3,64,3,256]{3,2,1,0:T(4,128)S(1)} fusion(f32[3,64,3,256]{3,2,1,0:T(4,128)S(1)} %get-tuple-element.211, s32[]{:T(128)} %get-tuple-element.210, f32[64,128]{1,0:T(8,128)S(1)} %bitcast.345, f32[64,128]{1,0:T(8,128)S(1)} %bitcast.347, f32[64,128]{1,0:T(8,128)S(1)} %bitcast.349, f32[64,128]{1,0:T(8,128)S(1)} %bitcast.351, ...), kind=kOutput, calls=%fused_computation.28.clone.1 | convolution fusion | flops 125902848 | bytes 819204 | tf_op jit(solution)/shard_map/while/body/eval_jaxpr/vmap()/dot_general | solution.py:50
  182.8 6.6 %scatter_fusion = f32[128,3,128]{2,1,0:T(4,128)} fusion(f32[128,3,128]{2,1,0:T(4,128)} %broadcast_in_dim.39, s32[64]{0:T(128)S(1)} %fusion.34, f32[64,3,128]{2,1,0:T(4,128)S(1)} %broadcast_multiply_fusion), kind=kCustom, calls=%fused_computation.6 | custom fusion | bytes 295168 | tf_op jit(solution)/shard_map/scatter | solution.py:139
  189.4 13.3 %all-to-all-start.3 = ((f32[128,3,128]{2,1,0:T(4,128)}), f32[128,3,128]{2,1,0:T(4,128)S(1)}, u32[]{:S(2)}, u32[]{:S(2)}) async-start(f32[128,3,128]{2,1,0:T(4,128)} %scatter_fusion), calls=%async_computation.3 | async-start | bytes 524288 | tf_op jit(solution)/shard_map/all_to_all | solution.py:142
  205.5 1.1 fusion.29
  206.6 8.7 %all-to-all-done.3 = f32[128,3,128]{2,1,0:T(4,128)S(1)} async-done(((f32[128,3,128]{2,1,0:T(4,128)}), f32[128,3,128]{2,1,0:T(4,128)S(1)}, u32[]{:S(2)}, u32[]{:S(2)}) %all-to-all-start.3) | async-done | bytes 196640 | tf_op jit(solution)/shard_map/all_to_all | solution.py:142
  215.8 6.1 %psum.7 = f32[8,128]{1,0:T(8,128)S(1)} all-reduce(f32[8,128]{1,0:T(8,128)S(1)} %fusion.31), channel_id=1, replica_groups=mesh['wide'=128,'narrow'=2] {'narrow'}, use_global_device_ids=true, to_apply=%region_5.6 | all-reduce | flops 1024 | bytes 8192 | tf_op jit(solution)/shard_map/psum | solution.py:154
  (138 shorter events, 13.7 us)
Async XLA Ops:
  0.6 42.9 %copy-start = (s32[2048]{0:T(1024)S(1)}, s32[2048]{0:T(1024)}, u32[]{:S(2)}) copy-start(s32[2048]{0:T(1024)} %param.20) | copy-start | bytes 24580
  0.6 23.8 %copy-start.1 = (f32[2,4,7,128]{3,1,2,0:T(4,128)S(1)}, f32[2,4,7,128]{3,1,2,0:T(4,128)}, u32[]{:S(2)}) copy-start(f32[2,4,7,128]{3,1,2,0:T(4,128)} %param.16) | copy-start | bytes 86020
  5.8 27.1 %all-to-all-start = ((s32[128,1,3]{2,1,0:T(1,128)}), s32[128,1,3]{2,1,0:T(1,128)S(1)}, u32[]{:S(2)}, u32[]{:S(2)}) async-start(s32[128,1,3]{2,1,0:T(1,128)} %bitcast.32), calls=%async_computation | async-start | bytes 131072 | tf_op jit(solution)/shard_map/all_to_all | solution.py:113
  35.6 7.9 %copy-start.7 = (s32[192]{0:T(256)S(1)}, s32[192]{0:T(256)}, u32[]{:S(2)}) copy-start(s32[192]{0:T(256)} %param.22) | copy-start | bytes 2308
  35.6 9.4 %copy-start.5 = (f32[8,3,256]{2,0,1:T(8,128)S(1)}, f32[8,3,256]{2,0,1:T(8,128)}, u32[]{:S(2)}) copy-start(f32[8,3,256]{2,0,1:T(8,128)} %param.13) | copy-start | bytes 73732
  35.6 9.4 %copy-start.8 = (s32[192]{0:T(256)S(1)}, s32[192]{0:T(256)}, u32[]{:S(2)}) copy-start(s32[192]{0:T(256)} %param.23) | copy-start | bytes 2308
  35.6 10.2 %copy-start.6 = (f32[8,256]{1,0:T(8,128)S(1)}, f32[8,256]{1,0:T(8,128)}, u32[]{:S(2)}) copy-start(f32[8,256]{1,0:T(8,128)} %param.15) | copy-start | bytes 24580
  35.6 44.0 %all-to-all-start.1 = ((f32[128,3,7,128]{3,2,1,0:T(8,128)}), f32[128,3,7,128]{3,2,1,0:T(8,128)S(1)}, u32[]{:S(2)}, u32[]{:S(2)}) async-start(f32[128,3,7,128]{3,2,1,0:T(8,128)} %bitcast.34), calls=%async_computation.1 | async-start | bytes 3145728 | tf_op jit(solution)/shard_map/all_to_all | solution.py:114
  79.6 109.8 %all-to-all-start.2 = ((f32[128,1,3]{2,1,0:T(1,128)}), f32[128,1,3]{2,1,0:T(1,128)S(1)}, u32[]{:S(2)}, u32[]{:S(2)}) async-start(f32[128,1,3]{2,1,0:T(1,128)} %bitcast.39), calls=%async_computation.2 | async-start | bytes 131072 | tf_op jit(solution)/shard_map/all_to_all | solution.py:143
  89.9 92.0 %copy-start.2 = (f32[64,3]{1,0:T(8,128)S(1)}, f32[64,3]{1,0:T(8,128)}, u32[]{:S(2)}) copy-start(f32[64,3]{1,0:T(8,128)} %mul.647) | copy-start | bytes 2308
  181.8 20.9 %copy-start.3 = (f32[2,6]{1,0:T(2,128)S(1)}, f32[2,6]{1,0:T(2,128)}, u32[]{:S(2)}) copy-start(f32[2,6]{1,0:T(2,128)} %param.18) | copy-start | bytes 148
  181.8 23.6 %copy-start.4 = (f32[8,3,256]{2,0,1:T(8,128)S(1)}, f32[8,3,256]{2,0,1:T(8,128)}, u32[]{:S(2)}) copy-start(f32[8,3,256]{2,0,1:T(8,128)} %param.14) | copy-start | bytes 73732
  189.4 25.9 %all-to-all-start.3 = ((f32[128,3,128]{2,1,0:T(4,128)}), f32[128,3,128]{2,1,0:T(4,128)S(1)}, u32[]{:S(2)}, u32[]{:S(2)}) async-start(f32[128,3,128]{2,1,0:T(4,128)} %scatter_fusion), calls=%async_computation.3 | async-start | bytes 524288 | tf_op jit(solution)/shard_map/all_to_all | solution.py:142
where the time goes:
time: 225 us; the launch traced here: 224 us
  matrix products  52 us (23%)
  waiting for transfers between devices  50.6 us (22%)
  starting transfers between devices  45.6 us (20%)
  other arithmetic  42.4 us (19%)
  local copies, waits for them, and re-layouts  26.3 us (12%)
  blocking collectives  6.1 us (3%)
    dot_general x3, matrix products, contact_tile(): push_sum = jnp.dot(pushed, weight, precision=lax.Precision.HIGHEST)  50.6 us
    reduce_sum x3, other arithmetic, contact_tile(): facet_load = jnp.sum(weight, axis=1)  37.8 us
    all_to_all x1, waiting for transfers between devices, shards(): lax.all_to_all(found, 'wide', split_axis=0, concat_axis=0, tiled=True)  33.8 us
    all_to_all x1, starting transfers between devices, shards(): lax.all_to_all(requests, 'wide', split_axis=0, concat_axis=0, tiled=True)  16.3 us
    all_to_all x1, starting transfers between devices, shards(): lax.all_to_all(outgoing, 'wide', split_axis=0, concat_axis=0, tiled=True)  13.3 us
    all_to_all x1, starting transfers between devices, shards(): lax.all_to_all(requests.astype(jnp.float32), 'wide', split_axis=0, concat...  9.64 us
    all_to_all x1, waiting for transfers between devices, shards(): lax.all_to_all(outgoing, 'wide', split_axis=0, concat_axis=0, tiled=True)  8.74 us
    all_to_all x1, waiting for transfers between devices, shards(): lax.all_to_all(requests, 'wide', split_axis=0, concat_axis=0, tiled=True)  8.08 us
  transfers between devices with their start and end apart: 4, of which 3 were waited for; matrix products, arithmetic and copies ran while one was open for 49% of the time, Pallas kernels for 0%

commit v1 on v0

v1 whole, which is shorter than its diff:
```python
import functools

import jax
import jax.numpy as jnp
from jax import lax
from jax.experimental import pallas as pl
from jax.experimental.pallas import tpu as pltpu
from jax.sharding import PartitionSpec as P

PENALTY = 0.3
SHARPNESS = 4.0
CONTACT_GAP = 0.1
TIME_STEP = 0.5

PLANE = 16
DEPTH = 8
BLOCKS = 8
TERMS = 32
FACETS = PLANE * BLOCKS
PARTICLES = DEPTH * BLOCKS
UNROLL = 2
VMEM_LIMIT = 48 * 1024 * 1024

F32 = jnp.float32
BF16 = jnp.bfloat16


def split3(value):
    high = value.astype(BF16).astype(F32)
    rest = value - high
    middle = rest.astype(BF16).astype(F32)
    return high, middle, (rest - middle).astype(BF16).astype(F32)


def facet_message(geometry_ref, pose_ref, out_ref):
    lane = lax.broadcasted_iota(jnp.int32, (4, 128), 1)
    for boulder in range(2):
        part = [geometry_ref[boulder, :, row, :] for row in range(7)]
        center = [pose_ref[boulder, row] for row in range(3)]
        rotation = [pose_ref[boulder, 3 + entry] for entry in range(9)]
        rows = []
        for first in (0, 3):
            for row in range(3):
                rows.append(
                    rotation[3 * row] * part[first]
                    + rotation[3 * row + 1] * part[first + 1]
                    + rotation[3 * row + 2] * part[first + 2]
                )
        rows.append(part[6])
        rows.append(
            jnp.where(
                lane == 0,
                center[0],
                jnp.where(lane == 1, center[1], jnp.where(lane == 2, center[2], 0.0)),
            )
        )
        for target in range(PLANE):
            for row in range(8):
                out_ref[target, row, 4 * boulder : 4 * boulder + 4, :] = rows[row]


def pair_message(
    position_ref, slot_ref, home_ref, facet_ref, block_ref, active_ref, out_ref, keep_ref
):
    pairs = facet_ref.shape[0]
    lane = lax.broadcasted_iota(jnp.int32, (pairs, 128), 1)

    def look_up(table, index):
        rows = table.shape[0]
        row = lax.broadcasted_iota(jnp.int32, (pairs, rows), 1)
        onehot = ((index >> 7) == row).astype(F32).astype(BF16)
        picked = jnp.dot(onehot, table.astype(F32).astype(BF16), preferred_element_type=F32)
        picked = jnp.where(lane == (index & 127), picked, 0.0)
        return jnp.sum(picked, axis=1, keepdims=True).astype(jnp.int32)

    facet = facet_ref[...]
    slot = look_up(slot_ref[...], facet >> 2)
    local_block = look_up(home_ref[...] & 7, block_ref[...])
    plane = slot >> 5
    code = local_block * 256 + ((slot & 31) * 4 + (facet & 3))
    code = code.astype(F32)
    active = active_ref[...] != 0
    member = jnp.logical_and(lane == plane, active).astype(F32)
    row = lax.broadcasted_iota(jnp.int32, (pairs, pairs), 0)
    column = lax.broadcasted_iota(jnp.int32, (pairs, pairs), 1)
    below = (column < row).astype(F32).astype(BF16)
    before = jnp.dot(below, member.astype(BF16), preferred_element_type=F32)
    rank = jnp.sum(before * member, axis=1, keepdims=True).astype(jnp.int32)
    rank = jnp.where(active, rank, 255)
    spread = jnp.where(lane == rank, code, 0.0)
    lane_row = lax.broadcasted_iota(jnp.int32, (1, 128), 1)
    for part in range(3):
        keep_ref[8 * part : 8 * part + 8, :] = position_ref[:, part, :]
    near = keep_ref[:, 0:128]
    far = keep_ref[:, 128:256]
    for target in range(DEPTH):
        here = jnp.logical_and(plane == target, active)
        listed = jnp.sum(jnp.where(here, spread, 0.0), axis=0, keepdims=True)
        count = jnp.sum(here.astype(F32), axis=0, keepdims=True)
        listed = jnp.where(lane_row == 127, count, listed)
        out_ref[target, 0:24, :] = near
        out_ref[target, 24:48, :] = far
        out_ref[target, 48:56, :] = jnp.broadcast_to(listed, (8, 128))


def facet_features(world_ref, terms_ref, push_ref, terms_keep, push_keep):
    terms_keep[...] = jnp.zeros(terms_keep.shape, F32)
    push_keep[...] = jnp.zeros(push_keep.shape, F32)

    def owner(index, carry):
        lever = [world_ref[index, part] for part in range(3)]
        normal = [world_ref[index, 3 + part] for part in range(3)]
        area = world_ref[index, 6]
        last = world_ref[index, 7]
        center = [lever[part] + last[:, part : part + 1] for part in range(3)]
        along = normal[0] * center[0] + normal[1] * center[1] + normal[2] * center[2]
        square = center[0] * center[0] + center[1] * center[1] + center[2] * center[2]
        sides = (
            ([-SHARPNESS * value for value in normal], SHARPNESS * (CONTACT_GAP + along), 0.0),
            ([2.0 * value for value in center], -square, 1.0),
        )
        for side, (factors, constant, tail) in enumerate(sides):
            split = [split3(value) for value in factors]
            order = (0, 1, 2, 0, 1, 0)
            for group, level in enumerate(order):
                for part in range(3):
                    terms_keep[side * TERMS + 3 * group + part] = split[part][level]
            for level, value in enumerate(split3(constant)):
                terms_keep[side * TERMS + 18 + level] = value
                terms_keep[side * TERMS + 21 + level] = jnp.full((8, 128), tail, F32)
        scaled = (PENALTY / SHARPNESS) * area
        push = [scaled * value for value in normal]
        push.append(lever[1] * push[2] - lever[2] * push[1])
        push.append(lever[2] * push[0] - lever[0] * push[2])
        push.append(lever[0] * push[1] - lever[1] * push[0])
        for part in range(6):
            high = push[part].astype(BF16).astype(F32)
            push_keep[part] = high
            push_keep[8 + part] = push[part] - high
        for block in range(BLOCKS):
            both = terms_keep[:, block, :]
            terms_ref[index * BLOCKS + block, 0:128, :] = both[:TERMS].T.astype(BF16)
            terms_ref[index * BLOCKS + block, 128:256, :] = both[TERMS:].T.astype(BF16)
            push_ref[index * BLOCKS + block] = push_keep[:, block, :].astype(BF16)
        return carry

    lax.fori_loop(0, PLANE, owner, 0)
    terms_ref[FACETS] = jnp.zeros((256, TERMS), BF16)
    push_ref[FACETS] = jnp.zeros((16, 128), BF16)


def contact(
    terms_ref, push_ref, given_ref, force_ref, load_ref,
    table, listed, point_keep, points, force_sum, load_sum, sem,
):
    copy = pltpu.make_async_copy(given_ref.at[:, pl.ds(48, 8), :], table, sem)
    copy.start()
    point_keep[...] = jnp.zeros(point_keep.shape, F32)
    force_sum[...] = jnp.zeros(force_sum.shape, F32)
    load_sum[...] = jnp.zeros(load_sum.shape, F32)
    points[PARTICLES] = jnp.zeros((TERMS, 256), BF16)

    def source(index, carry):
        for half in range(2):
            lanes = slice(128 * half, 128 * half + 128)
            place = [
                given_ref[index, 24 * half + 8 * part : 24 * half + 8 * part + 8, :]
                for part in range(3)
            ]
            square = place[0] * place[0] + place[1] * place[1] + place[2] * place[2]
            split = [split3(value) for value in place]
            for group, level in enumerate((0, 0, 0, 1, 1, 2)):
                for part in range(3):
                    point_keep[3 * group + part, :, lanes] = split[part][level]
            for level, value in enumerate(split3(-square)):
                point_keep[18 + level, :, lanes] = jnp.full((8, 128), 1.0, F32)
                point_keep[21 + level, :, lanes] = value
        for block in range(BLOCKS):
            points[index * BLOCKS + block] = point_keep[:, block, :].astype(BF16)
        return carry

    lax.fori_loop(0, DEPTH, source, 0)
    copy.wait()

    def gather(index, start):
        count = table[index, 0, 127].astype(jnp.int32)
        shift = index * (BLOCKS * 256)

        def entry(place, carry):
            listed[start + place] = table[index, 0, place].astype(jnp.int32) + shift
            return carry

        lax.fori_loop(0, count, entry, 0)
        return start + count

    total = lax.fori_loop(0, DEPTH, gather, 0)
    for spare in range(UNROLL):
        listed[total + spare] = PARTICLES * 256 + FACETS

    def step(index, carry):
        done = []
        for lane in range(UNROLL):
            code = listed[index * UNROLL + lane]
            block = code >> 8
            facet = code & 255
            both = jnp.dot(terms_ref[facet], points[block], preferred_element_type=F32)
            gap = both[:128]
            soft = jnp.where(gap > 80.0, gap, jnp.log(1.0 + jnp.exp(gap)))
            weight = jnp.exp(both[128:]) * soft
            high = weight.astype(BF16)
            low = (weight - high.astype(F32)).astype(BF16)
            push = push_ref[facet]
            result = jnp.dot(push, high, preferred_element_type=F32) + jnp.dot(
                push, low, preferred_element_type=F32
            )
            done.append((block, facet >> 2, result[0:8] + result[8:16]))
        for block, boulder, result in done:
            force_sum[block] += result
            load_sum[boulder] += result[:, :128] + result[:, 128:]
        return carry

    lax.fori_loop(0, (total + UNROLL - 1) // UNROLL, step, 0)
    for index in range(DEPTH):
        for block in range(BLOCKS):
            force_ref[index, 3 * block : 3 * block + 3, :] = force_sum[
                index * BLOCKS + block, 0:3, :
            ]
    load_ref[...] = load_sum[0 : 2 * PLANE]


def finish_particles(force_ref, velocity_ref, mass_ref, out_ref):
    total = force_ref[0]
    for index in range(1, DEPTH):
        total = total + force_ref[index]
    scaled = TIME_STEP * mass_ref[...]
    for block in range(BLOCKS):
        out_ref[block] = velocity_ref[block] + scaled[block : block + 1, :] * total[
            3 * block : 3 * block + 3, :
        ]


def sum_loads(load_ref, out_ref):
    total = load_ref[0]
    for index in range(1, PLANE):
        total = total + load_ref[index]
    out_ref[...] = total


def finish_boulders(own_ref, other_ref, pose_ref, velocity_ref, out_ref):
    row = lax.broadcasted_iota(jnp.int32, (2, 6), 0)
    column = lax.broadcasted_iota(jnp.int32, (2, 6), 1)
    change = jnp.zeros((2, 6), F32)
    for boulder in range(2):
        total = jnp.sum(own_ref[boulder] + other_ref[boulder], axis=1, keepdims=True)
        force = [-total[part : part + 1, :] for part in range(3)]
        torque = [-total[3 + part : 4 + part, :] for part in range(3)]
        moves = [pose_ref[boulder, 12] * value for value in force]
        body = []
        for part in range(3):
            turned = (
                pose_ref[boulder, 3 + part] * torque[0]
                + pose_ref[boulder, 6 + part] * torque[1]
                + pose_ref[boulder, 9 + part] * torque[2]
            )
            body.append(turned * pose_ref[boulder, 13 + part])
        for part in range(3):
            moves.append(
                pose_ref[boulder, 3 + 3 * part] * body[0]
                + pose_ref[boulder, 4 + 3 * part] * body[1]
                + pose_ref[boulder, 5 + 3 * part] * body[2]
            )
        for part in range(6):
            here = jnp.logical_and(row == boulder, column == part)
            change = change + jnp.where(here, moves[part], 0.0)
    out_ref[...] = velocity_ref[...] + TIME_STEP * change


VMEM = pl.BlockSpec(memory_space=pltpu.VMEM)
SMEM = pl.BlockSpec(memory_space=pltpu.SMEM)


def call(kernel, outs, in_specs, scratch=(), cost=None):
    single = not isinstance(outs, list)
    return pl.pallas_call(
        kernel,
        out_shape=outs,
        in_specs=in_specs,
        out_specs=VMEM if single else [VMEM] * len(outs),
        scratch_shapes=list(scratch),
        cost_estimate=cost,
        compiler_params=pltpu.CompilerParams(vmem_limit_bytes=VMEM_LIMIT),
    )


def shards(
    particle_position,
    particle_velocity,
    inverse_mass,
    facet_geometry,
    boulder_pose,
    boulder_velocity,
    boulder_slot,
    block_home,
    pair_facet,
    pair_block,
    pair_active,
):
    owners = lax.axis_size("wide")
    planes = [[PLANE * depth + spot for spot in range(PLANE)] for depth in range(owners // PLANE)]
    columns = [[PLANE * depth + spot for depth in range(DEPTH)] for spot in range(PLANE)]
    swap = functools.partial(
        lax.all_to_all, axis_name="wide", split_axis=0, concat_axis=0, tiled=True
    )
    pairs = pair_facet.shape[0]
    shape = jax.ShapeDtypeStruct

    facets = call(facet_message, shape((PLANE, 8, BLOCKS, 128), F32), [VMEM, SMEM])(
        facet_geometry, boulder_pose
    )
    facets = swap(facets, axis_index_groups=planes)
    particles = call(
        pair_message, shape((DEPTH, 56, 128), F32), [VMEM] * 6, [pltpu.VMEM((24, 256), F32)]
    )(
        particle_position,
        boulder_slot.reshape(2, 128),
        block_home.reshape(16, 128),
        pair_facet.reshape(pairs, 1),
        pair_block.reshape(pairs, 1),
        pair_active.reshape(pairs, 1),
    )
    particles = swap(particles, axis_index_groups=columns)
    terms, push = call(
        facet_features,
        [shape((FACETS + 1, 256, TERMS), BF16), shape((FACETS + 1, 16, 128), BF16)],
        [VMEM],
        [pltpu.VMEM((2 * TERMS, BLOCKS, 128), F32), pltpu.VMEM((16, BLOCKS, 128), F32)],
    )(facets)
    force, load = call(
        contact,
        [shape((DEPTH, 24, 256), F32), shape((2 * PLANE, 8, 128), F32)],
        [VMEM] * 3,
        [
            pltpu.SMEM((DEPTH, 8, 128), F32),
            pltpu.SMEM((DEPTH * 48 + UNROLL,), jnp.int32),
            pltpu.VMEM((TERMS, BLOCKS, 256), F32),
            pltpu.VMEM((PARTICLES + 1, TERMS, 256), BF16),
            pltpu.VMEM((PARTICLES + 1, 8, 256), F32),
            pltpu.VMEM((2 * PLANE + 1, 8, 128), F32),
            pltpu.SemaphoreType.DMA,
        ],
    )(terms, push, particles)
    load = swap(load, axis_index_groups=planes)
    load = call(sum_loads, shape((2, 8, 128), F32), [VMEM])(load.reshape(PLANE, 2, 8, 128))
    other = lax.ppermute(load, "narrow", [(0, 1), (1, 0)])
    boulder_motion = call(
        finish_boulders, shape(boulder_velocity.shape, F32), [VMEM, VMEM, SMEM, VMEM]
    )(load, other, boulder_pose, boulder_velocity)
    force = swap(force, axis_index_groups=columns)
    new_velocity = call(finish_particles, shape(particle_velocity.shape, F32), [VMEM] * 3)(
        force, particle_velocity, inverse_mass
    )
    return (new_velocity, boulder_motion)


def solution(mesh):
    return jax.shard_map(
        shards,
        mesh=mesh,
        in_specs=(
            P(("wide", "narrow"), None, None),
            P(("wide", "narrow"), None, None),
            P(("wide", "narrow"), None),
            P("wide", None, None, None),
            P("wide", None),
            P("wide", None),
            P(),
            P(),
            P(("wide", "narrow")),
            P(("wide", "narrow")),
            P(("wide", "narrow")),
        ),
        out_specs=(P(("wide", "narrow"), None, None), P("wide", None)),
        check_vma=False,
    )
```

time: 225 us -> 124 us (0.55)
  the two profiles are of different devices: /device:TPU:1 before, /device:TPU:2 now
where the time goes in v1:
time: 124 us; the launch traced here: 123 us
  Pallas kernels  60.2 us (49%)
  starting transfers between devices  26.5 us (21%)
  blocking collectives  15.7 us (13%)
  waiting for transfers between devices  12.8 us (10%)
  local copies, waits for them, and re-layouts  6.59 us (5%)
    pallas_call x1, Pallas kernels, shards(): call(contact, [shape((DEPTH, 24, 256), F32), shape((2 * PLANE, 8, 128), F...  47 us
    all_to_all x1, blocking collectives, shards(): load = swap(load, axis_index_groups=planes)  15.7 us
    all_to_all x1, starting transfers between devices, shards(): force = swap(force, axis_index_groups=columns)  10.4 us
    pallas_call x1, Pallas kernels, shards(): call(facet_features, [shape((FACETS + 1, 256, TERMS), BF16), shape((FACET...  9.06 us
    all_to_all x1, starting transfers between devices, shards(): particles = swap(particles, axis_index_groups=columns)  8.47 us
    all_to_all x1, starting transfers between devices, shards(): facets = swap(facets, axis_index_groups=planes)  7.48 us
    all_to_all x1, waiting for transfers between devices, shards(): force = swap(force, axis_index_groups=columns)  7.25 us
    unnamed x18, local copies, waits for them, and re-layouts  4.21 us
  transfers between devices with their start and end apart: 4, of which 4 were waited for; matrix products, arithmetic and copies ran while one was open for 3% of the time, Pallas kernels for 10%

profile of v1, /device:TPU:2, one launch (start us, length us, event | category | flops | bytes accessed | tf_op | source)
XLA Modules:
  0.0 122.5 jit_solution(7755892210972324574)
XLA Ops:
  0.6 0.0 copy-start.3
  0.7 0.8 copy.17.geometry_ref
  1.4 0.7 copy-done.2
  2.1 1.4 %shard_map.122 = f32[16,8,8,128]{3,2,1,0:T(8,128)} custom-call(f32[2,4,7,128]{3,2,1,0:T(8,128)S(1)} %copy.17.geometry_ref, f32[2,16]{1,0:T(2,128)S(1)} %copy-done.2), custom_call_target="tpu_custom_call" | custom-call | tf_op jit(solution)/shard_map/pallas_call | solution.py:317
  3.6 7.5 %all-to-all-start = ((f32[16,8,8,128]{3,2,1,0:T(8,128)}), f32[16,8,8,128]{3,2,1,0:T(8,128)S(1)}, u32[]{:S(2)}, u32[]{:S(2)}) async-start(f32[16,8,8,128]{3,2,1,0:T(8,128)} %shard_map.122), calls=%async_computation | async-start | bytes 1048576 | tf_op jit(solution)/shard_map/all_to_all | solution.py:320
  11.0 0.8 copy.19.facet_ref
  11.8 0.8 copy.20.block_ref
  12.6 0.8 copy.21.active_ref
  13.4 0.8 copy.18.position_ref
  14.2 0.7 copy-done
  14.9 0.7 copy-done.4
  15.6 1.5 %shard_map.124 = f32[8,56,128]{2,1,0:T(8,128)} custom-call(f32[8,3,256]{2,1,0:T(4,128)S(1)} %copy.18.position_ref, s32[2,128]{1,0:T(2,128)S(1)} %bitcast.8, s32[16,128]{1,0:T(8,128)S(1)} %bitcast.7, s32[192,1]{1,0:T(8,128)S(1)} %copy.19.facet_ref, s32[192,1]{1,0:T(8,128)S(1)} %copy.20.block_ref, s32[192,1]{1,0:T(8,128)S(1)} %copy.21.active_ref), custom_call_target="tpu_custom_call" | custom-call | tf_op jit(solution)/shard_map/pallas_call | solution.py:321
  17.1 3.3 %all-to-all-done.world_ref = f32[16,8,8,128]{3,2,1,0:T(8,128)S(1)} async-done(((f32[16,8,8,128]{3,2,1,0:T(8,128)}), f32[16,8,8,128]{3,2,1,0:T(8,128)S(1)}, u32[]{:S(2)}, u32[]{:S(2)}) %all-to-all-start) | async-done | bytes 524320 | tf_op jit(solution)/shard_map/all_to_all | solution.py:320
  20.4 8.5 %all-to-all-start.1 = ((f32[8,56,128]{2,1,0:T(8,128)}), f32[8,56,128]{2,1,0:T(8,128)S(1)}, u32[]{:S(2)}, u32[]{:S(2)}) async-start(f32[8,56,128]{2,1,0:T(8,128)} %shard_map.124), calls=%async_computation.1 | async-start | bytes 458752 | tf_op jit(solution)/shard_map/all_to_all | solution.py:331
  28.8 9.1 %shard_map.123 = (bf16[129,256,32]{2,1,0:T(8,128)(2,1)}, bf16[129,16,128]{2,1,0:T(8,128)(2,1)S(1)}) custom-call(f32[16,8,8,128]{3,2,1,0:T(8,128)S(1)} %all-to-all-done.world_ref), custom_call_target="tpu_custom_call" | custom-call | tf_op jit(solution)/shard_map/pallas_call | solution.py:332
  37.9 1.1 all-to-all-done.1.given_ref
  39.0 47.0 %shard_map.125 = (f32[8,24,256]{2,1,0:T(8,128)}, f32[32,8,128]{2,1,0:T(8,128)S(1)}) custom-call(bf16[129,256,32]{2,1,0:T(8,128)(2,1)} %get-tuple-element.6.terms_ref, bf16[129,16,128]{2,1,0:T(8,128)(2,1)S(1)} %get-tuple-element.7.push_ref, f32[8,56,128]{2,1,0:T(8,128)S(1)} %all-to-all-done.1.given_ref), custom_call_target="tpu_custom_call" | custom-call | tf_op jit(solution)/shard_map/pallas_call | solution.py:338
  86.0 15.7 %all_to_all.20 = f32[32,8,128]{2,1,0:T(8,128)S(1)} all-to-all(f32[32,8,128]{2,1,0:T(8,128)S(1)} %get-tuple-element.9), channel_id=1, replica_groups={{0,2,4,6,8,10,12,14,16,18,20,22,24,26,28,30},{32,34,36,38,40,42,44,46,4..., dimensions={0} | all-to-all | bytes 262144 | tf_op jit(solution)/shard_map/all_to_all | solution.py:352
  101.6 10.4 %all-to-all-start.2 = ((f32[8,24,256]{2,1,0:T(8,128)}), f32[8,24,256]{2,1,0:T(8,128)S(1)}, u32[]{:S(2)}, u32[]{:S(2)}) async-start(f32[8,24,256]{2,1,0:T(8,128)} %get-tuple-element.8), calls=%async_computation.2 | async-start | bytes 393216 | tf_op jit(solution)/shard_map/all_to_all | solution.py:358
  112.1 0.1 collective-permute-start
  112.2 1.1 collective-permute-done.other_ref
  113.4 1.2 %shard_map.128 = f32[2,6]{1,0:T(2,128)} custom-call(f32[2,8,128]{2,1,0:T(8,128)S(1)} %shard_map.127.own_ref, f32[2,8,128]{2,1,0:T(8,128)S(1)} %collective-permute-done.other_ref, f32[2,16]{1,0:T(2,128)S(1)} %copy-done.3, f32[2,6]{1,0:T(2,128)S(1)} %copy-done.5), custom_call_target="tpu_custom_call" | custom-call | tf_op jit(solution)/shard_map/pallas_call | solution.py:355
  114.6 7.2 %all-to-all-done.2.force_ref = f32[8,24,256]{2,1,0:T(8,128)S(1)} async-done(((f32[8,24,256]{2,1,0:T(8,128)}), f32[8,24,256]{2,1,0:T(8,128)S(1)}, u32[]{:S(2)}, u32[]{:S(2)}) %all-to-all-start.2) | async-done | bytes 196640 | tf_op jit(solution)/shard_map/all_to_all | solution.py:358
  121.9 0.6 copy.23
  (13 shorter events, 0.1 us)
Async XLA Ops:
  0.6 112.7 %copy-start.3 = (f32[2,16]{1,0:T(2,128)S(1)}, f32[2,16]{1,0:T(2,128)}, u32[]{:S(2)}) copy-start(f32[2,16]{1,0:T(2,128)} %pose_ref.3) | copy-start | bytes 388
  0.6 111.6 %copy-start.6 = (f32[8,3,256]{2,0,1:T(8,128)S(1)}, f32[8,3,256]{2,0,1:T(8,128)}, u32[]{:S(2)}) copy-start(f32[8,3,256]{2,0,1:T(8,128)} %param.12) | copy-start | bytes 73732
  0.7 112.7 %copy-start.5 = (f32[2,6]{1,0:T(2,128)S(1)}, f32[2,6]{1,0:T(2,128)}, u32[]{:S(2)}) copy-start(f32[2,6]{1,0:T(2,128)} %velocity_ref.2) | copy-start | bytes 148
  0.7 121.2 %copy-start.1 = (f32[8,256]{1,0:T(8,128)S(1)}, f32[8,256]{1,0:T(8,128)}, u32[]{:S(2)}) copy-start(f32[8,256]{1,0:T(8,128)} %mass_ref.1) | copy-start | bytes 24580
  1.4 0.7 copy-start.2
  3.6 16.8 %all-to-all-start = ((f32[16,8,8,128]{3,2,1,0:T(8,128)}), f32[16,8,8,128]{3,2,1,0:T(8,128)S(1)}, u32[]{:S(2)}, u32[]{:S(2)}) async-start(f32[16,8,8,128]{3,2,1,0:T(8,128)} %shard_map.122), calls=%async_computation | async-start | bytes 1048576 | tf_op jit(solution)/shard_map/all_to_all | solution.py:320
  14.2 0.7 copy-start
  14.9 0.7 copy-start.4
  20.4 18.6 %all-to-all-start.1 = ((f32[8,56,128]{2,1,0:T(8,128)}), f32[8,56,128]{2,1,0:T(8,128)S(1)}, u32[]{:S(2)}, u32[]{:S(2)}) async-start(f32[8,56,128]{2,1,0:T(8,128)} %shard_map.124), calls=%async_computation.1 | async-start | bytes 458752 | tf_op jit(solution)/shard_map/all_to_all | solution.py:331
  101.6 20.2 %all-to-all-start.2 = ((f32[8,24,256]{2,1,0:T(8,128)}), f32[8,24,256]{2,1,0:T(8,128)S(1)}, u32[]{:S(2)}, u32[]{:S(2)}) async-start(f32[8,24,256]{2,1,0:T(8,128)} %get-tuple-element.8), calls=%async_computation.2 | async-start | bytes 393216 | tf_op jit(solution)/shard_map/all_to_all | solution.py:358
  112.1 1.3 %collective-permute-start = (f32[2,8,128]{2,1,0:T(8,128)S(1)}, f32[2,8,128]{2,1,0:T(8,128)S(1)}, u32[]{:S(2)}, u32[]{:S(2)}) collective-permute-start(f32[2,8,128]{2,1,0:T(8,128)S(1)} %shard_map.127.own_ref), channel_id=1, source_target_pairs={{0,1},{1,0},{2,3},{3,2},{4,5},{5,4},{6,7},{7,6},{8,9},{9,8},{10,11... | collective-permute-start | bytes 24584 | tf_op jit(solution)/shard_map/ppermute | solution.py:354

commit v2 on v1

--- a/solution.py
+++ b/solution.py
@@ -18,8 +18,8 @@
 TERMS = 32
 FACETS = PLANE * BLOCKS
 PARTICLES = DEPTH * BLOCKS
-UNROLL = 2
-VMEM_LIMIT = 48 * 1024 * 1024
+GROUP = 2
+VMEM_LIMIT = 24 * 1024 * 1024
 
 F32 = jnp.float32
 BF16 = jnp.bfloat16
@@ -60,7 +60,7 @@
 
 
 def pair_message(
-    position_ref, slot_ref, home_ref, facet_ref, block_ref, active_ref, out_ref, keep_ref
+    position_ref, slot_ref, home_ref, facet_ref, block_ref, active_ref, out_ref
 ):
     pairs = facet_ref.shape[0]
     lane = lax.broadcasted_iota(jnp.int32, (pairs, 128), 1)
@@ -89,17 +89,17 @@
     rank = jnp.where(active, rank, 255)
     spread = jnp.where(lane == rank, code, 0.0)
     lane_row = lax.broadcasted_iota(jnp.int32, (1, 128), 1)
-    for part in range(3):
-        keep_ref[8 * part : 8 * part + 8, :] = position_ref[:, part, :]
-    near = keep_ref[:, 0:128]
-    far = keep_ref[:, 128:256]
     for target in range(DEPTH):
         here = jnp.logical_and(plane == target, active)
         listed = jnp.sum(jnp.where(here, spread, 0.0), axis=0, keepdims=True)
         count = jnp.sum(here.astype(F32), axis=0, keepdims=True)
         listed = jnp.where(lane_row == 127, count, listed)
-        out_ref[target, 0:24, :] = near
-        out_ref[target, 24:48, :] = far
+        for half in range(2):
+            for part in range(3):
+                first = 24 * half + 8 * part
+                out_ref[target, first : first + 8, :] = position_ref[
+                    part, :, 128 * half : 128 * half + 128
+                ]
         out_ref[target, 48:56, :] = jnp.broadcast_to(listed, (8, 128))
 
 
@@ -151,8 +151,11 @@
 
 def contact(
     terms_ref, push_ref, given_ref, force_ref, load_ref,
-    table, listed, point_keep, points, force_sum, load_sum, sem,
+    table, listed, point_keep, points, force_sum, load_sum,
+    sem, *buffers,
 ):
+    gaps = [buffers[0:GROUP], buffers[GROUP : 2 * GROUP]]
+    weights = [buffers[2 * GROUP : 3 * GROUP], buffers[3 * GROUP : 4 * GROUP]]
     copy = pltpu.make_async_copy(given_ref.at[:, pl.ds(48, 8), :], table, sem)
     copy.start()
     point_keep[...] = jnp.zeros(point_keep.shape, F32)
@@ -193,38 +196,55 @@
         lax.fori_loop(0, count, entry, 0)
         return start + count
 
-    total = lax.fori_loop(0, DEPTH, gather, 0)
-    for spare in range(UNROLL):
+    total = lax.fori_loop(0, DEPTH, gather, 2 * GROUP)
+    for spare in range(2 * GROUP):
+        listed[spare] = PARTICLES * 256 + FACETS
+    for spare in range(4 * GROUP):
         listed[total + spare] = PARTICLES * 256 + FACETS
 
+    def exponents(place, buffer):
+        code = listed[place]
+        buffer[...] = jnp.dot(
+            terms_ref[code & 255], points[code >> 8], preferred_element_type=F32
+        )
+
+    def weigh(buffer, weight_ref):
+        for first in range(0, 128, 16):
+            gap = buffer[first : first + 16, :]
+            soft = jnp.where(gap > 80.0, gap, jnp.log(1.0 + jnp.exp(gap)))
+            weight = jnp.exp(buffer[128 + first : 144 + first, :]) * soft
+            high = weight.astype(BF16)
+            weight_ref[first : first + 16, :] = high
+            weight_ref[128 + first : 144 + first, :] = (weight - high.astype(F32)).astype(BF16)
+
+    def add(place, weight_ref):
+        code = listed[place]
+        facet = code & 255
+        push = push_ref[facet]
+        result = jnp.dot(
+            jnp.concatenate([push, push], axis=1), weight_ref[...], preferred_element_type=F32
+        )
+        result = result[0:8] + result[8:16]
+        force_sum[code >> 8] += result
+        load_sum[facet >> 2] += result[:, :128] + result[:, 128:]
+
     def step(index, carry):
-        done = []
-        for lane in range(UNROLL):
-            code = listed[index * UNROLL + lane]
-            block = code >> 8
-            facet = code & 255
-            both = jnp.dot(terms_ref[facet], points[block], preferred_element_type=F32)
-            gap = both[:128]
-            soft = jnp.where(gap > 80.0, gap, jnp.log(1.0 + jnp.exp(gap)))
-            weight = jnp.exp(both[128:]) * soft
-            high = weight.astype(BF16)
-            low = (weight - high.astype(F32)).astype(BF16)
-            push = push_ref[facet]
-            result = jnp.dot(push, high, preferred_element_type=F32) + jnp.dot(
-                push, low, preferred_element_type=F32
-            )
-            done.append((block, facet >> 2, result[0:8] + result[8:16]))
-        for block, boulder, result in done:
-            force_sum[block] += result
-            load_sum[boulder] += result[:, :128] + result[:, 128:]
+        place = 2 * GROUP * index
+        for half in range(2):
+            here = place + half * GROUP
+            for member in range(GROUP):
+                exponents(here + 2 * GROUP + member, gaps[half][member])
+                weigh(gaps[1 - half][member], weights[1 - half][member])
+                add(here + member, weights[half][member])
         return carry
 
-    lax.fori_loop(0, (total + UNROLL - 1) // UNROLL, step, 0)
+    lax.fori_loop(0, (total + 2 * GROUP - 1) // (2 * GROUP), step, 0)
     for index in range(DEPTH):
         for block in range(BLOCKS):
-            force_ref[index, 3 * block : 3 * block + 3, :] = force_sum[
-                index * BLOCKS + block, 0:3, :
-            ]
+            for part in range(3):
+                force_ref[index, 8 * part + block : 8 * part + block + 1, :] = force_sum[
+                    index * BLOCKS + block, part : part + 1, :
+                ]
     load_ref[...] = load_sum[0 : 2 * PLANE]
 
 
@@ -233,10 +253,8 @@
     for index in range(1, DEPTH):
         total = total + force_ref[index]
     scaled = TIME_STEP * mass_ref[...]
-    for block in range(BLOCKS):
-        out_ref[block] = velocity_ref[block] + scaled[block : block + 1, :] * total[
-            3 * block : 3 * block + 3, :
-        ]
+    for part in range(3):
+        out_ref[part] = velocity_ref[part] + scaled * total[8 * part : 8 * part + 8, :]
 
 
 def sum_loads(load_ref, out_ref):
@@ -318,10 +336,8 @@
         facet_geometry, boulder_pose
     )
     facets = swap(facets, axis_index_groups=planes)
-    particles = call(
-        pair_message, shape((DEPTH, 56, 128), F32), [VMEM] * 6, [pltpu.VMEM((24, 256), F32)]
-    )(
-        particle_position,
+    particles = call(pair_message, shape((DEPTH, 56, 128), F32), [VMEM] * 6)(
+        particle_position.transpose(1, 0, 2),
         boulder_slot.reshape(2, 128),
         block_home.reshape(16, 128),
         pair_facet.reshape(pairs, 1),
@@ -341,13 +357,15 @@
         [VMEM] * 3,
         [
             pltpu.SMEM((DEPTH, 8, 128), F32),
-            pltpu.SMEM((DEPTH * 48 + UNROLL,), jnp.int32),
+            pltpu.SMEM((DEPTH * 48 + 6 * GROUP,), jnp.int32),
             pltpu.VMEM((TERMS, BLOCKS, 256), F32),
             pltpu.VMEM((PARTICLES + 1, TERMS, 256), BF16),
             pltpu.VMEM((PARTICLES + 1, 8, 256), F32),
             pltpu.VMEM((2 * PLANE + 1, 8, 128), F32),
             pltpu.SemaphoreType.DMA,
-        ],
+        ]
+        + [pltpu.VMEM((256, 256), F32)] * (2 * GROUP)
+        + [pltpu.VMEM((256, 256), BF16)] * (2 * GROUP),
     )(terms, push, particles)
     load = swap(load, axis_index_groups=planes)
     load = call(sum_loads, shape((2, 8, 128), F32), [VMEM])(load.reshape(PLANE, 2, 8, 128))
@@ -356,10 +374,11 @@
         finish_boulders, shape(boulder_velocity.shape, F32), [VMEM, VMEM, SMEM, VMEM]
     )(load, other, boulder_pose, boulder_velocity)
     force = swap(force, axis_index_groups=columns)
-    new_velocity = call(finish_particles, shape(particle_velocity.shape, F32), [VMEM] * 3)(
-        force, particle_velocity, inverse_mass
-    )
-    return (new_velocity, boulder_motion)
+    velocity = particle_velocity.transpose(1, 0, 2)
+    new_velocity = call(finish_particles, shape(velocity.shape, F32), [VMEM] * 3)(
+        force, velocity, inverse_mass
+    )
+    return (new_velocity.transpose(1, 0, 2), boulder_motion)
 
 
 def solution(mesh):

time: 124 us -> 89.4 us (0.72)
  Pallas kernels: 60.2 us -> 24.9 us
  local copies, waits for them, and re-layouts: 6.59 us -> 12.6 us
  starting transfers between devices: 26.5 us -> 23.3 us
  blocking collectives: 15.7 us -> 14.2 us
    pallas_call x1, Pallas kernels: 47 us -> 14.2 us  [shards(): call(contact, [shape((DEPTH, 24, 256), F32), shape((2 * PLANE, 8, 128), F...]
    unnamed x18 -> x21, local copies, waits for them, and re-layouts: 4.21 us -> 10.3 us
    pallas_call x1, Pallas kernels: 9.06 us -> 5.8 us  [shards(): call(facet_features, [shape((FACETS + 1, 256, TERMS), BF16), shape((FACET...]
    all_to_all x1, starting transfers between devices: 10.4 us -> 7.23 us  [shards(): force = swap(force, axis_index_groups=columns)]
    all_to_all x1, blocking collectives: 15.7 us -> 14.2 us  [shards(): load = swap(load, axis_index_groups=planes)]
where the time goes in v2:
time: 89.4 us; the launch traced here: 88.5 us
  Pallas kernels  24.9 us (28%)
  starting transfers between devices  23.3 us (26%)
  blocking collectives  14.2 us (16%)
  waiting for transfers between devices  12.8 us (14%)
  local copies, waits for them, and re-layouts  12.6 us (14%)
    pallas_call x1, Pallas kernels, shards(): call(contact, [shape((DEPTH, 24, 256), F32), shape((2 * PLANE, 8, 128), F...  14.2 us
    all_to_all x1, blocking collectives, shards(): load = swap(load, axis_index_groups=planes)  14.2 us
    unnamed x21, local copies, waits for them, and re-layouts  10.3 us
    all_to_all x1, starting transfers between devices, shards(): particles = swap(particles, axis_index_groups=columns)  8.47 us
    all_to_all x1, starting transfers between devices, shards(): facets = swap(facets, axis_index_groups=planes)  7.48 us
    all_to_all x1, waiting for transfers between devices, shards(): force = swap(force, axis_index_groups=columns)  7.25 us
    all_to_all x1, starting transfers between devices, shards(): force = swap(force, axis_index_groups=columns)  7.23 us
    pallas_call x1, Pallas kernels, shards(): call(facet_features, [shape((FACETS + 1, 256, TERMS), BF16), shape((FACET...  5.8 us
  transfers between devices with their start and end apart: 4, of which 4 were waited for; matrix products, arithmetic and copies ran while one was open for 3% of the time, Pallas kernels for 10%

profile of v2, /device:TPU:2, one launch (start us, length us, event | category | flops | bytes accessed | tf_op | source)
XLA Modules:
  0.0 88.5 jit_solution(10705952379741702481)
XLA Ops:
  0.7 0.8 copy.14.geometry_ref
  1.5 0.7 copy-done.6
  2.1 1.5 %shard_map.122 = f32[16,8,8,128]{3,2,1,0:T(8,128)} custom-call(f32[2,4,7,128]{3,2,1,0:T(8,128)S(1)} %copy.14.geometry_ref, f32[2,16]{1,0:T(2,128)S(1)} %copy-done.6), custom_call_target="tpu_custom_call" | custom-call | tf_op jit(solution)/shard_map/pallas_call | solution.py:335
  3.6 7.5 %all-to-all-start = ((f32[16,8,8,128]{3,2,1,0:T(8,128)}), f32[16,8,8,128]{3,2,1,0:T(8,128)S(1)}, u32[]{:S(2)}, u32[]{:S(2)}) async-start(f32[16,8,8,128]{3,2,1,0:T(8,128)} %shard_map.122), calls=%async_computation | async-start | bytes 1048576 | tf_op jit(solution)/shard_map/all_to_all | solution.py:338
  11.1 0.8 copy.15.facet_ref
  11.9 0.8 copy.16.block_ref
  12.7 0.8 copy.17.active_ref
  13.5 0.7 copy-done.2
  14.2 0.7 copy-done.4
  14.9 0.7 copy-done.8
  15.6 1.5 %shard_map.124 = f32[8,56,128]{2,1,0:T(8,128)} custom-call(f32[3,8,256]{2,1,0:T(8,128)S(1)} %bitcast.10, s32[2,128]{1,0:T(2,128)S(1)} %bitcast.13, s32[16,128]{1,0:T(8,128)S(1)} %bitcast.12, s32[192,1]{1,0:T(8,128)S(1)} %copy.15.facet_ref, s32[192,1]{1,0:T(8,128)S(1)} %copy.16.block_ref, s32[192,1]{1,0:T(8,128)S(1)} %copy.17.active_ref), custom_call_target="tpu_custom_call" | custom-call | tf_op jit(solution)/shard_map/pallas_call | solution.py:339
  17.1 3.3 %all-to-all-done.world_ref = f32[16,8,8,128]{3,2,1,0:T(8,128)S(1)} async-done(((f32[16,8,8,128]{3,2,1,0:T(8,128)}), f32[16,8,8,128]{3,2,1,0:T(8,128)S(1)}, u32[]{:S(2)}, u32[]{:S(2)}) %all-to-all-start) | async-done | bytes 524320 | tf_op jit(solution)/shard_map/all_to_all | solution.py:338
  20.4 8.5 %all-to-all-start.1 = ((f32[8,56,128]{2,1,0:T(8,128)}), f32[8,56,128]{2,1,0:T(8,128)S(1)}, u32[]{:S(2)}, u32[]{:S(2)}) async-start(f32[8,56,128]{2,1,0:T(8,128)} %shard_map.124), calls=%async_computation.1 | async-start | bytes 458752 | tf_op jit(solution)/shard_map/all_to_all | solution.py:347
  28.9 5.8 %shard_map.123 = (bf16[129,256,32]{2,1,0:T(8,128)(2,1)S(1)}, bf16[129,16,128]{2,1,0:T(8,128)(2,1)S(1)}) custom-call(f32[16,8,8,128]{3,2,1,0:T(8,128)S(1)} %all-to-all-done.world_ref), custom_call_target="tpu_custom_call" | custom-call | tf_op jit(solution)/shard_map/pallas_call | solution.py:348
  34.7 3.3 %copy-done = bf16[129,256,32]{2,1,0:T(8,128)(2,1)} copy-done((bf16[129,256,32]{2,1,0:T(8,128)(2,1)}, bf16[129,256,32]{2,1,0:T(8,128)(2,1)S(1)}, u32[]{:S(2)}) %copy-start) | copy-done | bytes 2113560
  37.9 1.1 %all-to-all-done.1.given_ref = f32[8,56,128]{2,1,0:T(8,128)S(1)} async-done(((f32[8,56,128]{2,1,0:T(8,128)}), f32[8,56,128]{2,1,0:T(8,128)S(1)}, u32[]{:S(2)}, u32[]{:S(2)}) %all-to-all-start.1) | async-done | bytes 229408 | tf_op jit(solution)/shard_map/all_to_all | solution.py:347
  39.0 3.4 %copy-done.1 = bf16[129,256,32]{2,1,0:T(8,128)(2,1)S(1)} copy-done((bf16[129,256,32]{2,1,0:T(8,128)(2,1)S(1)}, bf16[129,256,32]{2,1,0:T(8,128)(2,1)}, u32[]{:S(2)}) %copy-start.1) | copy-done | bytes 2113560
  42.4 14.2 %shard_map.125 = (f32[8,24,256]{2,1,0:T(8,128)}, f32[32,8,128]{2,1,0:T(8,128)S(1)}) custom-call(bf16[129,256,32]{2,1,0:T(8,128)(2,1)S(1)} %copy-done.1, bf16[129,16,128]{2,1,0:T(8,128)(2,1)S(1)} %get-tuple-element.7.push_ref, f32[8,56,128]{2,1,0:T(8,128)S(1)} %all-to-all-done.1.given_ref), custom_call_target="tpu_custom_call" | custom-call | tf_op jit(solution)/shard_map/pallas_call | solution.py:354
  56.7 14.2 %all_to_all.20 = f32[32,8,128]{2,1,0:T(8,128)S(1)} all-to-all(f32[32,8,128]{2,1,0:T(8,128)S(1)} %get-tuple-element.9), channel_id=1, replica_groups={{0,2,4,6,8,10,12,14,16,18,20,22,24,26,28,30},{32,34,36,38,40,42,44,46,4..., dimensions={0} | all-to-all | bytes 262144 | tf_op jit(solution)/shard_map/all_to_all | solution.py:370
  70.9 7.2 %all-to-all-start.2 = ((f32[8,24,256]{2,1,0:T(8,128)}), f32[8,24,256]{2,1,0:T(8,128)S(1)}, u32[]{:S(2)}, u32[]{:S(2)}) async-start(f32[8,24,256]{2,1,0:T(8,128)} %get-tuple-element.8), calls=%async_computation.2 | async-start | bytes 393216 | tf_op jit(solution)/shard_map/all_to_all | solution.py:376
  78.2 1.2 %collective-permute-done.other_ref = f32[2,8,128]{2,1,0:T(8,128)S(1)} collective-permute-done((f32[2,8,128]{2,1,0:T(8,128)S(1)}, f32[2,8,128]{2,1,0:T(8,128)S(1)}, u32[]{:S(2)}, u32[]{:S(2)}) %collective-permute-start) | collective-permute-done | bytes 8224 | tf_op jit(solution)/shard_map/ppermute | solution.py:372
  79.4 1.2 %shard_map.128 = f32[2,6]{1,0:T(2,128)} custom-call(f32[2,8,128]{2,1,0:T(8,128)S(1)} %shard_map.127.own_ref, f32[2,8,128]{2,1,0:T(8,128)S(1)} %collective-permute-done.other_ref, f32[2,16]{1,0:T(2,128)S(1)} %copy-done.7, f32[2,6]{1,0:T(2,128)S(1)} %copy-done.9), custom_call_target="tpu_custom_call" | custom-call | tf_op jit(solution)/shard_map/pallas_call | solution.py:373
  80.7 7.2 %all-to-all-done.2.force_ref = f32[8,24,256]{2,1,0:T(8,128)S(1)} async-done(((f32[8,24,256]{2,1,0:T(8,128)}), f32[8,24,256]{2,1,0:T(8,128)S(1)}, u32[]{:S(2)}, u32[]{:S(2)}) %all-to-all-start.2) | async-done | bytes 196640 | tf_op jit(solution)/shard_map/all_to_all | solution.py:376
  87.9 0.6 shard_map.126
  (16 shorter events, 0.1 us)
Async XLA Ops:
  0.6 78.8 %copy-start.7 = (f32[2,16]{1,0:T(2,128)S(1)}, f32[2,16]{1,0:T(2,128)}, u32[]{:S(2)}) copy-start(f32[2,16]{1,0:T(2,128)} %pose_ref.3) | copy-start | bytes 388
  0.6 78.8 %copy-start.9 = (f32[2,6]{1,0:T(2,128)S(1)}, f32[2,6]{1,0:T(2,128)}, u32[]{:S(2)}) copy-start(f32[2,6]{1,0:T(2,128)} %velocity_ref.1) | copy-start | bytes 148
  0.7 87.3 %copy-start.3 = (f32[8,3,256]{2,0,1:T(8,128)S(1)}, f32[8,3,256]{2,0,1:T(8,128)}, u32[]{:S(2)}) copy-start(f32[8,3,256]{2,0,1:T(8,128)} %param.12) | copy-start | bytes 73732
  0.7 87.2 %copy-start.5 = (f32[8,256]{1,0:T(8,128)S(1)}, f32[8,256]{1,0:T(8,128)}, u32[]{:S(2)}) copy-start(f32[8,256]{1,0:T(8,128)} %mass_ref.1) | copy-start | bytes 24580
  1.4 0.7 copy-start.6
  3.6 16.8 %all-to-all-start = ((f32[16,8,8,128]{3,2,1,0:T(8,128)}), f32[16,8,8,128]{3,2,1,0:T(8,128)S(1)}, u32[]{:S(2)}, u32[]{:S(2)}) async-start(f32[16,8,8,128]{3,2,1,0:T(8,128)} %shard_map.122), calls=%async_computation | async-start | bytes 1048576 | tf_op jit(solution)/shard_map/all_to_all | solution.py:338
  13.5 0.7 copy-start.2
  14.2 0.7 copy-start.4
  14.9 0.7 copy-start.8
  20.4 18.6 %all-to-all-start.1 = ((f32[8,56,128]{2,1,0:T(8,128)}), f32[8,56,128]{2,1,0:T(8,128)S(1)}, u32[]{:S(2)}, u32[]{:S(2)}) async-start(f32[8,56,128]{2,1,0:T(8,128)} %shard_map.124), calls=%async_computation.1 | async-start | bytes 458752 | tf_op jit(solution)/shard_map/all_to_all | solution.py:347
  34.7 3.3 %copy-start = (bf16[129,256,32]{2,1,0:T(8,128)(2,1)}, bf16[129,256,32]{2,1,0:T(8,128)(2,1)S(1)}, u32[]{:S(2)}) copy-start(bf16[129,256,32]{2,1,0:T(8,128)(2,1)S(1)} %get-tuple-element.6.terms_ref) | copy-start | bytes 6340612
  39.0 3.4 %copy-start.1 = (bf16[129,256,32]{2,1,0:T(8,128)(2,1)S(1)}, bf16[129,256,32]{2,1,0:T(8,128)(2,1)}, u32[]{:S(2)}) copy-start(bf16[129,256,32]{2,1,0:T(8,128)(2,1)} %copy-done) | copy-start | bytes 6340612
  70.9 17.0 %all-to-all-start.2 = ((f32[8,24,256]{2,1,0:T(8,128)}), f32[8,24,256]{2,1,0:T(8,128)S(1)}, u32[]{:S(2)}, u32[]{:S(2)}) async-start(f32[8,24,256]{2,1,0:T(8,128)} %get-tuple-element.8), calls=%async_computation.2 | async-start | bytes 393216 | tf_op jit(solution)/shard_map/all_to_all | solution.py:376
  78.1 1.3 %collective-permute-start = (f32[2,8,128]{2,1,0:T(8,128)S(1)}, f32[2,8,128]{2,1,0:T(8,128)S(1)}, u32[]{:S(2)}, u32[]{:S(2)}) collective-permute-start(f32[2,8,128]{2,1,0:T(8,128)S(1)} %shard_map.127.own_ref), channel_id=1, source_target_pairs={{0,1},{1,0},{2,3},{3,2},{4,5},{5,4},{6,7},{7,6},{8,9},{9,8},{10,11... | collective-permute-start | bytes 24584 | tf_op jit(solution)/shard_map/ppermute | solution.py:372

commit v3 on v2

--- a/solution.py
+++ b/solution.py
@@ -19,7 +19,7 @@
 FACETS = PLANE * BLOCKS
 PARTICLES = DEPTH * BLOCKS
 GROUP = 2
-VMEM_LIMIT = 24 * 1024 * 1024
+VMEM_LIMIT = 48 * 1024 * 1024
 
 F32 = jnp.float32
 BF16 = jnp.bfloat16
@@ -35,7 +35,7 @@
 def facet_message(geometry_ref, pose_ref, out_ref):
     lane = lax.broadcasted_iota(jnp.int32, (4, 128), 1)
     for boulder in range(2):
-        part = [geometry_ref[boulder, :, row, :] for row in range(7)]
+        part = [geometry_ref[boulder, row] for row in range(7)]
         center = [pose_ref[boulder, row] for row in range(3)]
         rotation = [pose_ref[boulder, 3 + entry] for entry in range(9)]
         rows = []
@@ -103,7 +103,7 @@
         out_ref[target, 48:56, :] = jnp.broadcast_to(listed, (8, 128))
 
 
-def facet_features(world_ref, terms_ref, push_ref, terms_keep, push_keep):
+def facet_features(world_ref, out_ref, push_ref, terms_ref, terms_keep, push_keep, sem):
     terms_keep[...] = jnp.zeros(terms_keep.shape, F32)
     push_keep[...] = jnp.zeros(push_keep.shape, F32)
 
@@ -142,22 +142,27 @@
             terms_ref[index * BLOCKS + block, 0:128, :] = both[:TERMS].T.astype(BF16)
             terms_ref[index * BLOCKS + block, 128:256, :] = both[TERMS:].T.astype(BF16)
             push_ref[index * BLOCKS + block] = push_keep[:, block, :].astype(BF16)
+        part = pl.ds(index * BLOCKS, BLOCKS)
+        pltpu.make_async_copy(terms_ref.at[part], out_ref.at[part], sem).start()
         return carry
 
     lax.fori_loop(0, PLANE, owner, 0)
-    terms_ref[FACETS] = jnp.zeros((256, TERMS), BF16)
     push_ref[FACETS] = jnp.zeros((16, 128), BF16)
+    pltpu.make_async_copy(terms_ref, out_ref, sem).wait()
 
 
 def contact(
-    terms_ref, push_ref, given_ref, force_ref, load_ref,
-    table, listed, point_keep, points, force_sum, load_sum,
+    held_ref, push_ref, given_ref, force_ref, load_ref,
+    terms_ref, terms_sem, table, listed, point_keep, points, force_sum, load_sum,
     sem, *buffers,
 ):
     gaps = [buffers[0:GROUP], buffers[GROUP : 2 * GROUP]]
     weights = [buffers[2 * GROUP : 3 * GROUP], buffers[3 * GROUP : 4 * GROUP]]
     copy = pltpu.make_async_copy(given_ref.at[:, pl.ds(48, 8), :], table, sem)
     copy.start()
+    terms = pltpu.make_async_copy(held_ref, terms_ref.at[pl.ds(0, FACETS)], terms_sem)
+    terms.start()
+    terms_ref[FACETS] = jnp.zeros((256, TERMS), BF16)
     point_keep[...] = jnp.zeros(point_keep.shape, F32)
     force_sum[...] = jnp.zeros(force_sum.shape, F32)
     load_sum[...] = jnp.zeros(load_sum.shape, F32)
@@ -238,6 +243,7 @@
                 add(here + member, weights[half][member])
         return carry
 
+    terms.wait()
     lax.fori_loop(0, (total + 2 * GROUP - 1) // (2 * GROUP), step, 0)
     for index in range(DEPTH):
         for block in range(BLOCKS):
@@ -295,17 +301,16 @@
 
 VMEM = pl.BlockSpec(memory_space=pltpu.VMEM)
 SMEM = pl.BlockSpec(memory_space=pltpu.SMEM)
-
-
-def call(kernel, outs, in_specs, scratch=(), cost=None):
-    single = not isinstance(outs, list)
+ANY = pl.BlockSpec(memory_space=pl.ANY)
+
+
+def call(kernel, outs, in_specs, scratch=(), out_specs=VMEM):
     return pl.pallas_call(
         kernel,
         out_shape=outs,
         in_specs=in_specs,
-        out_specs=VMEM if single else [VMEM] * len(outs),
+        out_specs=out_specs,
         scratch_shapes=list(scratch),
-        cost_estimate=cost,
         compiler_params=pltpu.CompilerParams(vmem_limit_bytes=VMEM_LIMIT),
     )
 
@@ -333,7 +338,7 @@
     shape = jax.ShapeDtypeStruct
 
     facets = call(facet_message, shape((PLANE, 8, BLOCKS, 128), F32), [VMEM, SMEM])(
-        facet_geometry, boulder_pose
+        facet_geometry.transpose(0, 2, 1, 3), boulder_pose
     )
     facets = swap(facets, axis_index_groups=planes)
     particles = call(pair_message, shape((DEPTH, 56, 128), F32), [VMEM] * 6)(
@@ -347,15 +352,23 @@
     particles = swap(particles, axis_index_groups=columns)
     terms, push = call(
         facet_features,
-        [shape((FACETS + 1, 256, TERMS), BF16), shape((FACETS + 1, 16, 128), BF16)],
+        [shape((FACETS, 256, TERMS), BF16), shape((FACETS + 1, 16, 128), BF16)],
         [VMEM],
-        [pltpu.VMEM((2 * TERMS, BLOCKS, 128), F32), pltpu.VMEM((16, BLOCKS, 128), F32)],
+        [
+            pltpu.VMEM((FACETS, 256, TERMS), BF16),
+            pltpu.VMEM((2 * TERMS, BLOCKS, 128), F32),
+            pltpu.VMEM((16, BLOCKS, 128), F32),
+            pltpu.SemaphoreType.DMA,
+        ],
+        out_specs=[ANY, VMEM],
     )(facets)
     force, load = call(
         contact,
         [shape((DEPTH, 24, 256), F32), shape((2 * PLANE, 8, 128), F32)],
-        [VMEM] * 3,
+        [ANY, VMEM, VMEM],
         [
+            pltpu.VMEM((FACETS + 1, 256, TERMS), BF16),
+            pltpu.SemaphoreType.DMA,
             pltpu.SMEM((DEPTH, 8, 128), F32),
             pltpu.SMEM((DEPTH * 48 + 6 * GROUP,), jnp.int32),
             pltpu.VMEM((TERMS, BLOCKS, 256), F32),
@@ -366,9 +379,28 @@
         ]
         + [pltpu.VMEM((256, 256), F32)] * (2 * GROUP)
         + [pltpu.VMEM((256, 256), BF16)] * (2 * GROUP),
+        out_specs=[VMEM, VMEM],
     )(terms, push, particles)
-    load = swap(load, axis_index_groups=planes)
-    load = call(sum_loads, shape((2, 8, 128), F32), [VMEM])(load.reshape(PLANE, 2, 8, 128))
+    grid = load.reshape(4, 4, 2, 8, 128)
+    spot = lax.axis_index("wide") % PLANE
+    down, across = spot // 4, spot % 4
+
+    def shift(step, unit):
+        moves = []
+        for device in range(owners):
+            place = device // unit % 4
+            moves.append((device, device + ((place + step) % 4 - place) * unit))
+        return moves
+
+    def pick(array, axis, index):
+        return lax.dynamic_index_in_dim(array, index % 4, axis, keepdims=False)
+
+    row = pick(grid, 1, across)
+    for step in (1, 2, 3):
+        row = row + lax.ppermute(pick(grid, 1, across + step), "wide", shift(step, 1))
+    load = pick(row, 0, down)
+    for step in (1, 2, 3):
+        load = load + lax.ppermute(pick(row, 0, down + step), "wide", shift(step, 4))
     other = lax.ppermute(load, "narrow", [(0, 1), (1, 0)])
     boulder_motion = call(
         finish_boulders, shape(boulder_velocity.shape, F32), [VMEM, VMEM, SMEM, VMEM]

time: 89.4 us -> 77.4 us (0.87)
  the two profiles are of different devices: /device:TPU:2 before, /device:TPU:1 now
where the time goes in v3:
time: 77.4 us; the launch traced here: 77 us
  starting transfers between devices  32.8 us (42%)
  Pallas kernels  26.4 us (34%)
  waiting for transfers between devices  11 us (14%)
  local copies, waits for them, and re-layouts  5.96 us (8%)
    pallas_call x1, Pallas kernels, shards(): call(contact, [shape((DEPTH, 24, 256), F32), shape((2 * PLANE, 8, 128), F...  14.9 us
    all_to_all x1, starting transfers between devices, shards(): particles = swap(particles, axis_index_groups=columns)  8.19 us
    all_to_all x1, starting transfers between devices, shards(): facets = swap(facets, axis_index_groups=planes)  7.58 us
    pallas_call x1, Pallas kernels, shards(): call(facet_features, [shape((FACETS, 256, TERMS), BF16), shape((FACETS +...  6.66 us
    ppermute x1, starting transfers between devices, shards(): other = lax.ppermute(load, 'narrow', [(0, 1), (1, 0)])  6.29 us
    ppermute x3, starting transfers between devices, shards(): lax.ppermute(pick(grid, 1, across + step), 'wide', shift(step, 1))  5.16 us
    all_to_all x1, waiting for transfers between devices, shards(): facets = swap(facets, axis_index_groups=planes)  4.3 us
    unnamed x18, local copies, waits for them, and re-layouts  3.55 us
  transfers between devices with their start and end apart: 10, of which 7 were waited for; matrix products, arithmetic and copies ran while one was open for 3% of the time, Pallas kernels for 12%

profile of v3, /device:TPU:1, one launch (start us, length us, event | category | flops | bytes accessed | tf_op | source)
XLA Modules:
  0.0 77.0 jit_solution(936523346575938859)
XLA Ops:
  0.7 0.7 copy-done
  2.1 1.5 %shard_map.122 = f32[16,8,8,128]{3,2,1,0:T(8,128)} custom-call(f32[2,7,4,128]{3,2,1,0:T(4,128)S(1)} %bitcast.36, f32[2,16]{1,0:T(2,128)S(1)} %copy-done.5), custom_call_target="tpu_custom_call" | custom-call | tf_op jit(solution)/shard_map/pallas_call | solution.py:340
  3.5 7.6 %all-to-all-start = ((f32[16,8,8,128]{3,2,1,0:T(8,128)}), f32[16,8,8,128]{3,2,1,0:T(8,128)S(1)}, u32[]{:S(2)}, u32[]{:S(2)}) async-start(f32[16,8,8,128]{3,2,1,0:T(8,128)} %shard_map.122), calls=%async_computation | async-start | bytes 1048576 | tf_op jit(solution)/shard_map/all_to_all | solution.py:343
  11.1 0.8 %copy.13.facet_ref = s32[192,1]{1,0:T(8,128)S(1)} copy(s32[192,1]{0,1:T(1,128)} %bitcast.42) | data formatting | bytes 1536 | tf_op jit(solution)/shard_map/reshape | solution.py:348
  11.9 0.8 %copy.14.block_ref = s32[192,1]{1,0:T(8,128)S(1)} copy(s32[192,1]{0,1:T(1,128)} %bitcast.43) | data formatting | bytes 1536 | tf_op jit(solution)/shard_map/reshape | solution.py:349
  12.7 0.8 %copy.15.active_ref = s32[192,1]{1,0:T(8,128)S(1)} copy(s32[192,1]{0,1:T(1,128)} %bitcast.44) | data formatting | bytes 1536 | tf_op jit(solution)/shard_map/reshape | solution.py:350
  13.5 0.7 copy-done.1
  14.3 0.7 copy-done.3
  15.7 1.5 %shard_map.124 = f32[8,56,128]{2,1,0:T(8,128)} custom-call(f32[3,8,256]{2,1,0:T(8,128)S(1)} %bitcast.37, s32[2,128]{1,0:T(2,128)S(1)} %bitcast.40, s32[16,128]{1,0:T(8,128)S(1)} %bitcast.39, s32[192,1]{1,0:T(8,128)S(1)} %copy.13.facet_ref, s32[192,1]{1,0:T(8,128)S(1)} %copy.14.block_ref, s32[192,1]{1,0:T(8,128)S(1)} %copy.15.active_ref), custom_call_target="tpu_custom_call" | custom-call | tf_op jit(solution)/shard_map/pallas_call | solution.py:344
  17.1 4.3 %all-to-all-done.world_ref = f32[16,8,8,128]{3,2,1,0:T(8,128)S(1)} async-done(((f32[16,8,8,128]{3,2,1,0:T(8,128)}), f32[16,8,8,128]{3,2,1,0:T(8,128)S(1)}, u32[]{:S(2)}, u32[]{:S(2)}) %all-to-all-start) | async-done | bytes 524320 | tf_op jit(solution)/shard_map/all_to_all | solution.py:343
  21.4 8.2 %all-to-all-start.1 = ((f32[8,56,128]{2,1,0:T(8,128)}), f32[8,56,128]{2,1,0:T(8,128)S(1)}, u32[]{:S(2)}, u32[]{:S(2)}) async-start(f32[8,56,128]{2,1,0:T(8,128)} %shard_map.124), calls=%async_computation.1 | async-start | bytes 458752 | tf_op jit(solution)/shard_map/all_to_all | solution.py:352
  29.6 6.7 %shard_map.123 = (bf16[128,256,32]{2,1,0:T(8,128)(2,1)}, bf16[129,16,128]{2,1,0:T(8,128)(2,1)S(1)}) custom-call(f32[16,8,8,128]{3,2,1,0:T(8,128)S(1)} %all-to-all-done.world_ref), custom_call_target="tpu_custom_call" | custom-call | tf_op jit(solution)/shard_map/pallas_call | solution.py:353
  36.3 2.4 %all-to-all-done.1.given_ref = f32[8,56,128]{2,1,0:T(8,128)S(1)} async-done(((f32[8,56,128]{2,1,0:T(8,128)}), f32[8,56,128]{2,1,0:T(8,128)S(1)}, u32[]{:S(2)}, u32[]{:S(2)}) %all-to-all-start.1) | async-done | bytes 229408 | tf_op jit(solution)/shard_map/all_to_all | solution.py:352
  38.7 14.9 %shard_map.125 = (f32[8,24,256]{2,1,0:T(8,128)}, f32[32,8,128]{2,1,0:T(8,128)S(1)}) custom-call(bf16[128,256,32]{2,1,0:T(8,128)(2,1)} %get-tuple-element.6.held_ref, bf16[129,16,128]{2,1,0:T(8,128)(2,1)S(1)} %get-tuple-element.7.push_ref, f32[8,56,128]{2,1,0:T(8,128)S(1)} %all-to-all-done.1.given_ref), custom_call_target="tpu_custom_call" | custom-call | tf_op jit(solution)/shard_map/pallas_call | solution.py:365
  53.6 2.1 %collective-permute-start.2 = (f32[4,2,8,128]{3,2,1,0:T(8,128)S(1)}, f32[4,2,8,128]{3,2,1,0:T(8,128)S(1)}, u32[]{:S(2)}, u32[]{:S(2)}) collective-permute-start(f32[4,2,8,128]{3,2,1,0:T(8,128)S(1)} %get-tuple-element.11), channel_id=1, source_target_pairs={{0,6},{2,0},{4,2},{6,4},{8,14},{10,8},{12,10},{14,12},{16,22},{18,... | collective-permute-start | bytes 98312 | tf_op jit(solution)/shard_map/ppermute | solution.py:400
  55.7 3.1 %collective-permute-start.1 = (f32[4,2,8,128]{3,2,1,0:T(8,128)S(1)}, f32[4,2,8,128]{3,2,1,0:T(8,128)S(1)}, u32[]{:S(2)}, u32[]{:S(2)}) collective-permute-start(f32[4,2,8,128]{3,2,1,0:T(8,128)S(1)} %get-tuple-element.12), channel_id=1, source_target_pairs={{0,4},{2,6},{4,0},{6,2},{8,12},{10,14},{12,8},{14,10},{16,20},{18,... | collective-permute-start | bytes 98312 | tf_op jit(solution)/shard_map/ppermute | solution.py:400
  58.8 3.4 %all-to-all-start.2 = ((f32[8,24,256]{2,1,0:T(8,128)}), f32[8,24,256]{2,1,0:T(8,128)S(1)}, u32[]{:S(2)}, u32[]{:S(2)}) async-start(f32[8,24,256]{2,1,0:T(8,128)} %get-tuple-element.8), calls=%async_computation.2 | async-start | bytes 393216 | tf_op jit(solution)/shard_map/all_to_all | solution.py:408
  62.8 0.7 collective-permute-start.5
  63.5 0.8 %collective-permute-start.4 = (f32[2,8,128]{2,1,0:T(8,128)S(1)}, f32[2,8,128]{2,1,0:T(8,128)S(1)}, u32[]{:S(2)}, u32[]{:S(2)}) collective-permute-start(f32[2,8,128]{2,1,0:T(8,128)S(1)} %get-tuple-element.15), channel_id=1, source_target_pairs={{0,16},{2,18},{4,20},{6,22},{8,24},{10,26},{12,28},{14,30},{16,0},... | collective-permute-start | bytes 24584 | tf_op jit(solution)/shard_map/ppermute | solution.py:403
  64.3 0.8 collective-permute-start.3
  65.4 2.1 %collective-permute-done.4 = f32[2,8,128]{2,1,0:T(8,128)S(1)} collective-permute-done((f32[2,8,128]{2,1,0:T(8,128)S(1)}, f32[2,8,128]{2,1,0:T(8,128)S(1)}, u32[]{:S(2)}, u32[]{:S(2)}) %collective-permute-start.4) | collective-permute-done | bytes 8224 | tf_op jit(solution)/shard_map/ppermute | solution.py:403
  68.0 6.3 %collective-permute-start.6 = (f32[2,8,128]{2,1,0:T(8,128)S(1)}, f32[2,8,128]{2,1,0:T(8,128)S(1)}, u32[]{:S(2)}, u32[]{:S(2)}) collective-permute-start(f32[2,8,128]{2,1,0:T(8,128)S(1)} %fusion.3.own_ref), channel_id=1, source_target_pairs={{0,1},{1,0},{2,3},{3,2},{4,5},{5,4},{6,7},{7,6},{8,9},{9,8},{10,11... | collective-permute-start | bytes 24584 | tf_op jit(solution)/shard_map/ppermute | solution.py:404
  74.3 0.8 %collective-permute-done.6.other_ref = f32[2,8,128]{2,1,0:T(8,128)S(1)} collective-permute-done((f32[2,8,128]{2,1,0:T(8,128)S(1)}, f32[2,8,128]{2,1,0:T(8,128)S(1)}, u32[]{:S(2)}, u32[]{:S(2)}) %collective-permute-start.6) | collective-permute-done | bytes 8224 | tf_op jit(solution)/shard_map/ppermute | solution.py:404
  75.1 1.2 %shard_map.127 = f32[2,6]{1,0:T(2,128)} custom-call(f32[2,8,128]{2,1,0:T(8,128)S(1)} %fusion.3.own_ref, f32[2,8,128]{2,1,0:T(8,128)S(1)} %collective-permute-done.6.other_ref, f32[2,16]{1,0:T(2,128)S(1)} %copy-done.6, f32[2,6]{1,0:T(2,128)S(1)} %copy-done.8), custom_call_target="tpu_custom_call" | custom-call | tf_op jit(solution)/shard_map/pallas_call | solution.py:405
  (27 shorter events, 3.5 us)
Async XLA Ops:
  0.6 74.5 %copy-start.6 = (f32[2,16]{1,0:T(2,128)S(1)}, f32[2,16]{1,0:T(2,128)}, u32[]{:S(2)}) copy-start(f32[2,16]{1,0:T(2,128)} %pose_ref.3) | copy-start | bytes 388
  0.6 0.8 copy-start
  1.4 0.7 copy-start.5
  2.1 73.0 %copy-start.8 = (f32[2,6]{1,0:T(2,128)S(1)}, f32[2,6]{1,0:T(2,128)}, u32[]{:S(2)}) copy-start(f32[2,6]{1,0:T(2,128)} %velocity_ref.1) | copy-start | bytes 148
  2.1 74.3 %copy-start.2 = (f32[8,3,256]{2,0,1:T(8,128)S(1)}, f32[8,3,256]{2,0,1:T(8,128)}, u32[]{:S(2)}) copy-start(f32[8,3,256]{2,0,1:T(8,128)} %param.12) | copy-start | bytes 73732
  2.1 74.3 %copy-start.4 = (f32[8,256]{1,0:T(8,128)S(1)}, f32[8,256]{1,0:T(8,128)}, u32[]{:S(2)}) copy-start(f32[8,256]{1,0:T(8,128)} %mass_ref.1) | copy-start | bytes 24580
  3.5 17.9 %all-to-all-start = ((f32[16,8,8,128]{3,2,1,0:T(8,128)}), f32[16,8,8,128]{3,2,1,0:T(8,128)S(1)}, u32[]{:S(2)}, u32[]{:S(2)}) async-start(f32[16,8,8,128]{3,2,1,0:T(8,128)} %shard_map.122), calls=%async_computation | async-start | bytes 1048576 | tf_op jit(solution)/shard_map/all_to_all | solution.py:343
  13.5 0.7 copy-start.1
  14.3 0.7 copy-start.3
  15.0 0.7 copy-start.7
  21.4 17.2 %all-to-all-start.1 = ((f32[8,56,128]{2,1,0:T(8,128)}), f32[8,56,128]{2,1,0:T(8,128)S(1)}, u32[]{:S(2)}, u32[]{:S(2)}) async-start(f32[8,56,128]{2,1,0:T(8,128)} %shard_map.124), calls=%async_computation.1 | async-start | bytes 458752 | tf_op jit(solution)/shard_map/all_to_all | solution.py:352
  53.6 8.6 %collective-permute-start.2 = (f32[4,2,8,128]{3,2,1,0:T(8,128)S(1)}, f32[4,2,8,128]{3,2,1,0:T(8,128)S(1)}, u32[]{:S(2)}, u32[]{:S(2)}) collective-permute-start(f32[4,2,8,128]{3,2,1,0:T(8,128)S(1)} %get-tuple-element.11), channel_id=1, source_target_pairs={{0,6},{2,0},{4,2},{6,4},{8,14},{10,8},{12,10},{14,12},{16,22},{18,... | collective-permute-start | bytes 98312 | tf_op jit(solution)/shard_map/ppermute | solution.py:400
  55.7 6.5 %collective-permute-start.1 = (f32[4,2,8,128]{3,2,1,0:T(8,128)S(1)}, f32[4,2,8,128]{3,2,1,0:T(8,128)S(1)}, u32[]{:S(2)}, u32[]{:S(2)}) collective-permute-start(f32[4,2,8,128]{3,2,1,0:T(8,128)S(1)} %get-tuple-element.12), channel_id=1, source_target_pairs={{0,4},{2,6},{4,0},{6,2},{8,12},{10,14},{12,8},{14,10},{16,20},{18,... | collective-permute-start | bytes 98312 | tf_op jit(solution)/shard_map/ppermute | solution.py:400
  58.8 4.0 %collective-permute-start = (f32[4,2,8,128]{3,2,1,0:T(8,128)S(1)}, f32[4,2,8,128]{3,2,1,0:T(8,128)S(1)}, u32[]{:S(2)}, u32[]{:S(2)}) collective-permute-start(f32[4,2,8,128]{3,2,1,0:T(8,128)S(1)} %get-tuple-element.10), channel_id=1, source_target_pairs={{0,2},{2,4},{4,6},{6,0},{8,10},{10,12},{12,14},{14,8},{16,18},{18,... | collective-permute-start | bytes 98312 | tf_op jit(solution)/shard_map/ppermute | solution.py:400
  58.8 17.6 %all-to-all-start.2 = ((f32[8,24,256]{2,1,0:T(8,128)}), f32[8,24,256]{2,1,0:T(8,128)S(1)}, u32[]{:S(2)}, u32[]{:S(2)}) async-start(f32[8,24,256]{2,1,0:T(8,128)} %get-tuple-element.8), calls=%async_computation.2 | async-start | bytes 393216 | tf_op jit(solution)/shard_map/all_to_all | solution.py:408
  62.8 2.6 %collective-permute-start.5 = (f32[2,8,128]{2,1,0:T(8,128)S(1)}, f32[2,8,128]{2,1,0:T(8,128)S(1)}, u32[]{:S(2)}, u32[]{:S(2)}) collective-permute-start(f32[2,8,128]{2,1,0:T(8,128)S(1)} %get-tuple-element.14), channel_id=1, source_target_pairs={{0,24},{2,26},{4,28},{6,30},{8,0},{10,2},{12,4},{14,6},{16,8},{18,... | collective-permute-start | bytes 24584 | tf_op jit(solution)/shard_map/ppermute | solution.py:403
  63.5 4.0 %collective-permute-start.4 = (f32[2,8,128]{2,1,0:T(8,128)S(1)}, f32[2,8,128]{2,1,0:T(8,128)S(1)}, u32[]{:S(2)}, u32[]{:S(2)}) collective-permute-start(f32[2,8,128]{2,1,0:T(8,128)S(1)} %get-tuple-element.15), channel_id=1, source_target_pairs={{0,16},{2,18},{4,20},{6,22},{8,24},{10,26},{12,28},{14,30},{16,0},... | collective-permute-start | bytes 24584 | tf_op jit(solution)/shard_map/ppermute | solution.py:403
  64.3 3.7 %collective-permute-start.3 = (f32[2,8,128]{2,1,0:T(8,128)S(1)}, f32[2,8,128]{2,1,0:T(8,128)S(1)}, u32[]{:S(2)}, u32[]{:S(2)}) collective-permute-start(f32[2,8,128]{2,1,0:T(8,128)S(1)} %get-tuple-element.13), channel_id=1, source_target_pairs={{0,8},{2,10},{4,12},{6,14},{8,16},{10,18},{12,20},{14,22},{16,24},... | collective-permute-start | bytes 24584 | tf_op jit(solution)/shard_map/ppermute | solution.py:403
  68.0 7.1 %collective-permute-start.6 = (f32[2,8,128]{2,1,0:T(8,128)S(1)}, f32[2,8,128]{2,1,0:T(8,128)S(1)}, u32[]{:S(2)}, u32[]{:S(2)}) collective-permute-start(f32[2,8,128]{2,1,0:T(8,128)S(1)} %fusion.3.own_ref), channel_id=1, source_target_pairs={{0,1},{1,0},{2,3},{3,2},{4,5},{5,4},{6,7},{7,6},{8,9},{9,8},{10,11... | collective-permute-start | bytes 24584 | tf_op jit(solution)/shard_map/ppermute | solution.py:404

commit v4 on v3

--- a/solution.py
+++ b/solution.py
@@ -16,10 +16,13 @@
 DEPTH = 8
 BLOCKS = 8
 TERMS = 32
+PITCH = 9
 FACETS = PLANE * BLOCKS
+ROW = 4 * BLOCKS
 PARTICLES = DEPTH * BLOCKS
 GROUP = 2
 VMEM_LIMIT = 48 * 1024 * 1024
+WHOLE_VMEM = 63 * 1024 * 1024
 
 F32 = jnp.float32
 BF16 = jnp.bfloat16
@@ -32,7 +35,23 @@
     return high, middle, (rest - middle).astype(BF16).astype(F32)
 
 
-def facet_message(geometry_ref, pose_ref, out_ref):
+def put(keep, row, value):
+    keep[PITCH * row : PITCH * row + BLOCKS, :] = value
+
+
+def fetch(pairs, sems):
+    copies = [
+        pltpu.make_async_copy(origin, target, sems.at[index])
+        for index, (origin, target) in enumerate(pairs)
+    ]
+    for copy in copies:
+        copy.start()
+    for copy in copies:
+        copy.wait()
+
+
+def facet_message(geometry_at, pose_at, out_ref, geometry_ref, pose_ref, sems):
+    fetch([(geometry_at, geometry_ref), (pose_at, pose_ref)], sems)
     lane = lax.broadcasted_iota(jnp.int32, (4, 128), 1)
     for boulder in range(2):
         part = [geometry_ref[boulder, row] for row in range(7)]
@@ -54,15 +73,22 @@
                 jnp.where(lane == 1, center[1], jnp.where(lane == 2, center[2], 0.0)),
             )
         )
-        for target in range(PLANE):
-            for row in range(8):
-                out_ref[target, row, 4 * boulder : 4 * boulder + 4, :] = rows[row]
-
-
-def pair_message(
-    position_ref, slot_ref, home_ref, facet_ref, block_ref, active_ref, out_ref
-):
-    pairs = facet_ref.shape[0]
+        for row in range(8):
+            out_ref[row, 4 * boulder : 4 * boulder + 4, :] = rows[row]
+
+
+def pair_message(*refs):
+    held, out_ref, (position_ref, slot_ref, home_ref), rows, sems = (
+        refs[:6], refs[7], refs[8:11], refs[11:14], refs[14],
+    )
+    fetch(list(zip(held, (position_ref, slot_ref, home_ref, *rows))), sems)
+    facet, block, active = [row[...] for row in rows]
+    pairs = facet.shape[1]
+    packed = jnp.where(active != 0, 1, 0) + 2 * facet + 2048 * block
+    packed = jnp.broadcast_to(packed, (128, pairs)).T[:, 0:1]
+    active = (packed & 1) != 0
+    facet = (packed >> 1) & 1023
+    block = packed >> 11
     lane = lax.broadcasted_iota(jnp.int32, (pairs, 128), 1)
 
     def look_up(table, index):
@@ -73,19 +99,21 @@
         picked = jnp.where(lane == (index & 127), picked, 0.0)
         return jnp.sum(picked, axis=1, keepdims=True).astype(jnp.int32)
 
-    facet = facet_ref[...]
     slot = look_up(slot_ref[...], facet >> 2)
-    local_block = look_up(home_ref[...] & 7, block_ref[...])
+    local_block = look_up(home_ref[...] & 7, block)
     plane = slot >> 5
     code = local_block * 256 + ((slot & 31) * 4 + (facet & 3))
     code = code.astype(F32)
-    active = active_ref[...] != 0
-    member = jnp.logical_and(lane == plane, active).astype(F32)
+    late = ((lax.axis_index("wide") >> 2) - (slot >> 3)) & 2
+    member = jnp.logical_and(lane == plane + DEPTH * (late >> 1), active).astype(F32)
     row = lax.broadcasted_iota(jnp.int32, (pairs, pairs), 0)
     column = lax.broadcasted_iota(jnp.int32, (pairs, pairs), 1)
     below = (column < row).astype(F32).astype(BF16)
     before = jnp.dot(below, member.astype(BF16), preferred_element_type=F32)
-    rank = jnp.sum(before * member, axis=1, keepdims=True).astype(jnp.int32)
+    rank = jnp.sum(before * member, axis=1, keepdims=True)
+    early = jnp.sum(member, axis=0, keepdims=True)
+    ahead = jnp.where(jnp.logical_and(lane == plane, late > 0), early, 0.0)
+    rank = (rank + jnp.sum(ahead, axis=1, keepdims=True)).astype(jnp.int32)
     rank = jnp.where(active, rank, 255)
     spread = jnp.where(lane == rank, code, 0.0)
     lane_row = lax.broadcasted_iota(jnp.int32, (1, 128), 1)
@@ -93,7 +121,8 @@
         here = jnp.logical_and(plane == target, active)
         listed = jnp.sum(jnp.where(here, spread, 0.0), axis=0, keepdims=True)
         count = jnp.sum(here.astype(F32), axis=0, keepdims=True)
-        listed = jnp.where(lane_row == 127, count, listed)
+        first = jnp.sum(jnp.where(lane_row == target, early, 0.0), axis=1, keepdims=True)
+        listed = jnp.where(lane_row == 126, first, jnp.where(lane_row == 127, count, listed))
         for half in range(2):
             for part in range(3):
                 first = 24 * half + 8 * part
@@ -103,15 +132,18 @@
         out_ref[target, 48:56, :] = jnp.broadcast_to(listed, (8, 128))
 
 
-def facet_features(world_ref, out_ref, push_ref, terms_ref, terms_keep, push_keep, sem):
+def facet_features(*refs):
+    *world_refs, out_ref, push_ref, terms_ref, terms_keep, push_keep, sem = refs
+    across = lax.axis_index("wide") & 3
     terms_keep[...] = jnp.zeros(terms_keep.shape, F32)
     push_keep[...] = jnp.zeros(push_keep.shape, F32)
 
-    def owner(index, carry):
-        lever = [world_ref[index, part] for part in range(3)]
-        normal = [world_ref[index, 3 + part] for part in range(3)]
-        area = world_ref[index, 6]
-        last = world_ref[index, 7]
+    def owner(number, world_ref, step):
+        index = 4 * number + ((across - step) & 3)
+        lever = [world_ref[step, part] for part in range(3)]
+        normal = [world_ref[step, 3 + part] for part in range(3)]
+        area = world_ref[step, 6]
+        last = world_ref[step, 7]
         center = [lever[part] + last[:, part : part + 1] for part in range(3)]
         along = normal[0] * center[0] + normal[1] * center[1] + normal[2] * center[2]
         square = center[0] * center[0] + center[1] * center[1] + center[2] * center[2]
@@ -124,10 +156,10 @@
             order = (0, 1, 2, 0, 1, 0)
             for group, level in enumerate(order):
                 for part in range(3):
-                    terms_keep[side * TERMS + 3 * group + part] = split[part][level]
+                    put(terms_keep, side * TERMS + 3 * group + part, split[part][level])
             for level, value in enumerate(split3(constant)):
-                terms_keep[side * TERMS + 18 + level] = value
-                terms_keep[side * TERMS + 21 + level] = jnp.full((8, 128), tail, F32)
+                put(terms_keep, side * TERMS + 18 + level, value)
+                put(terms_keep, side * TERMS + 21 + level, jnp.full((8, 128), tail, F32))
         scaled = (PENALTY / SHARPNESS) * area
         push = [scaled * value for value in normal]
         push.append(lever[1] * push[2] - lever[2] * push[1])
@@ -135,42 +167,63 @@
         push.append(lever[0] * push[1] - lever[1] * push[0])
         for part in range(6):
             high = push[part].astype(BF16).astype(F32)
-            push_keep[part] = high
-            push_keep[8 + part] = push[part] - high
+            put(push_keep, part, high)
+            put(push_keep, 8 + part, push[part] - high)
         for block in range(BLOCKS):
-            both = terms_keep[:, block, :]
+            both = terms_keep[pl.ds(block, 2 * TERMS, stride=PITCH), :]
             terms_ref[index * BLOCKS + block, 0:128, :] = both[:TERMS].T.astype(BF16)
             terms_ref[index * BLOCKS + block, 128:256, :] = both[TERMS:].T.astype(BF16)
-            push_ref[index * BLOCKS + block] = push_keep[:, block, :].astype(BF16)
+            push_ref[index * BLOCKS + block] = push_keep[
+                pl.ds(block, 16, stride=PITCH), :
+            ].astype(BF16)
         part = pl.ds(index * BLOCKS, BLOCKS)
         pltpu.make_async_copy(terms_ref.at[part], out_ref.at[part], sem).start()
-        return carry
-
-    lax.fori_loop(0, PLANE, owner, 0)
-    push_ref[FACETS] = jnp.zeros((16, 128), BF16)
+
+    for number, world_ref in enumerate(world_refs):
+
+        def step(index, carry):
+            owner(number, world_ref, index)
+            return carry
+
+        lax.fori_loop(0, 4, step, 0)
     pltpu.make_async_copy(terms_ref, out_ref, sem).wait()
 
 
 def contact(
-    held_ref, push_ref, given_ref, force_ref, load_ref,
-    terms_ref, terms_sem, table, listed, point_keep, points, force_sum, load_sum,
+    near_terms, far_terms, near_push, far_push, given_ref, force_ref, load_ref,
+    terms_ref, push_ref, held_sem, table, listed, near_keep, far_keep, points, force_sum, load_sum,
     sem, *buffers,
 ):
     gaps = [buffers[0:GROUP], buffers[GROUP : 2 * GROUP]]
     weights = [buffers[2 * GROUP : 3 * GROUP], buffers[3 * GROUP : 4 * GROUP]]
     copy = pltpu.make_async_copy(given_ref.at[:, pl.ds(48, 8), :], table, sem)
     copy.start()
-    terms = pltpu.make_async_copy(held_ref, terms_ref.at[pl.ds(0, FACETS)], terms_sem)
-    terms.start()
+    down = lax.axis_index("wide") >> 2
+    held = []
+    for step in range(4):
+        target = pl.ds(ROW * ((down - step) & 3), ROW)
+        source_at = pl.ds(ROW * max(step - 1, 0), ROW)
+        pairs = ((near_terms, far_terms, terms_ref), (near_push, far_push, push_ref))
+        for kind, (near, far, whole) in enumerate(pairs):
+            origin = far if step else near
+            held.append(
+                pltpu.make_async_copy(
+                    origin.at[source_at], whole.at[target], held_sem.at[2 * step + kind]
+                )
+            )
+            held[-1].start()
     terms_ref[FACETS] = jnp.zeros((256, TERMS), BF16)
-    point_keep[...] = jnp.zeros(point_keep.shape, F32)
+    push_ref[FACETS] = jnp.zeros((16, 128), BF16)
+    point_keep = [near_keep, far_keep]
+    for keep in point_keep:
+        keep[...] = jnp.zeros(keep.shape, F32)
     force_sum[...] = jnp.zeros(force_sum.shape, F32)
     load_sum[...] = jnp.zeros(load_sum.shape, F32)
     points[PARTICLES] = jnp.zeros((TERMS, 256), BF16)
 
     def source(index, carry):
         for half in range(2):
-            lanes = slice(128 * half, 128 * half + 128)
+            keep = point_keep[half]
             place = [
                 given_ref[index, 24 * half + 8 * part : 24 * half + 8 * part + 8, :]
                 for part in range(3)
@@ -179,29 +232,38 @@
             split = [split3(value) for value in place]
             for group, level in enumerate((0, 0, 0, 1, 1, 2)):
                 for part in range(3):
-                    point_keep[3 * group + part, :, lanes] = split[part][level]
+                    put(keep, 3 * group + part, split[part][level])
             for level, value in enumerate(split3(-square)):
-                point_keep[18 + level, :, lanes] = jnp.full((8, 128), 1.0, F32)
-                point_keep[21 + level, :, lanes] = value
+                put(keep, 18 + level, jnp.full((8, 128), 1.0, F32))
+                put(keep, 21 + level, value)
         for block in range(BLOCKS):
-            points[index * BLOCKS + block] = point_keep[:, block, :].astype(BF16)
+            for half in range(2):
+                points[index * BLOCKS + block, :, 128 * half : 128 * half + 128] = point_keep[half][
+                    pl.ds(block, TERMS, stride=PITCH), :
+                ].astype(BF16)
         return carry
 
     lax.fori_loop(0, DEPTH, source, 0)
     copy.wait()
 
-    def gather(index, start):
-        count = table[index, 0, 127].astype(jnp.int32)
-        shift = index * (BLOCKS * 256)
-
-        def entry(place, carry):
-            listed[start + place] = table[index, 0, place].astype(jnp.int32) + shift
-            return carry
-
-        lax.fori_loop(0, count, entry, 0)
-        return start + count
-
-    total = lax.fori_loop(0, DEPTH, gather, 2 * GROUP)
+    def gather(late, start):
+        def one(index, start):
+            early = table[index, 0, 126].astype(jnp.int32)
+            first = jnp.where(late, early, 0)
+            count = jnp.where(late, table[index, 0, 127].astype(jnp.int32) - early, early)
+            shift = index * (BLOCKS * 256)
+
+            def entry(place, carry):
+                listed[start + place] = table[index, 0, first + place].astype(jnp.int32) + shift
+                return carry
+
+            lax.fori_loop(0, count, entry, 0)
+            return start + count
+
+        return lax.fori_loop(0, DEPTH, one, start)
+
+    early = gather(False, 2 * GROUP)
+    total = gather(True, early)
     for spare in range(2 * GROUP):
         listed[spare] = PARTICLES * 256 + FACETS
     for spare in range(4 * GROUP):
@@ -243,8 +305,13 @@
                 add(here + member, weights[half][member])
         return carry
 
-    terms.wait()
-    lax.fori_loop(0, (total + 2 * GROUP - 1) // (2 * GROUP), step, 0)
+    for one in held[:4]:
+        one.wait()
+    steps = (early - 2 * GROUP) // (2 * GROUP)
+    lax.fori_loop(0, steps, step, 0)
+    for one in held[4:]:
+        one.wait()
+    lax.fori_loop(steps, (total + 2 * GROUP - 1) // (2 * GROUP), step, 0)
     for index in range(DEPTH):
         for block in range(BLOCKS):
             for part in range(3):
@@ -254,20 +321,18 @@
     load_ref[...] = load_sum[0 : 2 * PLANE]
 
 
-def finish_particles(force_ref, velocity_ref, mass_ref, out_ref):
+def finish(
+    force_ref, velocity_ref, mass_ref, own_ref, other_ref, pose_at, motion_at, out_ref, motion_ref,
+    pose_ref, spin_ref, sems,
+):
+    fetch([(pose_at, pose_ref), (motion_at, spin_ref)], sems)
+    finish_boulders(own_ref, other_ref, pose_ref, spin_ref, motion_ref)
     total = force_ref[0]
     for index in range(1, DEPTH):
         total = total + force_ref[index]
     scaled = TIME_STEP * mass_ref[...]
     for part in range(3):
         out_ref[part] = velocity_ref[part] + scaled * total[8 * part : 8 * part + 8, :]
-
-
-def sum_loads(load_ref, out_ref):
-    total = load_ref[0]
-    for index in range(1, PLANE):
-        total = total + load_ref[index]
-    out_ref[...] = total
 
 
 def finish_boulders(own_ref, other_ref, pose_ref, velocity_ref, out_ref):
@@ -300,18 +365,17 @@
 
 
 VMEM = pl.BlockSpec(memory_space=pltpu.VMEM)
-SMEM = pl.BlockSpec(memory_space=pltpu.SMEM)
 ANY = pl.BlockSpec(memory_space=pl.ANY)
 
 
-def call(kernel, outs, in_specs, scratch=(), out_specs=VMEM):
+def call(kernel, outs, in_specs, scratch=(), out_specs=VMEM, limit=VMEM_LIMIT):
     return pl.pallas_call(
         kernel,
         out_shape=outs,
         in_specs=in_specs,
         out_specs=out_specs,
         scratch_shapes=list(scratch),
-        compiler_params=pltpu.CompilerParams(vmem_limit_bytes=VMEM_LIMIT),
+        compiler_params=pltpu.CompilerParams(vmem_limit_bytes=limit),
     )
 
 
@@ -329,7 +393,6 @@
     pair_active,
 ):
     owners = lax.axis_size("wide")
-    planes = [[PLANE * depth + spot for spot in range(PLANE)] for depth in range(owners // PLANE)]
     columns = [[PLANE * depth + spot for depth in range(DEPTH)] for spot in range(PLANE)]
     swap = functools.partial(
         lax.all_to_all, axis_name="wide", split_axis=0, concat_axis=0, tiled=True
@@ -337,41 +400,76 @@
     pairs = pair_facet.shape[0]
     shape = jax.ShapeDtypeStruct
 
-    facets = call(facet_message, shape((PLANE, 8, BLOCKS, 128), F32), [VMEM, SMEM])(
-        facet_geometry.transpose(0, 2, 1, 3), boulder_pose
-    )
-    facets = swap(facets, axis_index_groups=planes)
-    particles = call(pair_message, shape((DEPTH, 56, 128), F32), [VMEM] * 6)(
+    def shift(step, unit):
+        moves = []
+        for device in range(owners):
+            place = device // unit % 4
+            moves.append((device, device + ((place + step) % 4 - place) * unit))
+        return moves
+
+    geometry = facet_geometry.transpose(0, 2, 1, 3)
+    own = call(
+        facet_message,
+        shape((8, BLOCKS, 128), F32),
+        [ANY, ANY],
+        [
+            pltpu.VMEM(geometry.shape, F32),
+            pltpu.SMEM(boulder_pose.shape, F32),
+            pltpu.SemaphoreType.DMA((2,)),
+        ],
+        limit=WHOLE_VMEM,
+    )(geometry, boulder_pose)
+    line = [own] + [lax.ppermute(own, "wide", shift(step, 1)) for step in (1, 2, 3)]
+    line = jnp.stack(line)
+    lists = [
         particle_position.transpose(1, 0, 2),
-        boulder_slot.reshape(2, 128),
-        block_home.reshape(16, 128),
-        pair_facet.reshape(pairs, 1),
-        pair_block.reshape(pairs, 1),
-        pair_active.reshape(pairs, 1),
-    )
+        boulder_slot.reshape(-1, 128),
+        block_home.reshape(-1, 128),
+        pair_facet.reshape(1, pairs),
+        pair_block.reshape(1, pairs),
+        pair_active.reshape(1, pairs),
+    ]
+    particles = call(
+        pair_message,
+        shape((DEPTH, 56, 128), F32),
+        [ANY] * 7,
+        [pltpu.VMEM(value.shape, value.dtype) for value in lists]
+        + [pltpu.SemaphoreType.DMA((6,))],
+        limit=WHOLE_VMEM,
+    )(*lists, own)
+    lines = [lax.ppermute(line, "wide", shift(step, 4)) for step in (1, 2, 3)]
+
+    def features(parts):
+        blocks = ROW * len(parts)
+        return call(
+            facet_features,
+            [shape((blocks, 256, TERMS), BF16), shape((blocks, 16, 128), BF16)],
+            [VMEM] * len(parts),
+            [
+                pltpu.VMEM((blocks, 256, TERMS), BF16),
+                pltpu.VMEM((2 * TERMS * PITCH, 128), F32),
+                pltpu.VMEM((16 * PITCH, 128), F32),
+                pltpu.SemaphoreType.DMA,
+            ],
+            out_specs=[ANY, VMEM],
+        )(*parts)
+
+    near_terms, near_push = features([line])
+    particles, near_push = lax.optimization_barrier((particles, near_push))
     particles = swap(particles, axis_index_groups=columns)
-    terms, push = call(
-        facet_features,
-        [shape((FACETS, 256, TERMS), BF16), shape((FACETS + 1, 16, 128), BF16)],
-        [VMEM],
-        [
-            pltpu.VMEM((FACETS, 256, TERMS), BF16),
-            pltpu.VMEM((2 * TERMS, BLOCKS, 128), F32),
-            pltpu.VMEM((16, BLOCKS, 128), F32),
-            pltpu.SemaphoreType.DMA,
-        ],
-        out_specs=[ANY, VMEM],
-    )(facets)
+    far_terms, far_push = features(lines)
     force, load = call(
         contact,
         [shape((DEPTH, 24, 256), F32), shape((2 * PLANE, 8, 128), F32)],
-        [ANY, VMEM, VMEM],
+        [ANY] * 4 + [VMEM],
         [
             pltpu.VMEM((FACETS + 1, 256, TERMS), BF16),
-            pltpu.SemaphoreType.DMA,
+            pltpu.VMEM((FACETS + 1, 16, 128), BF16),
+            pltpu.SemaphoreType.DMA((8,)),
             pltpu.SMEM((DEPTH, 8, 128), F32),
             pltpu.SMEM((DEPTH * 48 + 6 * GROUP,), jnp.int32),
-            pltpu.VMEM((TERMS, BLOCKS, 256), F32),
+            pltpu.VMEM((TERMS * PITCH, 128), F32),
+            pltpu.VMEM((TERMS * PITCH, 128), F32),
             pltpu.VMEM((PARTICLES + 1, TERMS, 256), BF16),
             pltpu.VMEM((PARTICLES + 1, 8, 256), F32),
             pltpu.VMEM((2 * PLANE + 1, 8, 128), F32),
@@ -380,18 +478,10 @@
         + [pltpu.VMEM((256, 256), F32)] * (2 * GROUP)
         + [pltpu.VMEM((256, 256), BF16)] * (2 * GROUP),
         out_specs=[VMEM, VMEM],
-    )(terms, push, particles)
+    )(near_terms, far_terms, near_push, far_push, particles)
     grid = load.reshape(4, 4, 2, 8, 128)
     spot = lax.axis_index("wide") % PLANE
     down, across = spot // 4, spot % 4
-
-    def shift(step, unit):
-        moves = []
-        for device in range(owners):
-            place = device // unit % 4
-            moves.append((device, device + ((place + step) % 4 - place) * unit))
-        return moves
-
     def pick(array, axis, index):
         return lax.dynamic_index_in_dim(array, index % 4, axis, keepdims=False)
 
@@ -402,14 +492,19 @@
     for step in (1, 2, 3):
         load = load + lax.ppermute(pick(row, 0, down + step), "wide", shift(step, 4))
     other = lax.ppermute(load, "narrow", [(0, 1), (1, 0)])
-    boulder_motion = call(
-        finish_boulders, shape(boulder_velocity.shape, F32), [VMEM, VMEM, SMEM, VMEM]
-    )(load, other, boulder_pose, boulder_velocity)
     force = swap(force, axis_index_groups=columns)
     velocity = particle_velocity.transpose(1, 0, 2)
-    new_velocity = call(finish_particles, shape(velocity.shape, F32), [VMEM] * 3)(
-        force, velocity, inverse_mass
-    )
+    new_velocity, boulder_motion = call(
+        finish,
+        [shape(velocity.shape, F32), shape(boulder_velocity.shape, F32)],
+        [VMEM] * 5 + [ANY] * 2,
+        [
+            pltpu.SMEM(boulder_pose.shape, F32),
+            pltpu.VMEM(boulder_velocity.shape, F32),
+            pltpu.SemaphoreType.DMA((2,)),
+        ],
+        out_specs=[VMEM, VMEM],
+    )(force, velocity, inverse_mass, load, other, boulder_pose, boulder_velocity)
     return (new_velocity.transpose(1, 0, 2), boulder_motion)
 
 

time: 77.4 us -> 76.3 us (0.986)
  starting transfers between devices: 32.8 us -> 39.5 us
  local copies, waits for them, and re-layouts: 5.96 us -> 0.05 us
  waiting for transfers between devices: 11 us -> 8.84 us
    ppermute x0 -> x6, starting transfers between devices: none -> 9.5 us  [the longest x3 4.81 us: shards(): lines = [lax.ppermute(line, 'wide', shift(step, 4)) for step in (1, 2, 3)]]
    all_to_all x1 -> x0, starting transfers between devices: 7.58 us -> none  [shards(): facets = swap(facets, axis_index_groups=planes)]
    all_to_all x1 -> x0, waiting for transfers between devices: 4.3 us -> none  [shards(): facets = swap(facets, axis_index_groups=planes)]
    ppermute x0 -> x6, waiting for transfers between devices: none -> 4.29 us  [the longest x3 3.07 us: shards(): lines = [lax.ppermute(line, 'wide', shift(step, 4)) for step in (1, 2, 3)]]
    unnamed x18 -> x8, local copies, waits for them, and re-layouts: 3.55 us -> 0.02 us
    all_to_all x1, starting transfers between devices: 3.39 us -> 6.73 us  [shards(): force = swap(force, axis_index_groups=columns)]
    reshape x3 -> x0, local copies, waits for them, and re-layouts: 2.38 us -> none  [the longest x1 0.79 us: shards(): pair_block.reshape(pairs, 1)]
    all_to_all x1, waiting for transfers between devices: 2.37 us -> 0.01 us  [shards(): particles = swap(particles, axis_index_groups=columns)]
  transfers between devices with their start and end apart: 10 -> 15, of which waited for: 7 -> 8; matrix products, arithmetic and copies ran while one was open for 3% -> 0% of each run, Pallas kernels for 12% -> 10%
where the time goes in v4:
time: 76.3 us; the launch traced here: 75.8 us
  starting transfers between devices  39.5 us (52%)
  Pallas kernels  25.8 us (34%)
  waiting for transfers between devices  8.84 us (12%)
  other arithmetic  0.79 us (1%)
  between operations  0.79 us (1%)
    pallas_call x1, Pallas kernels, shards(): call(contact, [shape((DEPTH, 24, 256), F32), shape((2 * PLANE, 8, 128), F...  14.3 us
    all_to_all x1, starting transfers between devices, shards(): particles = swap(particles, axis_index_groups=columns)  8.2 us
    all_to_all x1, starting transfers between devices, shards(): force = swap(force, axis_index_groups=columns)  6.73 us
    ppermute x1, starting transfers between devices, shards(): other = lax.ppermute(load, 'narrow', [(0, 1), (1, 0)])  6.56 us
    pallas_call x2, Pallas kernels, features(): call(facet_features, [shape((blocks, 256, TERMS), BF16), shape((blocks, 1...  6.24 us
    ppermute x3, starting transfers between devices, shards(): lax.ppermute(pick(grid, 1, across + step), 'wide', shift(step, 1))  5.24 us
    ppermute x3, starting transfers between devices, shards(): lines = [lax.ppermute(line, 'wide', shift(step, 4)) for step in (1, 2, 3)]  4.81 us
    ppermute x3, starting transfers between devices, shards(): lax.ppermute(own, 'wide', shift(step, 1))  4.68 us
  transfers between devices with their start and end apart: 15, of which 8 were waited for; matrix products, arithmetic and copies ran while one was open for 0% of the time, Pallas kernels for 10%

profile of v4, /device:TPU:1, one launch (start us, length us, event | category | flops | bytes accessed | tf_op | source)
XLA Modules:
  0.0 75.8 jit_solution(15182777079323793335)
XLA Ops:
  0.7 1.5 %shard_map.122.refs_6_ = f32[8,8,128]{2,1,0:T(8,128)} custom-call(f32[2,7,4,128]{3,2,1,0:T(4,128)} %bitcast.45, f32[2,16]{1,0:T(2,128)} %pose_at.3), custom_call_target="tpu_custom_call" | custom-call | tf_op jit(solution)/shard_map/pallas_call | solution.py:411
  2.1 3.6 %collective-permute-start.2 = (f32[8,8,128]{2,1,0:T(8,128)}, f32[8,8,128]{2,1,0:T(8,128)S(1)}, u32[]{:S(2)}, u32[]{:S(2)}) collective-permute-start(f32[8,8,128]{2,1,0:T(8,128)} %shard_map.122.refs_6_), channel_id=1, source_target_pairs={{0,6},{2,0},{4,2},{6,4},{8,14},{10,8},{12,10},{14,12},{16,22},{18,... | collective-permute-start | bytes 98312 | tf_op jit(solution)/shard_map/ppermute | solution.py:422
  6.8 2.6 %shard_map.125 = f32[8,56,128]{2,1,0:T(8,128)} custom-call(f32[3,8,256]{2,1,0:T(8,128)} %bitcast.46, s32[2,128]{1,0:T(2,128)} %bitcast.48, s32[16,128]{1,0:T(8,128)} %bitcast.47, s32[1,192]{1,0:T(1,128)} %bitcast.49, s32[1,192]{1,0:T(1,128)} %bitcast.50, s32[1,192]{1,0:T(1,128)} %bitcast.51, f32[8,8,128]{2,1,0:T(8,128)} %shard_map.122.refs_6_), custom_call_target="tpu_custom_call" | custom-call | tf_op jit(solution)/shard_map/pallas_call | solution.py:432
  9.4 0.9 %collective-permute-done.1 = f32[8,8,128]{2,1,0:T(8,128)S(1)} collective-permute-done((f32[8,8,128]{2,1,0:T(8,128)}, f32[8,8,128]{2,1,0:T(8,128)S(1)}, u32[]{:S(2)}, u32[]{:S(2)}) %collective-permute-start.1) | collective-permute-done | bytes 32800 | tf_op jit(solution)/shard_map/ppermute | solution.py:422
  10.6 0.8 %pad_maximum_fusion.refs_0_ = f32[4,8,8,128]{3,2,1,0:T(8,128)S(1)} fusion(f32[1,8,8,128]{3,2,1,0:T(8,128)S(1)} %bitcast.42, f32[1,8,8,128]{3,2,1,0:T(8,128)S(1)} %bitcast.43, f32[1,8,8,128]{3,2,1,0:T(8,128)S(1)} %bitcast.44, f32[1,8,8,128]{3,2,1,0:T(8,128)} %bitcast.41), kind=kLoop, calls=%fused_computation | loop fusion | flops 98304 | bytes 262144 | tf_op jit(solution)/shard_map/stack | solution.py:423
  11.4 1.5 %shard_map.123 = (bf16[32,256,32]{2,1,0:T(8,128)(2,1)S(1)}, bf16[32,16,128]{2,1,0:T(8,128)(2,1)S(1)}) custom-call(f32[4,8,8,128]{3,2,1,0:T(8,128)S(1)} %pad_maximum_fusion.refs_0_), custom_call_target="tpu_custom_call" | custom-call | tf_op jit(solution)/shard_map/pallas_call | solution.py:444
  12.9 8.2 %all-to-all-start = ((f32[8,56,128]{2,1,0:T(8,128)}), f32[8,56,128]{2,1,0:T(8,128)S(1)}, u32[]{:S(2)}, u32[]{:S(2)}) async-start(f32[8,56,128]{2,1,0:T(8,128)} %shard_map.125), calls=%async_computation | async-start | bytes 458752 | tf_op jit(solution)/shard_map/all_to_all | solution.py:459
  21.1 1.2 %collective-permute-start.3 = (f32[4,8,8,128]{3,2,1,0:T(8,128)S(1)}, f32[4,8,8,128]{3,2,1,0:T(8,128)S(1)}, u32[]{:S(2)}, u32[]{:S(2)}) collective-permute-start(f32[4,8,8,128]{3,2,1,0:T(8,128)S(1)} %pad_maximum_fusion.refs_0_), channel_id=1, source_target_pairs={{0,8},{2,10},{4,12},{6,14},{8,16},{10,18},{12,20},{14,22},{16,24},... | collective-permute-start | bytes 393224 | tf_op jit(solution)/shard_map/ppermute | solution.py:440
  22.3 2.5 %collective-permute-start.4 = (f32[4,8,8,128]{3,2,1,0:T(8,128)S(1)}, f32[4,8,8,128]{3,2,1,0:T(8,128)S(1)}, u32[]{:S(2)}, u32[]{:S(2)}) collective-permute-start(f32[4,8,8,128]{3,2,1,0:T(8,128)S(1)} %pad_maximum_fusion.refs_0_), channel_id=1, source_target_pairs={{0,16},{2,18},{4,20},{6,22},{8,24},{10,26},{12,28},{14,30},{16,0},... | collective-permute-start | bytes 393224 | tf_op jit(solution)/shard_map/ppermute | solution.py:440
  24.8 1.2 %collective-permute-start.5 = (f32[4,8,8,128]{3,2,1,0:T(8,128)S(1)}, f32[4,8,8,128]{3,2,1,0:T(8,128)S(1)}, u32[]{:S(2)}, u32[]{:S(2)}) collective-permute-start(f32[4,8,8,128]{3,2,1,0:T(8,128)S(1)} %pad_maximum_fusion.refs_0_), channel_id=1, source_target_pairs={{0,24},{2,26},{4,28},{6,30},{8,0},{10,2},{12,4},{14,6},{16,8},{18,... | collective-permute-start | bytes 393224 | tf_op jit(solution)/shard_map/ppermute | solution.py:440
  26.1 2.5 %collective-permute-done.4.refs_1_ = f32[4,8,8,128]{3,2,1,0:T(8,128)S(1)} collective-permute-done((f32[4,8,8,128]{3,2,1,0:T(8,128)S(1)}, f32[4,8,8,128]{3,2,1,0:T(8,128)S(1)}, u32[]{:S(2)}, u32[]{:S(2)}) %collective-permute-start.4) | collective-permute-done | bytes 131104 | tf_op jit(solution)/shard_map/ppermute | solution.py:440
  29.0 4.7 %shard_map.124 = (bf16[96,256,32]{2,1,0:T(8,128)(2,1)}, bf16[96,16,128]{2,1,0:T(8,128)(2,1)S(1)}) custom-call(f32[4,8,8,128]{3,2,1,0:T(8,128)S(1)} %collective-permute-done.3.refs_0_, f32[4,8,8,128]{3,2,1,0:T(8,128)S(1)} %collective-permute-done.4.refs_1_, f32[4,8,8,128]{3,2,1,0:T(8,128)S(1)} %collective-permute-done.5.refs_2_), custom_call_target="tpu_custom_call" | custom-call | tf_op jit(solution)/shard_map/pallas_call | solution.py:444
  33.7 14.3 %shard_map.126 = (f32[8,24,256]{2,1,0:T(8,128)}, f32[32,8,128]{2,1,0:T(8,128)S(1)}) custom-call(bf16[32,256,32]{2,1,0:T(8,128)(2,1)S(1)} %get-tuple-element.12.near_terms, bf16[96,256,32]{2,1,0:T(8,128)(2,1)} %get-tuple-element.13.far_terms, bf16[32,16,128]{2,1,0:T(8,128)(2,1)S(1)} %get-tuple-element.15.near_push, ...), custom_call_target="tpu_custom_call" | custom-call | tf_op jit(solution)/shard_map/pallas_call | solution.py:461
  48.1 3.2 %collective-permute-start.8 = (f32[4,2,8,128]{3,2,1,0:T(8,128)S(1)}, f32[4,2,8,128]{3,2,1,0:T(8,128)S(1)}, u32[]{:S(2)}, u32[]{:S(2)}) collective-permute-start(f32[4,2,8,128]{3,2,1,0:T(8,128)S(1)} %get-tuple-element.23), channel_id=1, source_target_pairs={{0,6},{2,0},{4,2},{6,4},{8,14},{10,8},{12,10},{14,12},{16,22},{18,... | collective-permute-start | bytes 98312 | tf_op jit(solution)/shard_map/ppermute | solution.py:490
  51.3 1.3 %collective-permute-start.7 = (f32[4,2,8,128]{3,2,1,0:T(8,128)S(1)}, f32[4,2,8,128]{3,2,1,0:T(8,128)S(1)}, u32[]{:S(2)}, u32[]{:S(2)}) collective-permute-start(f32[4,2,8,128]{3,2,1,0:T(8,128)S(1)} %get-tuple-element.24), channel_id=1, source_target_pairs={{0,4},{2,6},{4,0},{6,2},{8,12},{10,14},{12,8},{14,10},{16,20},{18,... | collective-permute-start | bytes 98312 | tf_op jit(solution)/shard_map/ppermute | solution.py:490
  52.5 0.8 %collective-permute-start.6 = (f32[4,2,8,128]{3,2,1,0:T(8,128)S(1)}, f32[4,2,8,128]{3,2,1,0:T(8,128)S(1)}, u32[]{:S(2)}, u32[]{:S(2)}) collective-permute-start(f32[4,2,8,128]{3,2,1,0:T(8,128)S(1)} %get-tuple-element.22), channel_id=1, source_target_pairs={{0,2},{2,4},{4,6},{6,0},{8,10},{10,12},{12,14},{14,8},{16,18},{18,... | collective-permute-start | bytes 98312 | tf_op jit(solution)/shard_map/ppermute | solution.py:490
  53.3 6.7 %all-to-all-start.1 = ((f32[8,24,256]{2,1,0:T(8,128)}), f32[8,24,256]{2,1,0:T(8,128)S(1)}, u32[]{:S(2)}, u32[]{:S(2)}) async-start(f32[8,24,256]{2,1,0:T(8,128)} %get-tuple-element.18), calls=%async_computation.1 | async-start | bytes 393216 | tf_op jit(solution)/shard_map/all_to_all | solution.py:495
  60.1 1.1 %collective-permute-start.11 = (f32[2,8,128]{2,1,0:T(8,128)S(1)}, f32[2,8,128]{2,1,0:T(8,128)S(1)}, u32[]{:S(2)}, u32[]{:S(2)}) collective-permute-start(f32[2,8,128]{2,1,0:T(8,128)S(1)} %get-tuple-element.26), channel_id=1, source_target_pairs={{0,24},{2,26},{4,28},{6,30},{8,0},{10,2},{12,4},{14,6},{16,8},{18,... | collective-permute-start | bytes 24584 | tf_op jit(solution)/shard_map/ppermute | solution.py:493
  61.2 2.2 %collective-permute-start.10 = (f32[2,8,128]{2,1,0:T(8,128)S(1)}, f32[2,8,128]{2,1,0:T(8,128)S(1)}, u32[]{:S(2)}, u32[]{:S(2)}) collective-permute-start(f32[2,8,128]{2,1,0:T(8,128)S(1)} %get-tuple-element.27), channel_id=1, source_target_pairs={{0,16},{2,18},{4,20},{6,22},{8,24},{10,26},{12,28},{14,30},{16,0},... | collective-permute-start | bytes 24584 | tf_op jit(solution)/shard_map/ppermute | solution.py:493
  63.4 1.8 %collective-permute-done.10 = f32[2,8,128]{2,1,0:T(8,128)S(1)} collective-permute-done((f32[2,8,128]{2,1,0:T(8,128)S(1)}, f32[2,8,128]{2,1,0:T(8,128)S(1)}, u32[]{:S(2)}, u32[]{:S(2)}) %collective-permute-start.10) | collective-permute-done | bytes 8224 | tf_op jit(solution)/shard_map/ppermute | solution.py:493
  65.2 1.9 %collective-permute-done.9 = f32[2,8,128]{2,1,0:T(8,128)S(1)} collective-permute-done((f32[2,8,128]{2,1,0:T(8,128)S(1)}, f32[2,8,128]{2,1,0:T(8,128)S(1)}, u32[]{:S(2)}, u32[]{:S(2)}) %collective-permute-start.9) | collective-permute-done | bytes 8224 | tf_op jit(solution)/shard_map/ppermute | solution.py:493
  67.1 6.6 %collective-permute-start.12 = (f32[2,8,128]{2,1,0:T(8,128)S(1)}, f32[2,8,128]{2,1,0:T(8,128)S(1)}, u32[]{:S(2)}, u32[]{:S(2)}) collective-permute-start(f32[2,8,128]{2,1,0:T(8,128)S(1)} %fusion.3.own_ref), channel_id=1, source_target_pairs={{0,1},{1,0},{2,3},{3,2},{4,5},{5,4},{6,7},{7,6},{8,9},{9,8},{10,11... | collective-permute-start | bytes 24584 | tf_op jit(solution)/shard_map/ppermute | solution.py:494
  73.7 0.8 %collective-permute-done.12.other_ref = f32[2,8,128]{2,1,0:T(8,128)S(1)} collective-permute-done((f32[2,8,128]{2,1,0:T(8,128)S(1)}, f32[2,8,128]{2,1,0:T(8,128)S(1)}, u32[]{:S(2)}, u32[]{:S(2)}) %collective-permute-start.12) | collective-permute-done | bytes 8224 | tf_op jit(solution)/shard_map/ppermute | solution.py:494
  74.5 1.3 %shard_map.127 = (f32[3,8,256]{2,1,0:T(8,128)}, f32[2,6]{1,0:T(2,128)}) custom-call(f32[8,24,256]{2,1,0:T(8,128)S(1)} %all-to-all-done.1.force_ref, f32[3,8,256]{2,1,0:T(8,128)S(1)} %bitcast.40, f32[8,256]{1,0:T(8,128)S(1)} %copy-done.1, f32[2,8,128]{2,1,0:T(8,128)S(1)} %fusion.3.own_ref, f32[2,8,128]{2,1,0:T(8,128)S(1)} %collective-permute-done.12.other_ref, ...), custom_call_target="tpu_custom_call" | custom-call | tf_op jit(solution)/shard_map/pallas_call | solution.py:497
  (25 shorter events, 2.0 us)
Async XLA Ops:
  0.6 73.9 %copy-start.2 = (f32[2,16]{1,0:T(2,128)S(1)}, f32[2,16]{1,0:T(2,128)}, u32[]{:S(2)}) copy-start(f32[2,16]{1,0:T(2,128)} %pose_at.3) | copy-start | bytes 388
  0.6 73.9 %copy-start = (f32[8,3,256]{2,0,1:T(8,128)S(1)}, f32[8,3,256]{2,0,1:T(8,128)}, u32[]{:S(2)}) copy-start(f32[8,3,256]{2,0,1:T(8,128)} %param.12) | copy-start | bytes 73732
  0.7 73.9 %copy-start.1 = (f32[8,256]{1,0:T(8,128)S(1)}, f32[8,256]{1,0:T(8,128)}, u32[]{:S(2)}) copy-start(f32[8,256]{1,0:T(8,128)} %mass_ref.1) | copy-start | bytes 24580
  0.7 73.9 %copy-start.3 = (f32[2,6]{1,0:T(2,128)S(1)}, f32[2,6]{1,0:T(2,128)}, u32[]{:S(2)}) copy-start(f32[2,6]{1,0:T(2,128)} %motion_at.1) | copy-start | bytes 148
  2.1 7.2 %collective-permute-start.2 = (f32[8,8,128]{2,1,0:T(8,128)}, f32[8,8,128]{2,1,0:T(8,128)S(1)}, u32[]{:S(2)}, u32[]{:S(2)}) collective-permute-start(f32[8,8,128]{2,1,0:T(8,128)} %shard_map.122.refs_6_), channel_id=1, source_target_pairs={{0,6},{2,0},{4,2},{6,4},{8,14},{10,8},{12,10},{14,12},{16,22},{18,... | collective-permute-start | bytes 98312 | tf_op jit(solution)/shard_map/ppermute | solution.py:422
  5.8 4.5 %collective-permute-start.1 = (f32[8,8,128]{2,1,0:T(8,128)}, f32[8,8,128]{2,1,0:T(8,128)S(1)}, u32[]{:S(2)}, u32[]{:S(2)}) collective-permute-start(f32[8,8,128]{2,1,0:T(8,128)} %shard_map.122.refs_6_), channel_id=1, source_target_pairs={{0,4},{2,6},{4,0},{6,2},{8,12},{10,14},{12,8},{14,10},{16,20},{18,... | collective-permute-start | bytes 98312 | tf_op jit(solution)/shard_map/ppermute | solution.py:422
  6.1 4.5 %collective-permute-start = (f32[8,8,128]{2,1,0:T(8,128)}, f32[8,8,128]{2,1,0:T(8,128)S(1)}, u32[]{:S(2)}, u32[]{:S(2)}) collective-permute-start(f32[8,8,128]{2,1,0:T(8,128)} %shard_map.122.refs_6_), channel_id=1, source_target_pairs={{0,2},{2,4},{4,6},{6,0},{8,10},{10,12},{12,14},{14,8},{16,18},{18,... | collective-permute-start | bytes 98312 | tf_op jit(solution)/shard_map/ppermute | solution.py:422
  12.9 20.8 %all-to-all-start = ((f32[8,56,128]{2,1,0:T(8,128)}), f32[8,56,128]{2,1,0:T(8,128)S(1)}, u32[]{:S(2)}, u32[]{:S(2)}) async-start(f32[8,56,128]{2,1,0:T(8,128)} %shard_map.125), calls=%async_computation | async-start | bytes 458752 | tf_op jit(solution)/shard_map/all_to_all | solution.py:459
  21.1 5.0 %collective-permute-start.3 = (f32[4,8,8,128]{3,2,1,0:T(8,128)S(1)}, f32[4,8,8,128]{3,2,1,0:T(8,128)S(1)}, u32[]{:S(2)}, u32[]{:S(2)}) collective-permute-start(f32[4,8,8,128]{3,2,1,0:T(8,128)S(1)} %pad_maximum_fusion.refs_0_), channel_id=1, source_target_pairs={{0,8},{2,10},{4,12},{6,14},{8,16},{10,18},{12,20},{14,22},{16,24},... | collective-permute-start | bytes 393224 | tf_op jit(solution)/shard_map/ppermute | solution.py:440
  22.3 6.3 %collective-permute-start.4 = (f32[4,8,8,128]{3,2,1,0:T(8,128)S(1)}, f32[4,8,8,128]{3,2,1,0:T(8,128)S(1)}, u32[]{:S(2)}, u32[]{:S(2)}) collective-permute-start(f32[4,8,8,128]{3,2,1,0:T(8,128)S(1)} %pad_maximum_fusion.refs_0_), channel_id=1, source_target_pairs={{0,16},{2,18},{4,20},{6,22},{8,24},{10,26},{12,28},{14,30},{16,0},... | collective-permute-start | bytes 393224 | tf_op jit(solution)/shard_map/ppermute | solution.py:440
  24.8 4.2 %collective-permute-start.5 = (f32[4,8,8,128]{3,2,1,0:T(8,128)S(1)}, f32[4,8,8,128]{3,2,1,0:T(8,128)S(1)}, u32[]{:S(2)}, u32[]{:S(2)}) collective-permute-start(f32[4,8,8,128]{3,2,1,0:T(8,128)S(1)} %pad_maximum_fusion.refs_0_), channel_id=1, source_target_pairs={{0,24},{2,26},{4,28},{6,30},{8,0},{10,2},{12,4},{14,6},{16,8},{18,... | collective-permute-start | bytes 393224 | tf_op jit(solution)/shard_map/ppermute | solution.py:440
  48.1 12.0 %collective-permute-start.8 = (f32[4,2,8,128]{3,2,1,0:T(8,128)S(1)}, f32[4,2,8,128]{3,2,1,0:T(8,128)S(1)}, u32[]{:S(2)}, u32[]{:S(2)}) collective-permute-start(f32[4,2,8,128]{3,2,1,0:T(8,128)S(1)} %get-tuple-element.23), channel_id=1, source_target_pairs={{0,6},{2,0},{4,2},{6,4},{8,14},{10,8},{12,10},{14,12},{16,22},{18,... | collective-permute-start | bytes 98312 | tf_op jit(solution)/shard_map/ppermute | solution.py:490
  51.3 8.8 %collective-permute-start.7 = (f32[4,2,8,128]{3,2,1,0:T(8,128)S(1)}, f32[4,2,8,128]{3,2,1,0:T(8,128)S(1)}, u32[]{:S(2)}, u32[]{:S(2)}) collective-permute-start(f32[4,2,8,128]{3,2,1,0:T(8,128)S(1)} %get-tuple-element.24), channel_id=1, source_target_pairs={{0,4},{2,6},{4,0},{6,2},{8,12},{10,14},{12,8},{14,10},{16,20},{18,... | collective-permute-start | bytes 98312 | tf_op jit(solution)/shard_map/ppermute | solution.py:490
  52.5 7.5 %collective-permute-start.6 = (f32[4,2,8,128]{3,2,1,0:T(8,128)S(1)}, f32[4,2,8,128]{3,2,1,0:T(8,128)S(1)}, u32[]{:S(2)}, u32[]{:S(2)}) collective-permute-start(f32[4,2,8,128]{3,2,1,0:T(8,128)S(1)} %get-tuple-element.22), channel_id=1, source_target_pairs={{0,2},{2,4},{4,6},{6,0},{8,10},{10,12},{12,14},{14,8},{16,18},{18,... | collective-permute-start | bytes 98312 | tf_op jit(solution)/shard_map/ppermute | solution.py:490
  53.3 21.2 %all-to-all-start.1 = ((f32[8,24,256]{2,1,0:T(8,128)}), f32[8,24,256]{2,1,0:T(8,128)S(1)}, u32[]{:S(2)}, u32[]{:S(2)}) async-start(f32[8,24,256]{2,1,0:T(8,128)} %get-tuple-element.18), calls=%async_computation.1 | async-start | bytes 393216 | tf_op jit(solution)/shard_map/all_to_all | solution.py:495
  60.1 3.3 %collective-permute-start.11 = (f32[2,8,128]{2,1,0:T(8,128)S(1)}, f32[2,8,128]{2,1,0:T(8,128)S(1)}, u32[]{:S(2)}, u32[]{:S(2)}) collective-permute-start(f32[2,8,128]{2,1,0:T(8,128)S(1)} %get-tuple-element.26), channel_id=1, source_target_pairs={{0,24},{2,26},{4,28},{6,30},{8,0},{10,2},{12,4},{14,6},{16,8},{18,... | collective-permute-start | bytes 24584 | tf_op jit(solution)/shard_map/ppermute | solution.py:493
  61.2 4.0 %collective-permute-start.10 = (f32[2,8,128]{2,1,0:T(8,128)S(1)}, f32[2,8,128]{2,1,0:T(8,128)S(1)}, u32[]{:S(2)}, u32[]{:S(2)}) collective-permute-start(f32[2,8,128]{2,1,0:T(8,128)S(1)} %get-tuple-element.27), channel_id=1, source_target_pairs={{0,16},{2,18},{4,20},{6,22},{8,24},{10,26},{12,28},{14,30},{16,0},... | collective-permute-start | bytes 24584 | tf_op jit(solution)/shard_map/ppermute | solution.py:493
  63.4 3.7 %collective-permute-start.9 = (f32[2,8,128]{2,1,0:T(8,128)S(1)}, f32[2,8,128]{2,1,0:T(8,128)S(1)}, u32[]{:S(2)}, u32[]{:S(2)}) collective-permute-start(f32[2,8,128]{2,1,0:T(8,128)S(1)} %get-tuple-element.25), channel_id=1, source_target_pairs={{0,8},{2,10},{4,12},{6,14},{8,16},{10,18},{12,20},{14,22},{16,24},... | collective-permute-start | bytes 24584 | tf_op jit(solution)/shard_map/ppermute | solution.py:493
  67.1 7.4 %collective-permute-start.12 = (f32[2,8,128]{2,1,0:T(8,128)S(1)}, f32[2,8,128]{2,1,0:T(8,128)S(1)}, u32[]{:S(2)}, u32[]{:S(2)}) collective-permute-start(f32[2,8,128]{2,1,0:T(8,128)S(1)} %fusion.3.own_ref), channel_id=1, source_target_pairs={{0,1},{1,0},{2,3},{3,2},{4,5},{5,4},{6,7},{7,6},{8,9},{9,8},{10,11... | collective-permute-start | bytes 24584 | tf_op jit(solution)/shard_map/ppermute | solution.py:494

commit v5 on v4

--- a/solution.py
+++ b/solution.py
@@ -21,6 +21,7 @@
 ROW = 4 * BLOCKS
 PARTICLES = DEPTH * BLOCKS
 GROUP = 2
+SIDE = 4
 VMEM_LIMIT = 48 * 1024 * 1024
 WHOLE_VMEM = 63 * 1024 * 1024
 
@@ -73,13 +74,14 @@
                 jnp.where(lane == 1, center[1], jnp.where(lane == 2, center[2], 0.0)),
             )
         )
-        for row in range(8):
-            out_ref[row, 4 * boulder : 4 * boulder + 4, :] = rows[row]
+        for target in range(PLANE):
+            for row in range(8):
+                out_ref[target, row, 4 * boulder : 4 * boulder + 4, :] = rows[row]
 
 
 def pair_message(*refs):
-    held, out_ref, (position_ref, slot_ref, home_ref), rows, sems = (
-        refs[:6], refs[7], refs[8:11], refs[11:14], refs[14],
+    held, (out_ref, own_ref), (position_ref, slot_ref, home_ref), rows, sems = (
+        refs[:6], refs[6:8], refs[8:11], refs[11:14], refs[14],
     )
     fetch(list(zip(held, (position_ref, slot_ref, home_ref, *rows))), sems)
     facet, block, active = [row[...] for row in rows]
@@ -104,7 +106,7 @@
     plane = slot >> 5
     code = local_block * 256 + ((slot & 31) * 4 + (facet & 3))
     code = code.astype(F32)
-    late = ((lax.axis_index("wide") >> 2) - (slot >> 3)) & 2
+    late = (slot >> 3) & 2
     member = jnp.logical_and(lane == plane + DEPTH * (late >> 1), active).astype(F32)
     row = lax.broadcasted_iota(jnp.int32, (pairs, pairs), 0)
     column = lax.broadcasted_iota(jnp.int32, (pairs, pairs), 1)
@@ -130,20 +132,89 @@
                     part, :, 128 * half : 128 * half + 128
                 ]
         out_ref[target, 48:56, :] = jnp.broadcast_to(listed, (8, 128))
-
-
-def facet_features(*refs):
-    *world_refs, out_ref, push_ref, terms_ref, terms_keep, push_keep, sem = refs
-    across = lax.axis_index("wide") & 3
-    terms_keep[...] = jnp.zeros(terms_keep.shape, F32)
-    push_keep[...] = jnp.zeros(push_keep.shape, F32)
-
-    def owner(number, world_ref, step):
-        index = 4 * number + ((across - step) & 3)
-        lever = [world_ref[step, part] for part in range(3)]
-        normal = [world_ref[step, 3 + part] for part in range(3)]
-        area = world_ref[step, 6]
-        last = world_ref[step, 7]
+    own_ref[...] = out_ref[lax.axis_index("wide") // PLANE]
+
+
+def particle_terms(place_ref, points, first, point_keep):
+    for half in range(2):
+        keep = point_keep[half]
+        place = [
+            place_ref[24 * half + 8 * part : 24 * half + 8 * part + 8, :]
+            for part in range(3)
+        ]
+        square = place[0] * place[0] + place[1] * place[1] + place[2] * place[2]
+        split = [split3(value) for value in place]
+        for group, level in enumerate((0, 0, 0, 1, 1, 2)):
+            for part in range(3):
+                put(keep, 3 * group + part, split[part][level])
+        for level, value in enumerate(split3(-square)):
+            put(keep, 18 + level, jnp.full((8, 128), 1.0, F32))
+            put(keep, 21 + level, value)
+    for block in range(BLOCKS):
+        for half in range(2):
+            points[first + block, :, 128 * half : 128 * half + 128] = point_keep[half][
+                pl.ds(block, TERMS, stride=PITCH), :
+            ].astype(BF16)
+
+
+def pipeline(terms_ref, push_ref, points, listed, force_sum, load_sum, buffers):
+    gaps = [buffers[0:GROUP], buffers[GROUP : 2 * GROUP]]
+    weights = [buffers[2 * GROUP : 3 * GROUP], buffers[3 * GROUP : 4 * GROUP]]
+
+    def exponents(place, buffer):
+        code = listed[place]
+        buffer[...] = jnp.dot(
+            terms_ref[code & 255], points[code >> 8], preferred_element_type=F32
+        )
+
+    def weigh(buffer, weight_ref):
+        for first in range(0, 128, 16):
+            gap = buffer[first : first + 16, :]
+            soft = jnp.where(gap > 80.0, gap, jnp.log(1.0 + jnp.exp(gap)))
+            weight = jnp.exp(buffer[128 + first : 144 + first, :]) * soft
+            high = weight.astype(BF16)
+            weight_ref[first : first + 16, :] = high
+            weight_ref[128 + first : 144 + first, :] = (weight - high.astype(F32)).astype(BF16)
+
+    def add(place, weight_ref):
+        code = listed[place]
+        facet = code & 255
+        push = push_ref[facet]
+        result = jnp.dot(
+            jnp.concatenate([push, push], axis=1), weight_ref[...], preferred_element_type=F32
+        )
+        result = result[0:8] + result[8:16]
+        force_sum[code >> 8] += result
+        load_sum[facet >> 2] += result[:, :128] + result[:, 128:]
+
+    def step(index, carry):
+        place = 2 * GROUP * index
+        for half in range(2):
+            here = place + half * GROUP
+            for member in range(GROUP):
+                exponents(here + 2 * GROUP + member, gaps[half][member])
+                weigh(gaps[1 - half][member], weights[1 - half][member])
+                add(here + member, weights[half][member])
+        return carry
+
+    return step
+
+
+def facet_features(
+    world_ref, own_ref, out_ref, push_ref, own_force, own_load,
+    terms_ref, sem, table, listed, points, force_sum, load_sum, own_sem, *buffers,
+):
+    keeps = buffers[4 * GROUP + 2 :]
+    copy = pltpu.make_async_copy(own_ref.at[pl.ds(48, 8), :], table, own_sem)
+    copy.start()
+    for keep in keeps:
+        keep[...] = jnp.zeros(keep.shape, F32)
+
+    def owner(index, terms_keep, push_keep):
+        lever = [world_ref[index, part] for part in range(3)]
+        normal = [world_ref[index, 3 + part] for part in range(3)]
+        area = world_ref[index, 6]
+        last = world_ref[index, 7]
         center = [lever[part] + last[:, part : part + 1] for part in range(3)]
         along = normal[0] * center[0] + normal[1] * center[1] + normal[2] * center[2]
         square = center[0] * center[0] + center[1] * center[1] + center[2] * center[2]
@@ -176,74 +247,80 @@
             push_ref[index * BLOCKS + block] = push_keep[
                 pl.ds(block, 16, stride=PITCH), :
             ].astype(BF16)
-        part = pl.ds(index * BLOCKS, BLOCKS)
+
+    def owners(index, carry):
+        for spare in range(SIDE):
+            owner(SIDE * index + spare, *keeps[2 * spare : 2 * spare + 2])
+        part = pl.ds(index * SIDE * BLOCKS, SIDE * BLOCKS)
         pltpu.make_async_copy(terms_ref.at[part], out_ref.at[part], sem).start()
-
-    for number, world_ref in enumerate(world_refs):
-
-        def step(index, carry):
-            owner(number, world_ref, index)
-            return carry
-
-        lax.fori_loop(0, 4, step, 0)
-    pltpu.make_async_copy(terms_ref, out_ref, sem).wait()
+        return carry
+
+    lax.fori_loop(0, PLANE // SIDE, owners, 0)
+    push_ref[FACETS] = jnp.zeros((16, 128), BF16)
+    terms_ref[FACETS] = jnp.zeros((256, TERMS), BF16)
+    points[BLOCKS] = jnp.zeros((TERMS, 256), BF16)
+    force_sum[...] = jnp.zeros(force_sum.shape, F32)
+    load_sum[...] = jnp.zeros(load_sum.shape, F32)
+    copy.wait()
+    particle_keep = buffers[4 * GROUP : 4 * GROUP + 2]
+    for keep in particle_keep:
+        keep[...] = jnp.zeros(keep.shape, F32)
+    particle_terms(own_ref, points, 0, particle_keep)
+    total = table[0, 127].astype(jnp.int32)
+
+    def entry(place, carry):
+        listed[2 * GROUP + place] = table[0, place].astype(jnp.int32)
+        return carry
+
+    lax.fori_loop(0, total, entry, 0)
+    for spare in range(2 * GROUP):
+        listed[spare] = BLOCKS * 256 + FACETS
+    for spare in range(4 * GROUP):
+        listed[2 * GROUP + total + spare] = BLOCKS * 256 + FACETS
+    step = pipeline(terms_ref, push_ref, points, listed, force_sum, load_sum, buffers)
+    lax.fori_loop(0, (total + 4 * GROUP - 1) // (2 * GROUP), step, 0)
+    for block in range(BLOCKS):
+        for part in range(3):
+            own_force[8 * part + block : 8 * part + block + 1, :] = force_sum[
+                block, part : part + 1, :
+            ]
+    own_load[...] = load_sum[0 : 2 * PLANE]
+    done = pltpu.make_async_copy(terms_ref.at[pl.ds(0, FACETS)], out_ref, sem)
+    done.wait()
 
 
 def contact(
-    near_terms, far_terms, near_push, far_push, given_ref, force_ref, load_ref,
-    terms_ref, push_ref, held_sem, table, listed, near_keep, far_keep, points, force_sum, load_sum,
+    held_ref, push_ref, given_ref, own_force, own_load, force_ref, load_ref,
+    terms_ref, held_sem, table, listed, points, force_sum, load_sum,
     sem, *buffers,
 ):
-    gaps = [buffers[0:GROUP], buffers[GROUP : 2 * GROUP]]
-    weights = [buffers[2 * GROUP : 3 * GROUP], buffers[3 * GROUP : 4 * GROUP]]
     copy = pltpu.make_async_copy(given_ref.at[:, pl.ds(48, 8), :], table, sem)
     copy.start()
-    down = lax.axis_index("wide") >> 2
     held = []
-    for step in range(4):
-        target = pl.ds(ROW * ((down - step) & 3), ROW)
-        source_at = pl.ds(ROW * max(step - 1, 0), ROW)
-        pairs = ((near_terms, far_terms, terms_ref), (near_push, far_push, push_ref))
-        for kind, (near, far, whole) in enumerate(pairs):
-            origin = far if step else near
-            held.append(
-                pltpu.make_async_copy(
-                    origin.at[source_at], whole.at[target], held_sem.at[2 * step + kind]
-                )
-            )
-            held[-1].start()
+    for part in range(4):
+        place = pl.ds(ROW * part, ROW)
+        held.append(
+            pltpu.make_async_copy(held_ref.at[place], terms_ref.at[place], held_sem.at[part])
+        )
+        held[-1].start()
     terms_ref[FACETS] = jnp.zeros((256, TERMS), BF16)
-    push_ref[FACETS] = jnp.zeros((16, 128), BF16)
-    point_keep = [near_keep, far_keep]
-    for keep in point_keep:
+    point_keeps = buffers[4 * GROUP :]
+    for keep in point_keeps:
         keep[...] = jnp.zeros(keep.shape, F32)
     force_sum[...] = jnp.zeros(force_sum.shape, F32)
-    load_sum[...] = jnp.zeros(load_sum.shape, F32)
+    load_sum[0 : 2 * PLANE] = own_load[...]
+    load_sum[2 * PLANE] = jnp.zeros((8, 128), F32)
+    plane = lax.axis_index("wide") // PLANE
     points[PARTICLES] = jnp.zeros((TERMS, 256), BF16)
 
-    def source(index, carry):
-        for half in range(2):
-            keep = point_keep[half]
-            place = [
-                given_ref[index, 24 * half + 8 * part : 24 * half + 8 * part + 8, :]
-                for part in range(3)
-            ]
-            square = place[0] * place[0] + place[1] * place[1] + place[2] * place[2]
-            split = [split3(value) for value in place]
-            for group, level in enumerate((0, 0, 0, 1, 1, 2)):
-                for part in range(3):
-                    put(keep, 3 * group + part, split[part][level])
-            for level, value in enumerate(split3(-square)):
-                put(keep, 18 + level, jnp.full((8, 128), 1.0, F32))
-                put(keep, 21 + level, value)
-        for block in range(BLOCKS):
-            for half in range(2):
-                points[index * BLOCKS + block, :, 128 * half : 128 * half + 128] = point_keep[half][
-                    pl.ds(block, TERMS, stride=PITCH), :
-                ].astype(BF16)
+    def sources(index, carry):
+        for spare in range(SIDE):
+            one = SIDE * index + spare
+            keeps = point_keeps[2 * spare : 2 * spare + 2]
+            particle_terms(given_ref.at[one], points, one * BLOCKS, keeps)
         return carry
 
-    lax.fori_loop(0, DEPTH, source, 0)
+    lax.fori_loop(0, DEPTH // SIDE, sources, 0)
     copy.wait()
 
     def gather(late, start):
@@ -251,6 +328,7 @@
             early = table[index, 0, 126].astype(jnp.int32)
             first = jnp.where(late, early, 0)
             count = jnp.where(late, table[index, 0, 127].astype(jnp.int32) - early, early)
+            count = jnp.where(index == plane, 0, count)
             shift = index * (BLOCKS * 256)
 
             def entry(place, carry):
@@ -269,47 +347,12 @@
     for spare in range(4 * GROUP):
         listed[total + spare] = PARTICLES * 256 + FACETS
 
-    def exponents(place, buffer):
-        code = listed[place]
-        buffer[...] = jnp.dot(
-            terms_ref[code & 255], points[code >> 8], preferred_element_type=F32
-        )
-
-    def weigh(buffer, weight_ref):
-        for first in range(0, 128, 16):
-            gap = buffer[first : first + 16, :]
-            soft = jnp.where(gap > 80.0, gap, jnp.log(1.0 + jnp.exp(gap)))
-            weight = jnp.exp(buffer[128 + first : 144 + first, :]) * soft
-            high = weight.astype(BF16)
-            weight_ref[first : first + 16, :] = high
-            weight_ref[128 + first : 144 + first, :] = (weight - high.astype(F32)).astype(BF16)
-
-    def add(place, weight_ref):
-        code = listed[place]
-        facet = code & 255
-        push = push_ref[facet]
-        result = jnp.dot(
-            jnp.concatenate([push, push], axis=1), weight_ref[...], preferred_element_type=F32
-        )
-        result = result[0:8] + result[8:16]
-        force_sum[code >> 8] += result
-        load_sum[facet >> 2] += result[:, :128] + result[:, 128:]
-
-    def step(index, carry):
-        place = 2 * GROUP * index
-        for half in range(2):
-            here = place + half * GROUP
-            for member in range(GROUP):
-                exponents(here + 2 * GROUP + member, gaps[half][member])
-                weigh(gaps[1 - half][member], weights[1 - half][member])
-                add(here + member, weights[half][member])
-        return carry
-
-    for one in held[:4]:
+    step = pipeline(terms_ref, push_ref, points, listed, force_sum, load_sum, buffers)
+    for one in held[:2]:
         one.wait()
     steps = (early - 2 * GROUP) // (2 * GROUP)
     lax.fori_loop(0, steps, step, 0)
-    for one in held[4:]:
+    for one in held[2:]:
         one.wait()
     lax.fori_loop(steps, (total + 2 * GROUP - 1) // (2 * GROUP), step, 0)
     for index in range(DEPTH):
@@ -318,14 +361,13 @@
                 force_ref[index, 8 * part + block : 8 * part + block + 1, :] = force_sum[
                     index * BLOCKS + block, part : part + 1, :
                 ]
+    force_ref[plane] = own_force[...]
     load_ref[...] = load_sum[0 : 2 * PLANE]
 
 
 def finish(
-    force_ref, velocity_ref, mass_ref, own_ref, other_ref, pose_at, motion_at, out_ref, motion_ref,
-    pose_ref, spin_ref, sems,
+    force_ref, velocity_ref, mass_ref, own_ref, other_ref, pose_ref, spin_ref, out_ref, motion_ref,
 ):
-    fetch([(pose_at, pose_ref), (motion_at, spin_ref)], sems)
     finish_boulders(own_ref, other_ref, pose_ref, spin_ref, motion_ref)
     total = force_ref[0]
     for index in range(1, DEPTH):
@@ -340,23 +382,24 @@
     column = lax.broadcasted_iota(jnp.int32, (2, 6), 1)
     change = jnp.zeros((2, 6), F32)
     for boulder in range(2):
+        pose = [pose_ref[boulder : boulder + 1, entry : entry + 1] for entry in range(16)]
         total = jnp.sum(own_ref[boulder] + other_ref[boulder], axis=1, keepdims=True)
         force = [-total[part : part + 1, :] for part in range(3)]
         torque = [-total[3 + part : 4 + part, :] for part in range(3)]
-        moves = [pose_ref[boulder, 12] * value for value in force]
+        moves = [pose[12] * value for value in force]
         body = []
         for part in range(3):
             turned = (
-                pose_ref[boulder, 3 + part] * torque[0]
-                + pose_ref[boulder, 6 + part] * torque[1]
-                + pose_ref[boulder, 9 + part] * torque[2]
+                pose[3 + part] * torque[0]
+                + pose[6 + part] * torque[1]
+                + pose[9 + part] * torque[2]
             )
-            body.append(turned * pose_ref[boulder, 13 + part])
+            body.append(turned * pose[13 + part])
         for part in range(3):
             moves.append(
-                pose_ref[boulder, 3 + 3 * part] * body[0]
-                + pose_ref[boulder, 4 + 3 * part] * body[1]
-                + pose_ref[boulder, 5 + 3 * part] * body[2]
+                pose[3 + 3 * part] * body[0]
+                + pose[4 + 3 * part] * body[1]
+                + pose[5 + 3 * part] * body[2]
             )
         for part in range(6):
             here = jnp.logical_and(row == boulder, column == part)
@@ -393,6 +436,7 @@
     pair_active,
 ):
     owners = lax.axis_size("wide")
+    planes = [[PLANE * depth + spot for spot in range(PLANE)] for depth in range(owners // PLANE)]
     columns = [[PLANE * depth + spot for depth in range(DEPTH)] for spot in range(PLANE)]
     swap = functools.partial(
         lax.all_to_all, axis_name="wide", split_axis=0, concat_axis=0, tiled=True
@@ -408,9 +452,9 @@
         return moves
 
     geometry = facet_geometry.transpose(0, 2, 1, 3)
-    own = call(
+    facets = call(
         facet_message,
-        shape((8, BLOCKS, 128), F32),
+        shape((PLANE, 8, BLOCKS, 128), F32),
         [ANY, ANY],
         [
             pltpu.VMEM(geometry.shape, F32),
@@ -419,8 +463,7 @@
         ],
         limit=WHOLE_VMEM,
     )(geometry, boulder_pose)
-    line = [own] + [lax.ppermute(own, "wide", shift(step, 1)) for step in (1, 2, 3)]
-    line = jnp.stack(line)
+    facets = swap(facets, axis_index_groups=planes)
     lists = [
         particle_position.transpose(1, 0, 2),
         boulder_slot.reshape(-1, 128),
@@ -429,56 +472,59 @@
         pair_block.reshape(1, pairs),
         pair_active.reshape(1, pairs),
     ]
-    particles = call(
+    particles, own = call(
         pair_message,
-        shape((DEPTH, 56, 128), F32),
-        [ANY] * 7,
+        [shape((DEPTH, 56, 128), F32), shape((56, 128), F32)],
+        [ANY] * 6,
         [pltpu.VMEM(value.shape, value.dtype) for value in lists]
         + [pltpu.SemaphoreType.DMA((6,))],
+        out_specs=[VMEM, VMEM],
         limit=WHOLE_VMEM,
-    )(*lists, own)
-    lines = [lax.ppermute(line, "wide", shift(step, 4)) for step in (1, 2, 3)]
-
-    def features(parts):
-        blocks = ROW * len(parts)
-        return call(
-            facet_features,
-            [shape((blocks, 256, TERMS), BF16), shape((blocks, 16, 128), BF16)],
-            [VMEM] * len(parts),
-            [
-                pltpu.VMEM((blocks, 256, TERMS), BF16),
-                pltpu.VMEM((2 * TERMS * PITCH, 128), F32),
-                pltpu.VMEM((16 * PITCH, 128), F32),
-                pltpu.SemaphoreType.DMA,
-            ],
-            out_specs=[ANY, VMEM],
-        )(*parts)
-
-    near_terms, near_push = features([line])
-    particles, near_push = lax.optimization_barrier((particles, near_push))
+    )(*lists)
+    work = [pltpu.VMEM((256, 256), F32)] * (2 * GROUP) + [pltpu.VMEM((256, 256), BF16)] * (2 * GROUP)
+    terms, push, own_force, own_load = call(
+        facet_features,
+        [
+            shape((FACETS, 256, TERMS), BF16),
+            shape((FACETS + 1, 16, 128), BF16),
+            shape((24, 256), F32),
+            shape((2 * PLANE, 8, 128), F32),
+        ],
+        [VMEM, VMEM],
+        [
+            pltpu.VMEM((FACETS + 1, 256, TERMS), BF16),
+            pltpu.SemaphoreType.DMA,
+            pltpu.SMEM((8, 128), F32),
+            pltpu.SMEM((48 + 6 * GROUP,), jnp.int32),
+            pltpu.VMEM((BLOCKS + 1, TERMS, 256), BF16),
+            pltpu.VMEM((BLOCKS + 1, 8, 256), F32),
+            pltpu.VMEM((2 * PLANE + 1, 8, 128), F32),
+            pltpu.SemaphoreType.DMA,
+        ]
+        + work
+        + [pltpu.VMEM((TERMS * PITCH, 128), F32)] * 2
+        + [pltpu.VMEM((2 * TERMS * PITCH, 128), F32), pltpu.VMEM((16 * PITCH, 128), F32)] * SIDE,
+        out_specs=[ANY, VMEM, VMEM, VMEM],
+    )(facets, own)
     particles = swap(particles, axis_index_groups=columns)
-    far_terms, far_push = features(lines)
     force, load = call(
         contact,
         [shape((DEPTH, 24, 256), F32), shape((2 * PLANE, 8, 128), F32)],
-        [ANY] * 4 + [VMEM],
+        [ANY] + [VMEM] * 4,
         [
             pltpu.VMEM((FACETS + 1, 256, TERMS), BF16),
-            pltpu.VMEM((FACETS + 1, 16, 128), BF16),
-            pltpu.SemaphoreType.DMA((8,)),
+            pltpu.SemaphoreType.DMA((4,)),
             pltpu.SMEM((DEPTH, 8, 128), F32),
             pltpu.SMEM((DEPTH * 48 + 6 * GROUP,), jnp.int32),
-            pltpu.VMEM((TERMS * PITCH, 128), F32),
-            pltpu.VMEM((TERMS * PITCH, 128), F32),
             pltpu.VMEM((PARTICLES + 1, TERMS, 256), BF16),
             pltpu.VMEM((PARTICLES + 1, 8, 256), F32),
             pltpu.VMEM((2 * PLANE + 1, 8, 128), F32),
             pltpu.SemaphoreType.DMA,
         ]
-        + [pltpu.VMEM((256, 256), F32)] * (2 * GROUP)
-        + [pltpu.VMEM((256, 256), BF16)] * (2 * GROUP),
+        + work
+        + [pltpu.VMEM((TERMS * PITCH, 128), F32)] * (2 * SIDE),
         out_specs=[VMEM, VMEM],
-    )(near_terms, far_terms, near_push, far_push, particles)
+    )(terms, push, particles, own_force, own_load)
     grid = load.reshape(4, 4, 2, 8, 128)
     spot = lax.axis_index("wide") % PLANE
     down, across = spot // 4, spot % 4
@@ -497,12 +543,7 @@
     new_velocity, boulder_motion = call(
         finish,
         [shape(velocity.shape, F32), shape(boulder_velocity.shape, F32)],
-        [VMEM] * 5 + [ANY] * 2,
-        [
-            pltpu.SMEM(boulder_pose.shape, F32),
-            pltpu.VMEM(boulder_velocity.shape, F32),
-            pltpu.SemaphoreType.DMA((2,)),
-        ],
+        [VMEM] * 7,
         out_specs=[VMEM, VMEM],
     )(force, velocity, inverse_mass, load, other, boulder_pose, boulder_velocity)
     return (new_velocity.transpose(1, 0, 2), boulder_motion)

time: 76.3 us -> 72.8 us (0.954)
  starting transfers between devices: 39.5 us -> 30.6 us
  waiting for transfers between devices: 8.84 us -> 14.3 us
  other arithmetic: 0.79 us -> 0.02 us
    ppermute x6 -> x0, starting transfers between devices: 9.5 us -> none  [the longest x3 4.81 us: shards(): lines = [lax.ppermute(line, 'wide', shift(step, 4)) for step in (1, 2, 3)]]
    all_to_all x0 -> x1, waiting for transfers between devices: none -> 7.73 us  [shards(): facets = swap(facets, axis_index_groups=planes)]
    all_to_all x0 -> x1, starting transfers between devices: none -> 7.6 us  [shards(): facets = swap(facets, axis_index_groups=planes)]
    ppermute x6 -> x0, waiting for transfers between devices: 4.29 us -> none  [the longest x3 3.07 us: shards(): lines = [lax.ppermute(line, 'wide', shift(step, 4)) for step in (1, 2, 3)]]
    ppermute x3, starting transfers between devices: 5.24 us -> 1.55 us  [shards(): lax.ppermute(pick(grid, 1, across + step), 'wide', shift(step, 1))]
    all_to_all x1, starting transfers between devices: 6.73 us -> 3.55 us  [shards(): force = swap(force, axis_index_groups=columns)]
    all_to_all x1, waiting for transfers between devices: 0.01 us -> 2.58 us  [shards(): particles = swap(particles, axis_index_groups=columns)]
    ppermute x1, starting transfers between devices: 6.56 us -> 5.04 us  [shards(): other = lax.ppermute(load, 'narrow', [(0, 1), (1, 0)])]
  transfers between devices with their start and end apart: 15 -> 10, of which waited for: 8 -> 6; matrix products, arithmetic and copies ran while one was open for 0% -> 0% of each run, Pallas kernels for 10% -> 11%
where the time goes in v5:
time: 72.8 us; the launch traced here: 72.6 us
  starting transfers between devices  30.6 us (42%)
  Pallas kernels  26.1 us (36%)
  waiting for transfers between devices  14.3 us (20%)
  local copies, waits for them, and re-layouts  0.79 us (1%)
  between operations  0.76 us (1%)
    pallas_call x1, Pallas kernels, shards(): call(contact, [shape((DEPTH, 24, 256), F32), shape((2 * PLANE, 8, 128), F...  15.2 us
    all_to_all x1, starting transfers between devices, shards(): particles = swap(particles, axis_index_groups=columns)  8.19 us
    all_to_all x1, waiting for transfers between devices, shards(): facets = swap(facets, axis_index_groups=planes)  7.73 us
    all_to_all x1, starting transfers between devices, shards(): facets = swap(facets, axis_index_groups=planes)  7.6 us
    pallas_call x1, Pallas kernels, shards(): call(facet_features, [shape((FACETS, 256, TERMS), BF16), shape((FACETS +...  5.7 us
    ppermute x1, starting transfers between devices, shards(): other = lax.ppermute(load, 'narrow', [(0, 1), (1, 0)])  5.04 us
    ppermute x3, starting transfers between devices, shards(): lax.ppermute(pick(row, 0, down + step), 'wide', shift(step, 4))  4.66 us
    all_to_all x1, starting transfers between devices, shards(): force = swap(force, axis_index_groups=columns)  3.55 us
  transfers between devices with their start and end apart: 10, of which 6 were waited for; matrix products, arithmetic and copies ran while one was open for 0% of the time, Pallas kernels for 11%

profile of v5, /device:TPU:1, one launch (start us, length us, event | category | flops | bytes accessed | tf_op | source)
XLA Modules:
  0.0 72.6 jit_solution(16545131737212859941)
XLA Ops:
  0.7 1.7 %shard_map.122 = f32[16,8,8,128]{3,2,1,0:T(8,128)} custom-call(f32[2,7,4,128]{3,2,1,0:T(4,128)} %bitcast.37, f32[2,16]{1,0:T(2,128)} %pose_ref.1), custom_call_target="tpu_custom_call" | custom-call | tf_op jit(solution)/shard_map/pallas_call | solution.py:455
  2.4 7.6 %all-to-all-start = ((f32[16,8,8,128]{3,2,1,0:T(8,128)}), f32[16,8,8,128]{3,2,1,0:T(8,128)S(1)}, u32[]{:S(2)}, u32[]{:S(2)}) async-start(f32[16,8,8,128]{3,2,1,0:T(8,128)} %shard_map.122), calls=%async_computation | async-start | bytes 1048576 | tf_op jit(solution)/shard_map/all_to_all | solution.py:466
  10.0 2.6 %shard_map.123 = (f32[8,56,128]{2,1,0:T(8,128)}, f32[56,128]{1,0:T(8,128)}) custom-call(f32[3,8,256]{2,1,0:T(8,128)} %bitcast.38, s32[2,128]{1,0:T(2,128)} %bitcast.40, s32[16,128]{1,0:T(8,128)} %bitcast.39, s32[1,192]{1,0:T(1,128)} %bitcast.41, s32[1,192]{1,0:T(1,128)} %bitcast.42, s32[1,192]{1,0:T(1,128)} %bitcast.43), custom_call_target="tpu_custom_call" | custom-call | tf_op jit(solution)/shard_map/pallas_call | solution.py:475
  12.6 7.7 %all-to-all-done.world_ref = f32[16,8,8,128]{3,2,1,0:T(8,128)S(1)} async-done(((f32[16,8,8,128]{3,2,1,0:T(8,128)}), f32[16,8,8,128]{3,2,1,0:T(8,128)S(1)}, u32[]{:S(2)}, u32[]{:S(2)}) %all-to-all-start) | async-done | bytes 524320 | tf_op jit(solution)/shard_map/all_to_all | solution.py:466
  20.3 8.2 %all-to-all-start.1 = ((f32[8,56,128]{2,1,0:T(8,128)}), f32[8,56,128]{2,1,0:T(8,128)S(1)}, u32[]{:S(2)}, u32[]{:S(2)}) async-start(f32[8,56,128]{2,1,0:T(8,128)} %get-tuple-element.15), calls=%async_computation.1 | async-start | bytes 458752 | tf_op jit(solution)/shard_map/all_to_all | solution.py:509
  28.5 0.7 %copy-done = f32[56,128]{1,0:T(8,128)S(1)} copy-done((f32[56,128]{1,0:T(8,128)S(1)}, f32[56,128]{1,0:T(8,128)}, u32[]{:S(2)}) %copy-start) | copy-done | bytes 28696
  29.3 5.7 %shard_map.124 = (bf16[128,256,32]{2,1,0:T(8,128)(2,1)}, bf16[129,16,128]{2,1,0:T(8,128)(2,1)S(1)}, f32[24,256]{1,0:T(8,128)S(1)}, f32[32,8,128]{2,1,0:T(8,128)S(1)}) custom-call(f32[16,8,8,128]{3,2,1,0:T(8,128)S(1)} %all-to-all-done.world_ref, f32[56,128]{1,0:T(8,128)S(1)} %copy-done), custom_call_target="tpu_custom_call" | custom-call | tf_op jit(solution)/shard_map/pallas_call | solution.py:485
  35.0 2.6 %all-to-all-done.1.given_ref = f32[8,56,128]{2,1,0:T(8,128)S(1)} async-done(((f32[8,56,128]{2,1,0:T(8,128)}), f32[8,56,128]{2,1,0:T(8,128)S(1)}, u32[]{:S(2)}, u32[]{:S(2)}) %all-to-all-start.1) | async-done | bytes 229408 | tf_op jit(solution)/shard_map/all_to_all | solution.py:509
  37.6 15.2 %shard_map.125 = (f32[8,24,256]{2,1,0:T(8,128)}, f32[32,8,128]{2,1,0:T(8,128)S(1)}) custom-call(bf16[128,256,32]{2,1,0:T(8,128)(2,1)} %get-tuple-element.13.held_ref, bf16[129,16,128]{2,1,0:T(8,128)(2,1)S(1)} %get-tuple-element.14.push_ref, f32[8,56,128]{2,1,0:T(8,128)S(1)} %all-to-all-done.1.given_ref, f32[24,256]{1,0:T(8,128)S(1)} %get-tuple-element.16.own_force, ...), custom_call_target="tpu_custom_call" | custom-call | tf_op jit(solution)/shard_map/pallas_call | solution.py:510
  52.8 0.7 collective-permute-start.2
  53.4 0.0 collective-permute-start.1
  53.4 0.8 %collective-permute-start = (f32[4,2,8,128]{3,2,1,0:T(8,128)S(1)}, f32[4,2,8,128]{3,2,1,0:T(8,128)S(1)}, u32[]{:S(2)}, u32[]{:S(2)}) collective-permute-start(f32[4,2,8,128]{3,2,1,0:T(8,128)S(1)} %get-tuple-element.22), channel_id=1, source_target_pairs={{0,2},{2,4},{4,6},{6,0},{8,10},{10,12},{12,14},{14,8},{16,18},{18,... | collective-permute-start | bytes 98312 | tf_op jit(solution)/shard_map/ppermute | solution.py:536
  54.3 3.5 %all-to-all-start.2 = ((f32[8,24,256]{2,1,0:T(8,128)}), f32[8,24,256]{2,1,0:T(8,128)S(1)}, u32[]{:S(2)}, u32[]{:S(2)}) async-start(f32[8,24,256]{2,1,0:T(8,128)} %get-tuple-element.18), calls=%async_computation.2 | async-start | bytes 393216 | tf_op jit(solution)/shard_map/all_to_all | solution.py:541
  57.9 0.0 collective-permute-done.1
  57.9 0.2 collective-permute-done
  58.1 1.5 %collective-permute-start.5 = (f32[2,8,128]{2,1,0:T(8,128)S(1)}, f32[2,8,128]{2,1,0:T(8,128)S(1)}, u32[]{:S(2)}, u32[]{:S(2)}) collective-permute-start(f32[2,8,128]{2,1,0:T(8,128)S(1)} %get-tuple-element.26), channel_id=1, source_target_pairs={{0,24},{2,26},{4,28},{6,30},{8,0},{10,2},{12,4},{14,6},{16,8},{18,... | collective-permute-start | bytes 24584 | tf_op jit(solution)/shard_map/ppermute | solution.py:539
  59.6 2.4 %collective-permute-start.4 = (f32[2,8,128]{2,1,0:T(8,128)S(1)}, f32[2,8,128]{2,1,0:T(8,128)S(1)}, u32[]{:S(2)}, u32[]{:S(2)}) collective-permute-start(f32[2,8,128]{2,1,0:T(8,128)S(1)} %get-tuple-element.27), channel_id=1, source_target_pairs={{0,16},{2,18},{4,20},{6,22},{8,24},{10,26},{12,28},{14,30},{16,0},... | collective-permute-start | bytes 24584 | tf_op jit(solution)/shard_map/ppermute | solution.py:539
  62.0 0.8 %collective-permute-start.3 = (f32[2,8,128]{2,1,0:T(8,128)S(1)}, f32[2,8,128]{2,1,0:T(8,128)S(1)}, u32[]{:S(2)}, u32[]{:S(2)}) collective-permute-start(f32[2,8,128]{2,1,0:T(8,128)S(1)} %get-tuple-element.25), channel_id=1, source_target_pairs={{0,8},{2,10},{4,12},{6,14},{8,16},{10,18},{12,20},{14,22},{16,24},... | collective-permute-start | bytes 24584 | tf_op jit(solution)/shard_map/ppermute | solution.py:539
  62.8 0.9 %collective-permute-done.4 = f32[2,8,128]{2,1,0:T(8,128)S(1)} collective-permute-done((f32[2,8,128]{2,1,0:T(8,128)S(1)}, f32[2,8,128]{2,1,0:T(8,128)S(1)}, u32[]{:S(2)}, u32[]{:S(2)}) %collective-permute-start.4) | collective-permute-done | bytes 8224 | tf_op jit(solution)/shard_map/ppermute | solution.py:539
  63.6 2.1 %collective-permute-done.3 = f32[2,8,128]{2,1,0:T(8,128)S(1)} collective-permute-done((f32[2,8,128]{2,1,0:T(8,128)S(1)}, f32[2,8,128]{2,1,0:T(8,128)S(1)}, u32[]{:S(2)}, u32[]{:S(2)}) %collective-permute-start.3) | collective-permute-done | bytes 8224 | tf_op jit(solution)/shard_map/ppermute | solution.py:539
  65.7 5.0 %collective-permute-start.6 = (f32[2,8,128]{2,1,0:T(8,128)S(1)}, f32[2,8,128]{2,1,0:T(8,128)S(1)}, u32[]{:S(2)}, u32[]{:S(2)}) collective-permute-start(f32[2,8,128]{2,1,0:T(8,128)S(1)} %fusion.3.own_ref), channel_id=1, source_target_pairs={{0,1},{1,0},{2,3},{3,2},{4,5},{5,4},{6,7},{7,6},{8,9},{9,8},{10,11... | collective-permute-start | bytes 24584 | tf_op jit(solution)/shard_map/ppermute | solution.py:540
  70.8 0.8 %collective-permute-done.6.other_ref = f32[2,8,128]{2,1,0:T(8,128)S(1)} collective-permute-done((f32[2,8,128]{2,1,0:T(8,128)S(1)}, f32[2,8,128]{2,1,0:T(8,128)S(1)}, u32[]{:S(2)}, u32[]{:S(2)}) %collective-permute-start.6) | collective-permute-done | bytes 8224 | tf_op jit(solution)/shard_map/ppermute | solution.py:540
  71.6 0.0 all-to-all-done.2.force_ref
  71.6 1.0 %shard_map.126 = (f32[3,8,256]{2,1,0:T(8,128)}, f32[2,6]{1,0:T(2,128)}) custom-call(f32[8,24,256]{2,1,0:T(8,128)S(1)} %all-to-all-done.2.force_ref, f32[3,8,256]{2,1,0:T(8,128)S(1)} %bitcast.36, f32[8,256]{1,0:T(8,128)S(1)} %copy-done.2, f32[2,8,128]{2,1,0:T(8,128)S(1)} %fusion.3.own_ref, f32[2,8,128]{2,1,0:T(8,128)S(1)} %collective-permute-done.6.other_ref, ...), custom_call_target="tpu_custom_call" | custom-call | tf_op jit(solution)/shard_map/pallas_call | solution.py:543
  (15 shorter events, 0.1 us)
Async XLA Ops:
  0.6 71.0 %copy-start.3 = (f32[2,16]{1,0:T(2,128)S(1)}, f32[2,16]{1,0:T(2,128)}, u32[]{:S(2)}) copy-start(f32[2,16]{1,0:T(2,128)} %pose_ref.1) | copy-start | bytes 388
  0.6 71.0 %copy-start.1 = (f32[8,3,256]{2,0,1:T(8,128)S(1)}, f32[8,3,256]{2,0,1:T(8,128)}, u32[]{:S(2)}) copy-start(f32[8,3,256]{2,0,1:T(8,128)} %param.12) | copy-start | bytes 73732
  0.7 71.0 %copy-start.2 = (f32[8,256]{1,0:T(8,128)S(1)}, f32[8,256]{1,0:T(8,128)}, u32[]{:S(2)}) copy-start(f32[8,256]{1,0:T(8,128)} %mass_ref.1) | copy-start | bytes 24580
  0.7 70.9 %copy-start.4 = (f32[2,6]{1,0:T(2,128)S(1)}, f32[2,6]{1,0:T(2,128)}, u32[]{:S(2)}) copy-start(f32[2,6]{1,0:T(2,128)} %spin_ref.1) | copy-start | bytes 148
  2.4 17.9 %all-to-all-start = ((f32[16,8,8,128]{3,2,1,0:T(8,128)}), f32[16,8,8,128]{3,2,1,0:T(8,128)S(1)}, u32[]{:S(2)}, u32[]{:S(2)}) async-start(f32[16,8,8,128]{3,2,1,0:T(8,128)} %shard_map.122), calls=%async_computation | async-start | bytes 1048576 | tf_op jit(solution)/shard_map/all_to_all | solution.py:466
  20.3 17.2 %all-to-all-start.1 = ((f32[8,56,128]{2,1,0:T(8,128)}), f32[8,56,128]{2,1,0:T(8,128)S(1)}, u32[]{:S(2)}, u32[]{:S(2)}) async-start(f32[8,56,128]{2,1,0:T(8,128)} %get-tuple-element.15), calls=%async_computation.1 | async-start | bytes 458752 | tf_op jit(solution)/shard_map/all_to_all | solution.py:509
  28.5 0.7 %copy-start = (f32[56,128]{1,0:T(8,128)S(1)}, f32[56,128]{1,0:T(8,128)}, u32[]{:S(2)}) copy-start(f32[56,128]{1,0:T(8,128)} %get-tuple-element.12.own_ref) | copy-start | bytes 86020
  52.8 5.1 %collective-permute-start.2 = (f32[4,2,8,128]{3,2,1,0:T(8,128)S(1)}, f32[4,2,8,128]{3,2,1,0:T(8,128)S(1)}, u32[]{:S(2)}, u32[]{:S(2)}) collective-permute-start(f32[4,2,8,128]{3,2,1,0:T(8,128)S(1)} %get-tuple-element.23), channel_id=1, source_target_pairs={{0,6},{2,0},{4,2},{6,4},{8,14},{10,8},{12,10},{14,12},{16,22},{18,... | collective-permute-start | bytes 98312 | tf_op jit(solution)/shard_map/ppermute | solution.py:536
  53.4 4.4 %collective-permute-start.1 = (f32[4,2,8,128]{3,2,1,0:T(8,128)S(1)}, f32[4,2,8,128]{3,2,1,0:T(8,128)S(1)}, u32[]{:S(2)}, u32[]{:S(2)}) collective-permute-start(f32[4,2,8,128]{3,2,1,0:T(8,128)S(1)} %get-tuple-element.24), channel_id=1, source_target_pairs={{0,4},{2,6},{4,0},{6,2},{8,12},{10,14},{12,8},{14,10},{16,20},{18,... | collective-permute-start | bytes 98312 | tf_op jit(solution)/shard_map/ppermute | solution.py:536
  53.4 4.6 %collective-permute-start = (f32[4,2,8,128]{3,2,1,0:T(8,128)S(1)}, f32[4,2,8,128]{3,2,1,0:T(8,128)S(1)}, u32[]{:S(2)}, u32[]{:S(2)}) collective-permute-start(f32[4,2,8,128]{3,2,1,0:T(8,128)S(1)} %get-tuple-element.22), channel_id=1, source_target_pairs={{0,2},{2,4},{4,6},{6,0},{8,10},{10,12},{12,14},{14,8},{16,18},{18,... | collective-permute-start | bytes 98312 | tf_op jit(solution)/shard_map/ppermute | solution.py:536
  54.3 17.3 %all-to-all-start.2 = ((f32[8,24,256]{2,1,0:T(8,128)}), f32[8,24,256]{2,1,0:T(8,128)S(1)}, u32[]{:S(2)}, u32[]{:S(2)}) async-start(f32[8,24,256]{2,1,0:T(8,128)} %get-tuple-element.18), calls=%async_computation.2 | async-start | bytes 393216 | tf_op jit(solution)/shard_map/all_to_all | solution.py:541
  58.1 4.7 %collective-permute-start.5 = (f32[2,8,128]{2,1,0:T(8,128)S(1)}, f32[2,8,128]{2,1,0:T(8,128)S(1)}, u32[]{:S(2)}, u32[]{:S(2)}) collective-permute-start(f32[2,8,128]{2,1,0:T(8,128)S(1)} %get-tuple-element.26), channel_id=1, source_target_pairs={{0,24},{2,26},{4,28},{6,30},{8,0},{10,2},{12,4},{14,6},{16,8},{18,... | collective-permute-start | bytes 24584 | tf_op jit(solution)/shard_map/ppermute | solution.py:539
  59.6 4.0 %collective-permute-start.4 = (f32[2,8,128]{2,1,0:T(8,128)S(1)}, f32[2,8,128]{2,1,0:T(8,128)S(1)}, u32[]{:S(2)}, u32[]{:S(2)}) collective-permute-start(f32[2,8,128]{2,1,0:T(8,128)S(1)} %get-tuple-element.27), channel_id=1, source_target_pairs={{0,16},{2,18},{4,20},{6,22},{8,24},{10,26},{12,28},{14,30},{16,0},... | collective-permute-start | bytes 24584 | tf_op jit(solution)/shard_map/ppermute | solution.py:539
  62.0 3.7 %collective-permute-start.3 = (f32[2,8,128]{2,1,0:T(8,128)S(1)}, f32[2,8,128]{2,1,0:T(8,128)S(1)}, u32[]{:S(2)}, u32[]{:S(2)}) collective-permute-start(f32[2,8,128]{2,1,0:T(8,128)S(1)} %get-tuple-element.25), channel_id=1, source_target_pairs={{0,8},{2,10},{4,12},{6,14},{8,16},{10,18},{12,20},{14,22},{16,24},... | collective-permute-start | bytes 24584 | tf_op jit(solution)/shard_map/ppermute | solution.py:539
  65.7 5.9 %collective-permute-start.6 = (f32[2,8,128]{2,1,0:T(8,128)S(1)}, f32[2,8,128]{2,1,0:T(8,128)S(1)}, u32[]{:S(2)}, u32[]{:S(2)}) collective-permute-start(f32[2,8,128]{2,1,0:T(8,128)S(1)} %fusion.3.own_ref), channel_id=1, source_target_pairs={{0,1},{1,0},{2,3},{3,2},{4,5},{5,4},{6,7},{7,6},{8,9},{9,8},{10,11... | collective-permute-start | bytes 24584 | tf_op jit(solution)/shard_map/ppermute | solution.py:540

commit v6 on v5

--- a/solution.py
+++ b/solution.py
@@ -21,6 +21,7 @@
 ROW = 4 * BLOCKS
 PARTICLES = DEPTH * BLOCKS
 GROUP = 2
+FAR = 1e15
 SIDE = 4
 VMEM_LIMIT = 48 * 1024 * 1024
 WHOLE_VMEM = 63 * 1024 * 1024
@@ -215,7 +216,9 @@
         normal = [world_ref[index, 3 + part] for part in range(3)]
         area = world_ref[index, 6]
         last = world_ref[index, 7]
-        center = [lever[part] + last[:, part : part + 1] for part in range(3)]
+        center = [
+            jnp.clip(lever[part] + last[:, part : part + 1], -FAR, FAR) for part in range(3)
+        ]
         along = normal[0] * center[0] + normal[1] * center[1] + normal[2] * center[2]
         square = center[0] * center[0] + center[1] * center[1] + center[2] * center[2]
         sides = (
@@ -268,11 +271,13 @@
     particle_terms(own_ref, points, 0, particle_keep)
     total = table[0, 127].astype(jnp.int32)
 
-    def entry(place, carry):
-        listed[2 * GROUP + place] = table[0, place].astype(jnp.int32)
+    def entry(step, carry):
+        for spare in range(4):
+            place = 4 * step + spare
+            listed[2 * GROUP + place] = table[0, place].astype(jnp.int32)
         return carry
 
-    lax.fori_loop(0, total, entry, 0)
+    lax.fori_loop(0, (total + 3) // 4, entry, 0)
     for spare in range(2 * GROUP):
         listed[spare] = BLOCKS * 256 + FACETS
     for spare in range(4 * GROUP):
@@ -331,11 +336,13 @@
             count = jnp.where(index == plane, 0, count)
             shift = index * (BLOCKS * 256)
 
-            def entry(place, carry):
-                listed[start + place] = table[index, 0, first + place].astype(jnp.int32) + shift
+            def entry(step, carry):
+                for spare in range(4):
+                    place = 4 * step + spare
+                    listed[start + place] = table[index, 0, first + place].astype(jnp.int32) + shift
                 return carry
 
-            lax.fori_loop(0, count, entry, 0)
+            lax.fori_loop(0, (count + 3) // 4, entry, 0)
             return start + count
 
         return lax.fori_loop(0, DEPTH, one, start)

time: 72.8 us -> 72.4 us (level); the launches traced: 72.6 us -> 71.4 us
  Pallas kernels: 26.1 us -> 23.7 us
  starting transfers between devices: 30.6 us -> 31.6 us
    pallas_call x1, Pallas kernels: 15.2 us -> 13.1 us  [shards(): call(contact, [shape((DEPTH, 24, 256), F32), shape((2 * PLANE, 8, 128), F...]
    ppermute x3, starting transfers between devices: 4.66 us -> 3.07 us  [shards(): lax.ppermute(pick(row, 0, down + step), 'wide', shift(step, 4))]
    all_to_all x1, starting transfers between devices: 3.55 us -> 4.65 us  [shards(): force = swap(force, axis_index_groups=columns)]
    ppermute x3, starting transfers between devices: 1.55 us -> 2.41 us  [shards(): lax.ppermute(pick(grid, 1, across + step), 'wide', shift(step, 1))]
  transfers between devices with their start and end apart: 10 -> 10, of which waited for: 6 -> 5; matrix products, arithmetic and copies ran while one was open for 0% -> 0% of each run, Pallas kernels for 11% -> 11%
where the time goes in v6:
time: 72.4 us; the launch traced here: 71.4 us
  starting transfers between devices  31.6 us (44%)
  Pallas kernels  23.7 us (33%)
  waiting for transfers between devices  14.5 us (20%)
  local copies, waits for them, and re-layouts  0.79 us (1%)
  between operations  0.77 us (1%)
    pallas_call x1, Pallas kernels, shards(): call(contact, [shape((DEPTH, 24, 256), F32), shape((2 * PLANE, 8, 128), F...  13.1 us
    all_to_all x1, starting transfers between devices, shards(): particles = swap(particles, axis_index_groups=columns)  8.19 us
    all_to_all x1, waiting for transfers between devices, shards(): facets = swap(facets, axis_index_groups=planes)  7.73 us
    all_to_all x1, starting transfers between devices, shards(): facets = swap(facets, axis_index_groups=planes)  7.6 us
    ppermute x1, starting transfers between devices, shards(): other = lax.ppermute(load, 'narrow', [(0, 1), (1, 0)])  5.74 us
    pallas_call x1, Pallas kernels, shards(): call(facet_features, [shape((FACETS, 256, TERMS), BF16), shape((FACETS +...  5.3 us
    all_to_all x1, starting transfers between devices, shards(): force = swap(force, axis_index_groups=columns)  4.65 us
    ppermute x3, starting transfers between devices, shards(): lax.ppermute(pick(row, 0, down + step), 'wide', shift(step, 4))  3.07 us
  transfers between devices with their start and end apart: 10, of which 5 were waited for; matrix products, arithmetic and copies ran while one was open for 0% of the time, Pallas kernels for 11%

profile of v6, /device:TPU:1, one launch (start us, length us, event | category | flops | bytes accessed | tf_op | source)
XLA Modules:
  0.0 71.4 jit_solution(5506964237398466907)
XLA Ops:
  0.7 1.7 %shard_map.122 = f32[16,8,8,128]{3,2,1,0:T(8,128)} custom-call(f32[2,7,4,128]{3,2,1,0:T(4,128)} %bitcast.37, f32[2,16]{1,0:T(2,128)} %pose_ref.1), custom_call_target="tpu_custom_call" | custom-call | tf_op jit(solution)/shard_map/pallas_call | solution.py:462
  2.4 7.6 %all-to-all-start = ((f32[16,8,8,128]{3,2,1,0:T(8,128)}), f32[16,8,8,128]{3,2,1,0:T(8,128)S(1)}, u32[]{:S(2)}, u32[]{:S(2)}) async-start(f32[16,8,8,128]{3,2,1,0:T(8,128)} %shard_map.122), calls=%async_computation | async-start | bytes 1048576 | tf_op jit(solution)/shard_map/all_to_all | solution.py:473
  10.0 2.6 %shard_map.123 = (f32[8,56,128]{2,1,0:T(8,128)}, f32[56,128]{1,0:T(8,128)}) custom-call(f32[3,8,256]{2,1,0:T(8,128)} %bitcast.38, s32[2,128]{1,0:T(2,128)} %bitcast.40, s32[16,128]{1,0:T(8,128)} %bitcast.39, s32[1,192]{1,0:T(1,128)} %bitcast.41, s32[1,192]{1,0:T(1,128)} %bitcast.42, s32[1,192]{1,0:T(1,128)} %bitcast.43), custom_call_target="tpu_custom_call" | custom-call | tf_op jit(solution)/shard_map/pallas_call | solution.py:482
  12.6 7.7 %all-to-all-done.world_ref = f32[16,8,8,128]{3,2,1,0:T(8,128)S(1)} async-done(((f32[16,8,8,128]{3,2,1,0:T(8,128)}), f32[16,8,8,128]{3,2,1,0:T(8,128)S(1)}, u32[]{:S(2)}, u32[]{:S(2)}) %all-to-all-start) | async-done | bytes 524320 | tf_op jit(solution)/shard_map/all_to_all | solution.py:473
  20.3 8.2 %all-to-all-start.1 = ((f32[8,56,128]{2,1,0:T(8,128)}), f32[8,56,128]{2,1,0:T(8,128)S(1)}, u32[]{:S(2)}, u32[]{:S(2)}) async-start(f32[8,56,128]{2,1,0:T(8,128)} %get-tuple-element.15), calls=%async_computation.1 | async-start | bytes 458752 | tf_op jit(solution)/shard_map/all_to_all | solution.py:516
  28.5 0.7 %copy-done = f32[56,128]{1,0:T(8,128)S(1)} copy-done((f32[56,128]{1,0:T(8,128)S(1)}, f32[56,128]{1,0:T(8,128)}, u32[]{:S(2)}) %copy-start) | copy-done | bytes 28696
  29.3 5.3 %shard_map.124 = (bf16[128,256,32]{2,1,0:T(8,128)(2,1)}, bf16[129,16,128]{2,1,0:T(8,128)(2,1)S(1)}, f32[24,256]{1,0:T(8,128)S(1)}, f32[32,8,128]{2,1,0:T(8,128)S(1)}) custom-call(f32[16,8,8,128]{3,2,1,0:T(8,128)S(1)} %all-to-all-done.world_ref, f32[56,128]{1,0:T(8,128)S(1)} %copy-done), custom_call_target="tpu_custom_call" | custom-call | tf_op jit(solution)/shard_map/pallas_call | solution.py:492
  34.6 3.0 %all-to-all-done.1.given_ref = f32[8,56,128]{2,1,0:T(8,128)S(1)} async-done(((f32[8,56,128]{2,1,0:T(8,128)}), f32[8,56,128]{2,1,0:T(8,128)S(1)}, u32[]{:S(2)}, u32[]{:S(2)}) %all-to-all-start.1) | async-done | bytes 229408 | tf_op jit(solution)/shard_map/all_to_all | solution.py:516
  37.6 13.1 %shard_map.125 = (f32[8,24,256]{2,1,0:T(8,128)}, f32[32,8,128]{2,1,0:T(8,128)S(1)}) custom-call(bf16[128,256,32]{2,1,0:T(8,128)(2,1)} %get-tuple-element.13.held_ref, bf16[129,16,128]{2,1,0:T(8,128)(2,1)S(1)} %get-tuple-element.14.push_ref, f32[8,56,128]{2,1,0:T(8,128)S(1)} %all-to-all-done.1.given_ref, f32[24,256]{1,0:T(8,128)S(1)} %get-tuple-element.16.own_force, ...), custom_call_target="tpu_custom_call" | custom-call | tf_op jit(solution)/shard_map/pallas_call | solution.py:517
  50.7 0.4 collective-permute-start.2
  51.0 2.1 %collective-permute-start.1 = (f32[4,2,8,128]{3,2,1,0:T(8,128)S(1)}, f32[4,2,8,128]{3,2,1,0:T(8,128)S(1)}, u32[]{:S(2)}, u32[]{:S(2)}) collective-permute-start(f32[4,2,8,128]{3,2,1,0:T(8,128)S(1)} %get-tuple-element.24), channel_id=1, source_target_pairs={{0,4},{2,6},{4,0},{6,2},{8,12},{10,14},{12,8},{14,10},{16,20},{18,... | collective-permute-start | bytes 98312 | tf_op jit(solution)/shard_map/ppermute | solution.py:543
  53.1 0.0 collective-permute-start
  53.1 4.6 %all-to-all-start.2 = ((f32[8,24,256]{2,1,0:T(8,128)}), f32[8,24,256]{2,1,0:T(8,128)S(1)}, u32[]{:S(2)}, u32[]{:S(2)}) async-start(f32[8,24,256]{2,1,0:T(8,128)} %get-tuple-element.18), calls=%async_computation.2 | async-start | bytes 393216 | tf_op jit(solution)/shard_map/all_to_all | solution.py:548
  57.7 0.0 collective-permute-done.1
  57.8 1.1 %collective-permute-start.5 = (f32[2,8,128]{2,1,0:T(8,128)S(1)}, f32[2,8,128]{2,1,0:T(8,128)S(1)}, u32[]{:S(2)}, u32[]{:S(2)}) collective-permute-start(f32[2,8,128]{2,1,0:T(8,128)S(1)} %get-tuple-element.26), channel_id=1, source_target_pairs={{0,24},{2,26},{4,28},{6,30},{8,0},{10,2},{12,4},{14,6},{16,8},{18,... | collective-permute-start | bytes 24584 | tf_op jit(solution)/shard_map/ppermute | solution.py:546
  58.9 1.2 %collective-permute-start.4 = (f32[2,8,128]{2,1,0:T(8,128)S(1)}, f32[2,8,128]{2,1,0:T(8,128)S(1)}, u32[]{:S(2)}, u32[]{:S(2)}) collective-permute-start(f32[2,8,128]{2,1,0:T(8,128)S(1)} %get-tuple-element.27), channel_id=1, source_target_pairs={{0,16},{2,18},{4,20},{6,22},{8,24},{10,26},{12,28},{14,30},{16,0},... | collective-permute-start | bytes 24584 | tf_op jit(solution)/shard_map/ppermute | solution.py:546
  60.1 0.8 %collective-permute-start.3 = (f32[2,8,128]{2,1,0:T(8,128)S(1)}, f32[2,8,128]{2,1,0:T(8,128)S(1)}, u32[]{:S(2)}, u32[]{:S(2)}) collective-permute-start(f32[2,8,128]{2,1,0:T(8,128)S(1)} %get-tuple-element.25), channel_id=1, source_target_pairs={{0,8},{2,10},{4,12},{6,14},{8,16},{10,18},{12,20},{14,22},{16,24},... | collective-permute-start | bytes 24584 | tf_op jit(solution)/shard_map/ppermute | solution.py:546
  60.9 0.0 collective-permute-done.5
  60.9 2.1 %collective-permute-done.4 = f32[2,8,128]{2,1,0:T(8,128)S(1)} collective-permute-done((f32[2,8,128]{2,1,0:T(8,128)S(1)}, f32[2,8,128]{2,1,0:T(8,128)S(1)}, u32[]{:S(2)}, u32[]{:S(2)}) %collective-permute-start.4) | collective-permute-done | bytes 8224 | tf_op jit(solution)/shard_map/ppermute | solution.py:546
  62.9 0.9 %collective-permute-done.3 = f32[2,8,128]{2,1,0:T(8,128)S(1)} collective-permute-done((f32[2,8,128]{2,1,0:T(8,128)S(1)}, f32[2,8,128]{2,1,0:T(8,128)S(1)}, u32[]{:S(2)}, u32[]{:S(2)}) %collective-permute-start.3) | collective-permute-done | bytes 8224 | tf_op jit(solution)/shard_map/ppermute | solution.py:546
  63.8 5.7 %collective-permute-start.6 = (f32[2,8,128]{2,1,0:T(8,128)S(1)}, f32[2,8,128]{2,1,0:T(8,128)S(1)}, u32[]{:S(2)}, u32[]{:S(2)}) collective-permute-start(f32[2,8,128]{2,1,0:T(8,128)S(1)} %fusion.3.own_ref), channel_id=1, source_target_pairs={{0,1},{1,0},{2,3},{3,2},{4,5},{5,4},{6,7},{7,6},{8,9},{9,8},{10,11... | collective-permute-start | bytes 24584 | tf_op jit(solution)/shard_map/ppermute | solution.py:547
  69.6 0.8 %collective-permute-done.6.other_ref = f32[2,8,128]{2,1,0:T(8,128)S(1)} collective-permute-done((f32[2,8,128]{2,1,0:T(8,128)S(1)}, f32[2,8,128]{2,1,0:T(8,128)S(1)}, u32[]{:S(2)}, u32[]{:S(2)}) %collective-permute-start.6) | collective-permute-done | bytes 8224 | tf_op jit(solution)/shard_map/ppermute | solution.py:547
  70.4 0.0 all-to-all-done.2.force_ref
  70.4 1.0 %shard_map.126 = (f32[3,8,256]{2,1,0:T(8,128)}, f32[2,6]{1,0:T(2,128)}) custom-call(f32[8,24,256]{2,1,0:T(8,128)S(1)} %all-to-all-done.2.force_ref, f32[3,8,256]{2,1,0:T(8,128)S(1)} %bitcast.36, f32[8,256]{1,0:T(8,128)S(1)} %copy-done.2, f32[2,8,128]{2,1,0:T(8,128)S(1)} %fusion.3.own_ref, f32[2,8,128]{2,1,0:T(8,128)S(1)} %collective-permute-done.6.other_ref, ...), custom_call_target="tpu_custom_call" | custom-call | tf_op jit(solution)/shard_map/pallas_call | solution.py:550
  (15 shorter events, 0.1 us)
Async XLA Ops:
  0.6 69.8 %copy-start.3 = (f32[2,16]{1,0:T(2,128)S(1)}, f32[2,16]{1,0:T(2,128)}, u32[]{:S(2)}) copy-start(f32[2,16]{1,0:T(2,128)} %pose_ref.1) | copy-start | bytes 388
  0.6 69.8 %copy-start.1 = (f32[8,3,256]{2,0,1:T(8,128)S(1)}, f32[8,3,256]{2,0,1:T(8,128)}, u32[]{:S(2)}) copy-start(f32[8,3,256]{2,0,1:T(8,128)} %param.12) | copy-start | bytes 73732
  0.7 69.8 %copy-start.2 = (f32[8,256]{1,0:T(8,128)S(1)}, f32[8,256]{1,0:T(8,128)}, u32[]{:S(2)}) copy-start(f32[8,256]{1,0:T(8,128)} %mass_ref.1) | copy-start | bytes 24580
  0.7 69.8 %copy-start.4 = (f32[2,6]{1,0:T(2,128)S(1)}, f32[2,6]{1,0:T(2,128)}, u32[]{:S(2)}) copy-start(f32[2,6]{1,0:T(2,128)} %spin_ref.1) | copy-start | bytes 148
  2.4 17.9 %all-to-all-start = ((f32[16,8,8,128]{3,2,1,0:T(8,128)}), f32[16,8,8,128]{3,2,1,0:T(8,128)S(1)}, u32[]{:S(2)}, u32[]{:S(2)}) async-start(f32[16,8,8,128]{3,2,1,0:T(8,128)} %shard_map.122), calls=%async_computation | async-start | bytes 1048576 | tf_op jit(solution)/shard_map/all_to_all | solution.py:473
  20.3 17.2 %all-to-all-start.1 = ((f32[8,56,128]{2,1,0:T(8,128)}), f32[8,56,128]{2,1,0:T(8,128)S(1)}, u32[]{:S(2)}, u32[]{:S(2)}) async-start(f32[8,56,128]{2,1,0:T(8,128)} %get-tuple-element.15), calls=%async_computation.1 | async-start | bytes 458752 | tf_op jit(solution)/shard_map/all_to_all | solution.py:516
  28.5 0.7 %copy-start = (f32[56,128]{1,0:T(8,128)S(1)}, f32[56,128]{1,0:T(8,128)}, u32[]{:S(2)}) copy-start(f32[56,128]{1,0:T(8,128)} %get-tuple-element.12.own_ref) | copy-start | bytes 86020
  50.7 7.1 %collective-permute-start.2 = (f32[4,2,8,128]{3,2,1,0:T(8,128)S(1)}, f32[4,2,8,128]{3,2,1,0:T(8,128)S(1)}, u32[]{:S(2)}, u32[]{:S(2)}) collective-permute-start(f32[4,2,8,128]{3,2,1,0:T(8,128)S(1)} %get-tuple-element.23), channel_id=1, source_target_pairs={{0,6},{2,0},{4,2},{6,4},{8,14},{10,8},{12,10},{14,12},{16,22},{18,... | collective-permute-start | bytes 98312 | tf_op jit(solution)/shard_map/ppermute | solution.py:543
  51.0 6.7 %collective-permute-start.1 = (f32[4,2,8,128]{3,2,1,0:T(8,128)S(1)}, f32[4,2,8,128]{3,2,1,0:T(8,128)S(1)}, u32[]{:S(2)}, u32[]{:S(2)}) collective-permute-start(f32[4,2,8,128]{3,2,1,0:T(8,128)S(1)} %get-tuple-element.24), channel_id=1, source_target_pairs={{0,4},{2,6},{4,0},{6,2},{8,12},{10,14},{12,8},{14,10},{16,20},{18,... | collective-permute-start | bytes 98312 | tf_op jit(solution)/shard_map/ppermute | solution.py:543
  53.1 4.7 %collective-permute-start = (f32[4,2,8,128]{3,2,1,0:T(8,128)S(1)}, f32[4,2,8,128]{3,2,1,0:T(8,128)S(1)}, u32[]{:S(2)}, u32[]{:S(2)}) collective-permute-start(f32[4,2,8,128]{3,2,1,0:T(8,128)S(1)} %get-tuple-element.22), channel_id=1, source_target_pairs={{0,2},{2,4},{4,6},{6,0},{8,10},{10,12},{12,14},{14,8},{16,18},{18,... | collective-permute-start | bytes 98312 | tf_op jit(solution)/shard_map/ppermute | solution.py:543
  53.1 17.3 %all-to-all-start.2 = ((f32[8,24,256]{2,1,0:T(8,128)}), f32[8,24,256]{2,1,0:T(8,128)S(1)}, u32[]{:S(2)}, u32[]{:S(2)}) async-start(f32[8,24,256]{2,1,0:T(8,128)} %get-tuple-element.18), calls=%async_computation.2 | async-start | bytes 393216 | tf_op jit(solution)/shard_map/all_to_all | solution.py:548
  57.8 3.1 %collective-permute-start.5 = (f32[2,8,128]{2,1,0:T(8,128)S(1)}, f32[2,8,128]{2,1,0:T(8,128)S(1)}, u32[]{:S(2)}, u32[]{:S(2)}) collective-permute-start(f32[2,8,128]{2,1,0:T(8,128)S(1)} %get-tuple-element.26), channel_id=1, source_target_pairs={{0,24},{2,26},{4,28},{6,30},{8,0},{10,2},{12,4},{14,6},{16,8},{18,... | collective-permute-start | bytes 24584 | tf_op jit(solution)/shard_map/ppermute | solution.py:546
  58.9 4.0 %collective-permute-start.4 = (f32[2,8,128]{2,1,0:T(8,128)S(1)}, f32[2,8,128]{2,1,0:T(8,128)S(1)}, u32[]{:S(2)}, u32[]{:S(2)}) collective-permute-start(f32[2,8,128]{2,1,0:T(8,128)S(1)} %get-tuple-element.27), channel_id=1, source_target_pairs={{0,16},{2,18},{4,20},{6,22},{8,24},{10,26},{12,28},{14,30},{16,0},... | collective-permute-start | bytes 24584 | tf_op jit(solution)/shard_map/ppermute | solution.py:546
  60.1 3.7 %collective-permute-start.3 = (f32[2,8,128]{2,1,0:T(8,128)S(1)}, f32[2,8,128]{2,1,0:T(8,128)S(1)}, u32[]{:S(2)}, u32[]{:S(2)}) collective-permute-start(f32[2,8,128]{2,1,0:T(8,128)S(1)} %get-tuple-element.25), channel_id=1, source_target_pairs={{0,8},{2,10},{4,12},{6,14},{8,16},{10,18},{12,20},{14,22},{16,24},... | collective-permute-start | bytes 24584 | tf_op jit(solution)/shard_map/ppermute | solution.py:546
  63.8 6.6 %collective-permute-start.6 = (f32[2,8,128]{2,1,0:T(8,128)S(1)}, f32[2,8,128]{2,1,0:T(8,128)S(1)}, u32[]{:S(2)}, u32[]{:S(2)}) collective-permute-start(f32[2,8,128]{2,1,0:T(8,128)S(1)} %fusion.3.own_ref), channel_id=1, source_target_pairs={{0,1},{1,0},{2,3},{3,2},{4,5},{5,4},{6,7},{7,6},{8,9},{9,8},{10,11... | collective-permute-start | bytes 24584 | tf_op jit(solution)/shard_map/ppermute | solution.py:547
